TPU v7x, 32 devices: a whole 2x2x4 slice. The times are simulated.
32 devices in a mesh: grp: 4 (over z), dev: 8 (over y, x, core).
Axes of the slice: x: 2, y: 2, z: 4, core: 2. Of those that a mesh axis runs over, the one named last changes fastest.
Arguments:
- subspace: bfloat16 [64, 65536], P(None, ('grp', 'dev')), may hold values from -6 to 6
- tiles: bfloat16 [512, 16, 128, 128], P(('grp', 'dev')), as said below
- tile_count: int32 [512], P(('grp', 'dev')), may hold values from 1 to 16, as said below
- tile_slot: int32 [512, 16], P(('grp', 'dev')), may hold values from 0 to 15, as said below
- fetch_list: int32 [32, 8, 2], P(('grp', 'dev')), may hold values from 0 to 15, as said below
Outputs:
- orthonormal: float32 [64, 65536], P(None, ('grp', 'dev'))
Inputs may be any that keep to these rules, and one draw needn't show every extreme that they name: `tile_count`: at least 1 and at most 16; every device has a block row with 16. `tile_slot`: each entry of a device's fetch list is named by some slot of that device. `fetch_list`: the 2 entries for one pair of devices differ. `tiles`: entries positive.
All inputs are finite; a program needn't handle non-finite values.
Results may differ from a plain program's by a relative error of at most 0.007.
Values may be sent and summed in bfloat16 or wider, within the bound.
No kernel may reach another device: no remote copies, remote signals or barrier semaphores. Data moves between devices by JAX's collectives and lax.ppermute only.
A program may use at most 64 MiB of HBM per device.

v0:
```python
import jax
import jax.numpy as jnp
from jax import lax
from jax.sharding import PartitionSpec as P


def body(subspace, tiles, tile_count, tile_slot, fetch_list):
    k_dim, row_count = subspace.shape
    blocks, slot_count, tile_rows, tile_cols = tiles.shape
    live_mask = (
        lax.broadcasted_iota(jnp.int32, (blocks, slot_count), 1) < tile_count[:, None]
    ).astype(jnp.bfloat16)
    degree = jnp.einsum("btrc,bt->br", tiles, live_mask, preferred_element_type=jnp.float32)
    inv_root = lax.rsqrt(degree).reshape(1, row_count)
    scaled = (subspace.astype(jnp.float32) * inv_root).astype(jnp.bfloat16)
    own_blocks = scaled.reshape(k_dim, blocks, tile_cols)
    peer_count = lax.axis_size("dev")
    group_blocks = lax.all_gather(own_blocks, "dev", axis=1, tiled=True)
    column_index = (
        jnp.arange(peer_count, dtype=jnp.int32)[:, None] * blocks + fetch_list[0]
    ).reshape(-1)
    chosen = jnp.take(group_blocks, column_index, axis=1)
    operand = jnp.take(chosen, tile_slot.reshape(-1), axis=1).reshape(
        k_dim, blocks, slot_count, tile_cols
    )
    operand = operand * live_mask[None, :, :, None]
    product = jnp.einsum("kbtc,btrc->kbr", operand, tiles, preferred_element_type=jnp.float32)
    applied = product.reshape(k_dim, row_count) * inv_root
    gram_local = jnp.dot(applied, applied.T, precision=lax.Precision.HIGHEST)
    gram_total = lax.psum(gram_local, ("grp", "dev"))
    factor = jnp.linalg.cholesky(gram_total)
    return jax.scipy.linalg.solve_triangular(factor, applied, lower=True)


def solution(mesh):
    placed = (
        P(None, ("grp", "dev")),
        P(("grp", "dev"), None, None, None),
        P(("grp", "dev")),
        P(("grp", "dev"), None),
        P(("grp", "dev"), None, None),
    )
    return jax.shard_map(
        body, mesh=mesh, in_specs=placed, out_specs=P(None, ("grp", "dev")), check_vma=False
    )
```

profile of v0, /device:TPU:0, one launch (start us, length us, event | category | flops | bytes accessed | tf_op | source)
XLA Modules:
  0.0 116.2 jit_solution(10575237535968287706)
XLA Ops:
  6.5 0.0 copy-start.1
  6.5 0.0 copy-start.3
  6.5 0.0 copy-start
  6.5 0.0 copy-start.2
  6.5 0.0 all-gather.2.cloned.1.call-start
  6.6 5.7 %convert_reduce_fusion = bf16[16,16,128]{2,1,0:T(8,128)(2,1)S(1)} fusion(bf16[16,16,128,128]{3,2,1,0:T(8,128)(2,1)} %param.6), kind=kLoop, calls=%fused_computation.2 | loop fusion | flops 8355840 | bytes 8454144 | tf_op jit(solution)/shard_map/btrc,bt->br/reduce_sum | solution.py:13
  12.3 0.0 copy-done.1
  12.3 0.0 copy-done.3
  12.3 0.1 fusion.22
  12.4 0.1 fusion.20
  12.6 0.0 copy-done
  12.6 0.8 copy_bitcast_fusion
  13.3 0.0 all-gather.2.cloned.1.call-update
  13.4 0.1 reshape.135
  13.5 0.1 add.79
  13.5 0.1 add.83
  13.6 0.1 add.80
  13.7 0.0 copy-done.2
  13.7 0.1 copy.22
  13.8 0.1 squeeze.6
  13.9 0.1 squeeze.5
  14.0 30.1 %all-gather.2.cloned.1.call-done = bf16[64,128,128]{2,0,1:T(8,128)(2,1)} async-done(((bf16[64,16,128]{2,0,1:T(8,128)(2,1)}), bf16[64,128,128]{2,0,1:T(8,128)(2,1)}) %all-gather.2.cloned.1.call-update) | async-done | bytes 2097168 | tf_op jit(solution)/shard_map/all_gather | solution.py:18
  44.1 2.2 %gather_fusion = bf16[16,64,128]{2,1,0:T(8,128)(2,1)S(1)} fusion(bf16[64,128,128]{2,0,1:T(8,128)(2,1)} %all-gather.2.cloned.1.call-done, s32[1024]{0:T(1024)S(1)} %pad_clamp_fusion.1), kind=kCustom, calls=%fused_computation | custom fusion | bytes 524352 | tf_op jit(solution)/shard_map/jit(_take)/gather | solution.py:22
  46.3 0.1 select_bitcast_fusion
  46.4 3.0 %gather_fusion.1 = bf16[256,64,128]{2,1,0:T(8,128)(2,1)} fusion(bf16[64,16,128]{2,0,1:T(8,128)(2,1)S(1)} %select_bitcast_fusion, s32[1024]{0:T(1024)S(1)} %pad_clamp_fusion), kind=kCustom, calls=%fused_computation.1 | custom fusion | bytes 8389632 | tf_op jit(solution)/shard_map/jit(_take)/gather | solution.py:23
  49.4 6.3 %fusion.9 = f32[16,64,128]{2,1,0:T(8,128)S(1)} fusion(bf16[16,16,128,128]{3,2,1,0:T(8,128)(2,1)} %param.6, bf16[64,16,16,128]{3,0,2,1:T(8,128)(2,1)} %bitcast.47, pred[16,16]{1,0:T(8,128)(4,1)S(1)} %get-tuple-element.9, bf16[16,16]{1,0:T(8,128)(2,1)S(1)} %get-tuple-element.7, f32[16,128]{1,0:T(8,128)S(1)} %get-tuple-element.5), kind=kOutput, calls=%fused_computation.10 | convolution fusion | flops 541196288 | bytes 13116160 | tf_op jit(solution)/shard_map/kbtc,btrc->kbr/dot_general | solution.py:27
  55.7 0.6 convolution_bitcast_fusion
  56.3 39.5 %psum.7 = f32[64,64]{0,1:T(8,128)S(1)} all-reduce(f32[64,64]{0,1:T(8,128)S(1)} %convolution_bitcast_fusion), channel_id=1, replica_groups=mesh['grp'=4,'dev'=8] {'grp','dev'}, use_global_device_ids=true, to_apply=%region_1.2 | all-reduce | flops 4096 | bytes 32768 | tf_op jit(solution)/shard_map/psum | solution.py:30
  95.8 0.1 copy.26
  95.9 5.8 %cholesky.16 = f32[64,64]{1,0:T(8,128)S(1)} custom-call(f32[64,64]{1,0:T(8,128)S(1)} %fusion.19), custom_call_target="Cholesky" | custom-call | tf_op jit(solution)/shard_map/jit(cholesky)/cholesky | solution.py:31
  101.8 0.6 compare_reduce_fusion
  102.4 0.7 fusion.17
  103.1 4.9 %custom-call.7 = f32[1,64,64]{1,2,0:T(8,128)S(1)} custom-call(f32[1,64,64]{2,1,0:T(8,128)S(1)} %fusion.17), custom_call_target="InvertDiagBlocksLowerTriangular" | custom-call | tf_op jit(solution)/shard_map/jit(_solve_triangular)/triangular_solve | solution.py:32
  108.0 1.4 %fusion.12 = f32[64,2048]{1,0:T(8,128)} fusion(f32[1,64,64]{1,2,0:T(8,128)S(1)} %custom-call.7, f32[16,64,128]{2,1,0:T(8,128)S(1)} %fusion.9), kind=kOutput, calls=%fused_computation.12 | convolution fusion | flops 100663296 | bytes 1064960 | tf_op jit(solution)/shard_map/jit(_solve_triangular)/triangular_solve | solution.py:32
  (9 shorter events, 0.1 us)
Async XLA Ops:
  6.5 5.8 %copy-start.1 = (s32[16,16]{1,0:T(8,128)S(1)}, s32[16,16]{1,0:T(8,128)}, u32[]{:S(2)}) copy-start(s32[16,16]{1,0:T(8,128)} %param.8) | copy-start | bytes 3076
  6.5 5.8 %copy-start.3 = (s32[16]{0:T(128)S(1)}, s32[16]{0:T(128)}, u32[]{:S(2)}) copy-start(s32[16]{0:T(128)} %param.7) | copy-start | bytes 196
  6.5 6.0 %copy-start = (bf16[64,2048]{1,0:T(8,128)(2,1)S(1)}, bf16[64,2048]{1,0:T(8,128)(2,1)}, u32[]{:S(2)}) copy-start(bf16[64,2048]{1,0:T(8,128)(2,1)} %param.5) | copy-start | bytes 786436
  6.5 7.1 %copy-start.2 = (s32[1,8,2]{1,2,0:T(2,128)S(1)}, s32[1,8,2]{1,2,0:T(2,128)}, u32[]{:S(2)}) copy-start(s32[1,8,2]{1,2,0:T(2,128)} %param.9) | copy-start | bytes 196
  6.5 37.6 %all-gather.2.cloned.1.call-start = ((), (), s32[]{:S(2)}) async-start(), calls=%async_computation | async-start | bytes 2359296 | tf_op jit(solution)/shard_map/all_gather | solution.py:18
Sparse Core Ops, SparseCore 0:
  13.5 30.5 all-gather.1
where the time goes:
time: 117 us; the launch traced here: 116 us
  blocking collectives  39.5 us (34%)
  waiting for transfers between devices  30.1 us (26%)
  other arithmetic  18.8 us (16%)
  between operations  13.5 us (12%)
  matrix products  8.4 us (7%)
  local copies, waits for them, and re-layouts  5.86 us (5%)
    psum x1, blocking collectives, body(): gram_total = lax.psum(gram_local, ('grp', 'dev'))  39.5 us
    all_gather x1, waiting for transfers between devices, body(): group_blocks = lax.all_gather(own_blocks, 'dev', axis=1, tiled=True)  30.1 us
    another operation x3, other arithmetic, body(): factor = jnp.linalg.cholesky(gram_total)  6.52 us
    dot_general x1, matrix products, body(): jnp.einsum('kbtc,btrc->kbr', operand, tiles, preferred_element_type=jnp.f...  6.25 us
    reduce_sum x1, other arithmetic, body(): jnp.einsum('btrc,bt->br', tiles, live_mask, preferred_element_type=jnp.fl...  5.72 us
    another operation x2, other arithmetic, body(): return jax.scipy.linalg.solve_triangular(factor, applied, lower=True)  5.55 us
    gather x1, local copies, waits for them, and re-layouts, body(): jnp.take(chosen, tile_slot.reshape(-1), axis=1)  3.02 us
  transfers between devices with their start and end apart: 1, of which 1 were waited for; matrix products, arithmetic and copies ran while one was open for 1% of the time, Pallas kernels for 0%

commit v1 on v0

v1 whole, which is shorter than its diff:
```python
import functools

import jax
import jax.numpy as jnp
from jax import lax
from jax.experimental import pallas as pl
from jax.experimental.pallas import tpu as pltpu
from jax.sharding import PartitionSpec as P

CHUNK = 4
VMEM = pl.BlockSpec(memory_space=pltpu.VMEM)
SMEM = pl.BlockSpec(memory_space=pltpu.SMEM)
NT = (((1,), (1,)), ((), ()))


def degree_kernel(count_ref, tiles_ref, sub_ref, scaled_ref, inv_ref, held_ref, sems):
    blocks, slots, rows, cols = tiles_ref.shape
    chunks = slots // CHUNK

    def copy(b, c):
        part = pl.ds(c * CHUNK, CHUNK)
        return pltpu.make_async_copy(
            tiles_ref.at[b, part], held_ref.at[b, part], sems.at[b, c]
        )

    for b in range(blocks):
        for c in range(chunks):

            @pl.when(c * CHUNK < count_ref[b])
            def _():
                copy(b, c).start()

    ones = jnp.ones((8, cols), jnp.bfloat16)
    for b in range(blocks):
        count = count_ref[b]

        def add(c, total):
            copy(b, c).wait()
            for t in range(CHUNK):
                tile = held_ref[b, c * CHUNK + t].astype(jnp.float32)
                total = total + jnp.where(c * CHUNK + t < count, tile, 0.0)
            return total

        total = lax.fori_loop(
            0, pl.cdiv(count, CHUNK), add, jnp.zeros((rows, cols), jnp.float32)
        )
        high = total.astype(jnp.bfloat16)
        low = (total - high.astype(jnp.float32)).astype(jnp.bfloat16)
        degree = lax.dot_general(ones, high, NT, preferred_element_type=jnp.float32)
        degree = degree + lax.dot_general(ones, low, NT, preferred_element_type=jnp.float32)
        inv = lax.rsqrt(degree)
        lanes = slice(b * rows, (b + 1) * rows)
        inv_ref[:, lanes] = inv
        scaled_ref[b] = (sub_ref[:, lanes].astype(jnp.float32) * inv[:1]).astype(jnp.bfloat16)


def select_kernel(me_ref, lists_ref, scaled_ref, *send_refs):
    cap = send_refs[0].shape[1]
    me = me_ref[0]
    for i, send in enumerate(send_refs):
        for core in range(2):
            for j in range(cap):
                block = lists_ref[2 * i + core, me * cap + j]
                send[core, j] = scaled_ref[block]


def product_kernel(me_ref, count_ref, slot_ref, inv_ref, held_ref, own_ref, *refs):
    *near_refs, far_ref, applied_ref, gram_ref, table = refs
    blocks, slots, rows, cols = held_ref.shape
    cap, k_dim, _ = own_ref.shape[1:]
    me = me_ref[0]
    for i, near in enumerate([own_ref, *near_refs]):
        for j in range(cap):
            table[2 * i * cap + j] = near[0, j]
            table[(2 * i + 1) * cap + j] = far_ref[i, j]
    for b in range(blocks):
        count = count_ref[b]

        def add(c, total):
            parts, tiles = [], []
            for t in range(CHUNK):
                slot = slot_ref[b, c * CHUNK + t]
                entry = (lax.div(slot, cap) ^ me) * cap + lax.rem(slot, cap)
                operand = table[entry]
                parts.append(
                    jnp.where(c * CHUNK + t < count, operand, jnp.zeros_like(operand))
                )
                tiles.append(held_ref[b, c * CHUNK + t])
            return total + lax.dot_general(
                jnp.concatenate(parts, axis=1),
                jnp.concatenate(tiles, axis=1),
                NT,
                preferred_element_type=jnp.float32,
            )

        total = lax.fori_loop(
            0, pl.cdiv(count, CHUNK), add, jnp.zeros((k_dim, rows), jnp.float32)
        )
        lanes = slice(b * rows, (b + 1) * rows)
        applied_ref[:, lanes] = total * inv_ref[:1, lanes]
    applied = applied_ref[...]
    high = applied.astype(jnp.bfloat16)
    low = (applied - high.astype(jnp.float32)).astype(jnp.bfloat16)
    both = jnp.concatenate([high, low], axis=0)
    wide = lax.dot_general(both, both, NT, preferred_element_type=jnp.float32)
    wide = wide[:k_dim] + wide[k_dim:]
    gram = wide[:, :k_dim] + wide[:, k_dim:]
    half = k_dim // 2
    gram_ref[...] = jnp.concatenate([gram[:half], gram[half:]], axis=1)


def solve_kernel(here_ref, there_ref, applied_ref, out_ref):
    half, wide = here_ref.shape
    k_dim = wide // 2
    packed = here_ref[...] + there_ref[...]
    gram = jnp.concatenate([packed[:, :k_dim], packed[:, k_dim:]], axis=0)
    eye = (
        lax.broadcasted_iota(jnp.int32, (k_dim, k_dim), 0)
        == lax.broadcasted_iota(jnp.int32, (k_dim, k_dim), 1)
    ).astype(jnp.float32)
    whole = jnp.concatenate([gram, eye], axis=1)
    groups = [whole[8 * i : 8 * i + 8] for i in range(k_dim // 8)]
    row_ids = lax.broadcasted_iota(jnp.int32, (8, 1), 0)
    for j in range(k_dim):
        g, s = divmod(j, 8)
        row = groups[g][s : s + 1]
        step = row / row[:, j : j + 1]
        for i in range(g, k_dim // 8):
            column = groups[i][:, j : j + 1]
            if i == g:
                column = jnp.where(row_ids > s, column, 0.0)
            groups[i] = groups[i] - column * step
    whole = jnp.concatenate(groups, axis=0)
    diagonal = jnp.sum(whole[:, :k_dim] * eye, axis=1, keepdims=True)
    inverse = whole[:, k_dim:] * lax.rsqrt(diagonal)
    out_ref[...] = jnp.dot(
        inverse,
        applied_ref[...],
        precision=lax.Precision.HIGHEST,
        preferred_element_type=jnp.float32,
    )


def swap(x, axis, mask):
    size = lax.axis_size(axis)
    return lax.ppermute(x, axis, [(i, i ^ mask) for i in range(size)])


def bits(axis):
    size = lax.axis_size(axis)
    return [1 << i for i in range(size.bit_length() - 1)]


def body(subspace, tiles, tile_count, tile_slot, fetch_list):
    k_dim, row_count = subspace.shape
    blocks, slots, rows, cols = tiles.shape
    peers = lax.axis_size("dev")
    cap = fetch_list.shape[2]
    chips = peers // 2
    me = lax.axis_index("dev").astype(jnp.int32).reshape(1)

    lists = fetch_list.reshape(1, peers * cap)
    for mask in bits("dev"):
        lists = jnp.concatenate([lists, swap(lists, "dev", mask)], axis=0)

    scaled, inv_root, held = pl.pallas_call(
        degree_kernel,
        out_shape=(
            jax.ShapeDtypeStruct((blocks, k_dim, cols), jnp.bfloat16),
            jax.ShapeDtypeStruct((8, row_count), jnp.float32),
            pltpu.VMEM(tiles.shape, tiles.dtype),
        ),
        in_specs=[SMEM, pl.BlockSpec(memory_space=pl.ANY), VMEM],
        out_specs=(VMEM, VMEM, VMEM),
        scratch_shapes=[pltpu.SemaphoreType.DMA((blocks, slots // CHUNK))],
        compiler_params=pltpu.CompilerParams(vmem_limit_bytes=24 << 20),
        cost_estimate=pl.CostEstimate(
            flops=2 * tiles.size, bytes_accessed=2 * tiles.size, transcendentals=0
        ),
        name="degree",
    )(tile_count, tiles, subspace)

    sends = pl.pallas_call(
        select_kernel,
        out_shape=[jax.ShapeDtypeStruct((2, cap, k_dim, cols), jnp.bfloat16)] * chips,
        in_specs=[SMEM, SMEM, VMEM],
        out_specs=[VMEM] * chips,
        name="select",
    )(me, lists, scaled)

    own = sends[0]
    near = [swap(sends[i], "dev", 2 * i) for i in range(1, chips)]
    far = swap(jnp.stack([part[1] for part in [own, *near]]), "dev", 1)

    applied, gram = pl.pallas_call(
        product_kernel,
        out_shape=(
            jax.ShapeDtypeStruct((k_dim, row_count), jnp.float32),
            jax.ShapeDtypeStruct((k_dim // 2, 2 * k_dim), jnp.float32),
        ),
        in_specs=[SMEM, SMEM, SMEM] + [VMEM] * (chips + 3),
        out_specs=(VMEM, VMEM),
        scratch_shapes=[pltpu.VMEM((peers * cap, k_dim, cols), jnp.bfloat16)],
        compiler_params=pltpu.CompilerParams(vmem_limit_bytes=24 << 20),
        cost_estimate=pl.CostEstimate(
            flops=2 * tiles.size * k_dim, bytes_accessed=row_count * k_dim * 4, transcendentals=0
        ),
        name="product",
    )(me, tile_count, tile_slot, inv_root, held, own, *near, far)

    stages = [("dev", mask) for mask in bits("dev")] + [("grp", mask) for mask in bits("grp")]
    for axis, mask in stages[:-1]:
        gram = gram + swap(gram, axis, mask)
    other = swap(gram, *stages[-1])

    return pl.pallas_call(
        solve_kernel,
        out_shape=jax.ShapeDtypeStruct((k_dim, row_count), jnp.float32),
        in_specs=[VMEM] * 3,
        out_specs=VMEM,
        name="solve",
    )(gram, other, applied)


def solution(mesh):
    placed = (
        P(None, ("grp", "dev")),
        P(("grp", "dev"), None, None, None),
        P(("grp", "dev")),
        P(("grp", "dev"), None),
        P(("grp", "dev"), None, None),
    )
    return jax.shard_map(
        body, mesh=mesh, in_specs=placed, out_specs=P(None, ("grp", "dev")), check_vma=False
    )
```

time: 117 us -> 80.3 us (0.69)
  blocking collectives: 39.5 us -> 0 us
  Pallas kernels: 0 us -> 30.5 us
  other arithmetic: 18.8 us -> 0.65 us
  starting transfers between devices: 0.03 us -> 14.5 us
  between operations: 13.5 us -> 0.07 us
  waiting for transfers between devices: 30.1 us -> 17.3 us
  local copies, waits for them, and re-layouts: 5.86 us -> 16.2 us
  matrix products: 8.4 us -> 0 us
    psum x1 -> x0, blocking collectives: 39.5 us -> none  [body(): gram_total = lax.psum(gram_local, ('grp', 'dev'))]
    pallas_call x0 -> x4, Pallas kernels: none -> 30.5 us  [the longest x1 12.6 us: body(): pl.pallas_call(degree_kernel, out_shape=(jax.ShapeDtypeStruct((blocks, k_...]
    all_gather x1 -> x0, waiting for transfers between devices: 30.1 us -> none  [body(): group_blocks = lax.all_gather(own_blocks, 'dev', axis=1, tiled=True)]
    ppermute x0 -> x12, waiting for transfers between devices: none -> 17.3 us  [swap(): return lax.ppermute(x, axis, [(i, i ^ mask) for i in range(size)])]
    unnamed x9 -> x25, local copies, waits for them, and re-layouts: 0.1 us -> 15.4 us
    ppermute x0 -> x12, starting transfers between devices: none -> 14.5 us  [swap(): return lax.ppermute(x, axis, [(i, i ^ mask) for i in range(size)])]
    another operation x5 -> x1, other arithmetic: 12.1 us -> 0.02 us  [body(): far = swap(jnp.stack([part[1] for part in [own, *near]]), 'dev', 1)]
    dot_general x3 -> x0, matrix products: 6.96 us -> none  [the longest x1 6.25 us: body(): jnp.einsum('kbtc,btrc->kbr', operand, tiles, preferred_element_type=jnp.f...]
  transfers between devices with their start and end apart: 1 -> 12, of which waited for: 1 -> 11; matrix products, arithmetic and copies ran while one was open for 1% -> 1% of each run, Pallas kernels for 0% -> 16%
where the time goes in v1:
time: 80.3 us; the launch traced here: 79.2 us
  Pallas kernels  30.5 us (38%)
  waiting for transfers between devices  17.3 us (22%)
  local copies, waits for them, and re-layouts  16.2 us (20%)
  starting transfers between devices  14.5 us (18%)
    ppermute x12, waiting for transfers between devices, swap(): return lax.ppermute(x, axis, [(i, i ^ mask) for i in range(size)])  17.3 us
    unnamed x25, local copies, waits for them, and re-layouts  15.4 us
    ppermute x12, starting transfers between devices, swap(): return lax.ppermute(x, axis, [(i, i ^ mask) for i in range(size)])  14.5 us
    pallas_call x1, Pallas kernels, body(): pl.pallas_call(degree_kernel, out_shape=(jax.ShapeDtypeStruct((blocks, k_...  12.6 us
    pallas_call x1, Pallas kernels, body(): pl.pallas_call(product_kernel, out_shape=(jax.ShapeDtypeStruct((k_dim, ro...  8.2 us
    pallas_call x1, Pallas kernels, body(): pl.pallas_call(solve_kernel, out_shape=jax.ShapeDtypeStruct((k_dim, row_c...  7.93 us
    pallas_call x1, Pallas kernels, body(): pl.pallas_call(select_kernel, out_shape=[jax.ShapeDtypeStruct((2, cap, k_...  1.69 us
  transfers between devices with their start and end apart: 12, of which 11 were waited for; matrix products, arithmetic and copies ran while one was open for 1% of the time, Pallas kernels for 16%

profile of v1, /device:TPU:0, one launch (start us, length us, event | category | flops | bytes accessed | tf_op | source)
XLA Modules:
  0.0 79.2 jit_solution(8933338855973837902)
XLA Ops:
  0.0 0.0 copy-start.9
  0.0 0.0 copy-start.7
  0.0 0.8 copy.7
  0.8 0.1 reshape.7
  0.9 0.5 collective-permute-start
  1.3 0.8 %collective-permute-done = s32[1,16]{1,0:T(1,128)S(1)} collective-permute-done((s32[1,16]{1,0:T(1,128)S(1)}, s32[1,16]{1,0:T(1,128)S(1)}, u32[]{:S(2)}, u32[]{:S(2)}) %collective-permute-start) | collective-permute-done | bytes 96 | tf_op jit(solution)/shard_map/ppermute | solution.py:146
  2.2 2.8 %collective-permute-start.1 = (s32[2,16]{1,0:T(2,128)S(1)}, s32[2,16]{1,0:T(2,128)S(1)}, u32[]{:S(2)}, u32[]{:S(2)}) collective-permute-start(s32[2,16]{1,0:T(2,128)S(1)} %pad_add_fusion.2), channel_id=1, source_target_pairs={{0,2},{1,3},{2,0},{3,1},{4,6},{5,7},{6,4},{7,5},{8,10},{9,11},{10,... | collective-permute-start | bytes 392 | tf_op jit(solution)/shard_map/ppermute | solution.py:146
  5.0 1.5 %collective-permute-done.1 = s32[2,16]{1,0:T(2,128)S(1)} collective-permute-done((s32[2,16]{1,0:T(2,128)S(1)}, s32[2,16]{1,0:T(2,128)S(1)}, u32[]{:S(2)}, u32[]{:S(2)}) %collective-permute-start.1) | collective-permute-done | bytes 160 | tf_op jit(solution)/shard_map/ppermute | solution.py:146
  6.6 2.1 %collective-permute-start.2 = (s32[4,16]{1,0:T(4,128)S(1)}, s32[4,16]{1,0:T(4,128)S(1)}, u32[]{:S(2)}, u32[]{:S(2)}) collective-permute-start(s32[4,16]{1,0:T(4,128)S(1)} %pad_add_fusion.1), channel_id=1, source_target_pairs={{0,4},{1,5},{2,6},{3,7},{4,0},{5,1},{6,2},{7,3},{8,12},{9,13},{10,... | collective-permute-start | bytes 776 | tf_op jit(solution)/shard_map/ppermute | solution.py:146
  8.7 0.0 copy-start
  8.7 3.4 %copy-done = bf16[16,16,128,128]{3,2,1,0:T(8,128)(2,1)S(1)} copy-done((bf16[16,16,128,128]{3,2,1,0:T(8,128)(2,1)S(1)}, bf16[16,16,128,128]{3,2,1,0:T(8,128)(2,1)}, u32[]{:S(2)}) %copy-start) | copy-done | bytes 8388632
  12.1 0.9 %copy-done.4 = bf16[64,2048]{1,0:T(8,128)(2,1)S(1)} copy-done((bf16[64,2048]{1,0:T(8,128)(2,1)S(1)}, bf16[64,2048]{1,0:T(8,128)(2,1)}, u32[]{:S(2)}) %copy-start.4) | copy-done | bytes 262168
  13.0 0.7 copy-done.8
  13.7 12.6 %degree.1 = (bf16[16,64,128]{2,1,0:T(8,128)(2,1)S(1)}, f32[8,2048]{1,0:T(8,128)S(1)}, bf16[16,16,128,128]{3,2,1,0:T(8,128)(2,1)S(1)}) custom-call(s32[16]{0:T(128)S(1)} %copy-done.8, bf16[16,16,128,128]{3,2,1,0:T(8,128)(2,1)S(1)} %copy-done, bf16[64,2048]{1,0:T(8,128)(2,1)S(1)} %copy-done.4), custom_call_target="tpu_custom_call" | custom-call | flops 8388608 | bytes 8388608 | tf_op jit(solution)/shard_map/degree/pallas_call | solution.py:166
  26.3 0.0 copy-start.1
  26.3 3.3 %copy-done.1 = bf16[16,16,128,128]{3,2,1,0:T(8,128)(2,1)} copy-done((bf16[16,16,128,128]{3,2,1,0:T(8,128)(2,1)}, bf16[16,16,128,128]{3,2,1,0:T(8,128)(2,1)S(1)}, u32[]{:S(2)}) %copy-start.1) | copy-done | bytes 8388632
  29.6 0.7 copy-done.5
  30.3 0.0 collective-permute-done.2
  30.3 0.6 pad_add_fusion.lists_ref
  30.9 1.7 %select.1 = (bf16[2,2,64,128]{3,2,1,0:T(8,128)(2,1)}, bf16[2,2,64,128]{3,2,1,0:T(8,128)(2,1)}, bf16[2,2,64,128]{3,2,1,0:T(8,128)(2,1)}, bf16[2,2,64,128]{3,2,1,0:T(8,128)(2,1)}) custom-call(s32[1]{0:T(128)} %bitcast.me_ref, s32[8,16]{1,0:T(8,128)} %pad_add_fusion.lists_ref, bf16[16,64,128]{2,1,0:T(8,128)(2,1)} %copy-done.5), custom_call_target="tpu_custom_call" | custom-call | tf_op jit(solution)/shard_map/select/pallas_call | solution.py:183
  32.6 0.9 %collective-permute-start.3 = (bf16[2,2,64,128]{3,2,1,0:T(8,128)(2,1)}, bf16[2,2,64,128]{3,2,1,0:T(8,128)(2,1)S(1)}, u32[]{:S(2)}, u32[]{:S(2)}) collective-permute-start(bf16[2,2,64,128]{3,2,1,0:T(8,128)(2,1)} %get-tuple-element.18), channel_id=1, source_target_pairs={{0,2},{1,3},{2,0},{3,1},{4,6},{5,7},{6,4},{7,5},{8,10},{9,11},{10,... | collective-permute-start | bytes 196616 | tf_op jit(solution)/shard_map/ppermute | solution.py:146
  33.5 0.0 collective-permute-start.4
  33.5 2.6 %collective-permute-start.5 = (bf16[2,2,64,128]{3,2,1,0:T(8,128)(2,1)}, bf16[2,2,64,128]{3,2,1,0:T(8,128)(2,1)S(1)}, u32[]{:S(2)}, u32[]{:S(2)}) collective-permute-start(bf16[2,2,64,128]{3,2,1,0:T(8,128)(2,1)} %get-tuple-element.20), channel_id=1, source_target_pairs={{0,6},{1,7},{2,4},{3,5},{4,2},{5,3},{6,0},{7,1},{8,14},{9,15},{10,... | collective-permute-start | bytes 196616 | tf_op jit(solution)/shard_map/ppermute | solution.py:146
  36.1 0.8 slice.12
  36.8 0.6 collective-permute-done.3.refs_0_
  37.4 0.5 collective-permute-done.4.refs_1_
  38.0 0.9 %collective-permute-done.5.refs_2_ = bf16[2,2,64,128]{3,2,1,0:T(8,128)(2,1)S(1)} collective-permute-done((bf16[2,2,64,128]{3,2,1,0:T(8,128)(2,1)}, bf16[2,2,64,128]{3,2,1,0:T(8,128)(2,1)S(1)}, u32[]{:S(2)}, u32[]{:S(2)}) %collective-permute-start.5) | collective-permute-done | bytes 65568 | tf_op jit(solution)/shard_map/ppermute | solution.py:146
  38.9 0.1 collective-permute-start.6
  39.0 1.3 %collective-permute-done.6.refs_3_ = bf16[4,2,64,128]{3,2,1,0:T(8,128)(2,1)S(1)} collective-permute-done((bf16[4,2,64,128]{3,2,1,0:T(8,128)(2,1)S(1)}, bf16[4,2,64,128]{3,2,1,0:T(8,128)(2,1)S(1)}, u32[]{:S(2)}, u32[]{:S(2)}) %collective-permute-start.6) | collective-permute-done | bytes 131104 | tf_op jit(solution)/shard_map/ppermute | solution.py:146
  40.3 0.0 copy-done.9
  40.3 0.0 copy-done.7
  40.3 3.4 %copy-done.2 = bf16[16,16,128,128]{3,2,1,0:T(8,128)(2,1)S(1)} copy-done((bf16[16,16,128,128]{3,2,1,0:T(8,128)(2,1)S(1)}, bf16[16,16,128,128]{3,2,1,0:T(8,128)(2,1)}, u32[]{:S(2)}) %copy-start.2) | copy-done | bytes 8388632
  43.7 0.8 %copy-done.6 = bf16[2,2,64,128]{3,2,1,0:T(8,128)(2,1)S(1)} copy-done((bf16[2,2,64,128]{3,2,1,0:T(8,128)(2,1)S(1)}, bf16[2,2,64,128]{3,2,1,0:T(8,128)(2,1)}, u32[]{:S(2)}) %copy-start.6) | copy-done | bytes 65560
  44.5 8.2 %product.1 = (f32[64,2048]{1,0:T(8,128)S(1)}, f32[32,128]{1,0:T(8,128)S(1)}) custom-call(s32[1]{0:T(128)} %bitcast.me_ref, s32[16]{0:T(128)S(1)} %copy-done.9, s32[16,16]{1,0:T(8,128)S(1)} %copy-done.7, f32[8,2048]{1,0:T(8,128)S(1)} %get-tuple-element.14.inv_ref, bf16[16,16,128,128]{3,2,1,0:T(8,128)(2,1)S(1)} %copy-done.2, ...), custom_call_target="tpu_custom_call" | custom-call | flops 536870912 | bytes 524288 | tf_op jit(solution)/shard_map/product/pallas_call | solution.py:195
  52.7 0.8 %copy-done.3 = f32[64,2048]{1,0:T(8,128)} copy-done((f32[64,2048]{1,0:T(8,128)}, f32[64,2048]{1,0:T(8,128)S(1)}, u32[]{:S(2)}) %copy-start.3) | copy-done | bytes 524312
  53.5 0.0 collective-permute-start.7
  53.5 1.2 %collective-permute-done.7 = f32[32,128]{1,0:T(8,128)S(1)} collective-permute-done((f32[32,128]{1,0:T(8,128)S(1)}, f32[32,128]{1,0:T(8,128)S(1)}, u32[]{:S(2)}, u32[]{:S(2)}) %collective-permute-start.7) | collective-permute-done | bytes 16416 | tf_op jit(solution)/shard_map/ppermute | solution.py:146
  54.7 1.1 %collective-permute-start.8 = (f32[32,128]{1,0:T(8,128)S(1)}, f32[32,128]{1,0:T(8,128)S(1)}, u32[]{:S(2)}, u32[]{:S(2)}) collective-permute-start(f32[32,128]{1,0:T(8,128)S(1)} %add.12), channel_id=1, source_target_pairs={{0,2},{1,3},{2,0},{3,1},{4,6},{5,7},{6,4},{7,5},{8,10},{9,11},{10,... | collective-permute-start | bytes 49160 | tf_op jit(solution)/shard_map/ppermute | solution.py:146
  55.8 2.6 %collective-permute-done.8 = f32[32,128]{1,0:T(8,128)S(1)} collective-permute-done((f32[32,128]{1,0:T(8,128)S(1)}, f32[32,128]{1,0:T(8,128)S(1)}, u32[]{:S(2)}, u32[]{:S(2)}) %collective-permute-start.8) | collective-permute-done | bytes 16416 | tf_op jit(solution)/shard_map/ppermute | solution.py:146
  58.5 0.1 collective-permute-start.9
  58.6 3.6 %collective-permute-done.9 = f32[32,128]{1,0:T(8,128)S(1)} collective-permute-done((f32[32,128]{1,0:T(8,128)S(1)}, f32[32,128]{1,0:T(8,128)S(1)}, u32[]{:S(2)}, u32[]{:S(2)}) %collective-permute-start.9) | collective-permute-done | bytes 16416 | tf_op jit(solution)/shard_map/ppermute | solution.py:146
  62.2 1.4 %collective-permute-start.10 = (f32[32,128]{1,0:T(8,128)S(1)}, f32[32,128]{1,0:T(8,128)S(1)}, u32[]{:S(2)}, u32[]{:S(2)}) collective-permute-start(f32[32,128]{1,0:T(8,128)S(1)} %add.14), channel_id=1, source_target_pairs={{0,8},{8,0},{16,24},{24,16},{1,9},{9,1},{17,25},{25,17},{2,10},{10... | collective-permute-start | bytes 49160 | tf_op jit(solution)/shard_map/ppermute | solution.py:146
  63.6 2.4 %collective-permute-done.10 = f32[32,128]{1,0:T(8,128)S(1)} collective-permute-done((f32[32,128]{1,0:T(8,128)S(1)}, f32[32,128]{1,0:T(8,128)S(1)}, u32[]{:S(2)}, u32[]{:S(2)}) %collective-permute-start.10) | collective-permute-done | bytes 16416 | tf_op jit(solution)/shard_map/ppermute | solution.py:146
  66.0 2.9 %collective-permute-start.11 = (f32[32,128]{1,0:T(8,128)S(1)}, f32[32,128]{1,0:T(8,128)S(1)}, u32[]{:S(2)}, u32[]{:S(2)}) collective-permute-start(f32[32,128]{1,0:T(8,128)S(1)} %add.15.here_ref), channel_id=1, source_target_pairs={{0,16},{8,24},{16,0},{24,8},{1,17},{9,25},{17,1},{25,9},{2,18},{10... | collective-permute-start | bytes 49160 | tf_op jit(solution)/shard_map/ppermute | solution.py:146
  68.9 1.7 %collective-permute-done.11.there_ref = f32[32,128]{1,0:T(8,128)S(1)} collective-permute-done((f32[32,128]{1,0:T(8,128)S(1)}, f32[32,128]{1,0:T(8,128)S(1)}, u32[]{:S(2)}, u32[]{:S(2)}) %collective-permute-start.11) | collective-permute-done | bytes 16416 | tf_op jit(solution)/shard_map/ppermute | solution.py:146
  70.6 0.0 copy-done.10
  70.6 0.6 copy-done.11
  71.2 7.9 %solve.1 = f32[64,2048]{1,0:T(8,128)} custom-call(f32[32,128]{1,0:T(8,128)} %copy-done.10, f32[32,128]{1,0:T(8,128)} %copy-done.11, f32[64,2048]{1,0:T(8,128)} %copy-done.3), custom_call_target="tpu_custom_call" | custom-call | tf_op jit(solution)/shard_map/solve/pallas_call | solution.py:216
  (18 shorter events, 0.1 us)
Async XLA Ops:
  0.0 40.3 %copy-start.9 = (s32[16]{0:T(128)S(1)}, s32[16]{0:T(128)}, u32[]{:S(2)}) copy-start(s32[16]{0:T(128)} %count_ref.3) | copy-start | bytes 196
  0.0 40.3 %copy-start.7 = (s32[16,16]{1,0:T(8,128)S(1)}, s32[16,16]{1,0:T(8,128)}, u32[]{:S(2)}) copy-start(s32[16,16]{1,0:T(8,128)} %slot_ref.1) | copy-start | bytes 3076
  0.9 1.3 %collective-permute-start = (s32[1,16]{1,0:T(1,128)S(1)}, s32[1,16]{1,0:T(1,128)S(1)}, u32[]{:S(2)}, u32[]{:S(2)}) collective-permute-start(s32[1,16]{1,0:T(1,128)S(1)} %reshape.7), channel_id=1, source_target_pairs={{0,1},{1,0},{2,3},{3,2},{4,5},{5,4},{6,7},{7,6},{8,9},{9,8},{10,11... | collective-permute-start | bytes 200 | tf_op jit(solution)/shard_map/ppermute | solution.py:146
  2.2 4.4 %collective-permute-start.1 = (s32[2,16]{1,0:T(2,128)S(1)}, s32[2,16]{1,0:T(2,128)S(1)}, u32[]{:S(2)}, u32[]{:S(2)}) collective-permute-start(s32[2,16]{1,0:T(2,128)S(1)} %pad_add_fusion.2), channel_id=1, source_target_pairs={{0,2},{1,3},{2,0},{3,1},{4,6},{5,7},{6,4},{7,5},{8,10},{9,11},{10,... | collective-permute-start | bytes 392 | tf_op jit(solution)/shard_map/ppermute | solution.py:146
  6.6 23.7 %collective-permute-start.2 = (s32[4,16]{1,0:T(4,128)S(1)}, s32[4,16]{1,0:T(4,128)S(1)}, u32[]{:S(2)}, u32[]{:S(2)}) collective-permute-start(s32[4,16]{1,0:T(4,128)S(1)} %pad_add_fusion.1), channel_id=1, source_target_pairs={{0,4},{1,5},{2,6},{3,7},{4,0},{5,1},{6,2},{7,3},{8,12},{9,13},{10,... | collective-permute-start | bytes 776 | tf_op jit(solution)/shard_map/ppermute | solution.py:146
  8.7 3.4 %copy-start = (bf16[16,16,128,128]{3,2,1,0:T(8,128)(2,1)S(1)}, bf16[16,16,128,128]{3,2,1,0:T(8,128)(2,1)}, u32[]{:S(2)}) copy-start(bf16[16,16,128,128]{3,2,1,0:T(8,128)(2,1)} %tiles_ref.1) | copy-start | bytes 25165828
  12.1 0.9 %copy-start.4 = (bf16[64,2048]{1,0:T(8,128)(2,1)S(1)}, bf16[64,2048]{1,0:T(8,128)(2,1)}, u32[]{:S(2)}) copy-start(bf16[64,2048]{1,0:T(8,128)(2,1)} %sub_ref.1) | copy-start | bytes 786436
  13.0 0.7 copy-start.8
  26.3 3.3 %copy-start.1 = (bf16[16,16,128,128]{3,2,1,0:T(8,128)(2,1)}, bf16[16,16,128,128]{3,2,1,0:T(8,128)(2,1)S(1)}, u32[]{:S(2)}) copy-start(bf16[16,16,128,128]{3,2,1,0:T(8,128)(2,1)S(1)} %get-tuple-element.15.held_ref) | copy-start | bytes 25165828
  29.6 0.7 copy-start.5
  32.6 4.8 %collective-permute-start.3 = (bf16[2,2,64,128]{3,2,1,0:T(8,128)(2,1)}, bf16[2,2,64,128]{3,2,1,0:T(8,128)(2,1)S(1)}, u32[]{:S(2)}, u32[]{:S(2)}) collective-permute-start(bf16[2,2,64,128]{3,2,1,0:T(8,128)(2,1)} %get-tuple-element.18), channel_id=1, source_target_pairs={{0,2},{1,3},{2,0},{3,1},{4,6},{5,7},{6,4},{7,5},{8,10},{9,11},{10,... | collective-permute-start | bytes 196616 | tf_op jit(solution)/shard_map/ppermute | solution.py:146
  33.5 4.5 %collective-permute-start.4 = (bf16[2,2,64,128]{3,2,1,0:T(8,128)(2,1)}, bf16[2,2,64,128]{3,2,1,0:T(8,128)(2,1)S(1)}, u32[]{:S(2)}, u32[]{:S(2)}) collective-permute-start(bf16[2,2,64,128]{3,2,1,0:T(8,128)(2,1)} %get-tuple-element.19), channel_id=1, source_target_pairs={{0,4},{1,5},{2,6},{3,7},{4,0},{5,1},{6,2},{7,3},{8,12},{9,13},{10,... | collective-permute-start | bytes 196616 | tf_op jit(solution)/shard_map/ppermute | solution.py:146
  33.5 5.4 %collective-permute-start.5 = (bf16[2,2,64,128]{3,2,1,0:T(8,128)(2,1)}, bf16[2,2,64,128]{3,2,1,0:T(8,128)(2,1)S(1)}, u32[]{:S(2)}, u32[]{:S(2)}) collective-permute-start(bf16[2,2,64,128]{3,2,1,0:T(8,128)(2,1)} %get-tuple-element.20), channel_id=1, source_target_pairs={{0,6},{1,7},{2,4},{3,5},{4,2},{5,3},{6,0},{7,1},{8,14},{9,15},{10,... | collective-permute-start | bytes 196616 | tf_op jit(solution)/shard_map/ppermute | solution.py:146
  38.9 1.4 %collective-permute-start.6 = (bf16[4,2,64,128]{3,2,1,0:T(8,128)(2,1)S(1)}, bf16[4,2,64,128]{3,2,1,0:T(8,128)(2,1)S(1)}, u32[]{:S(2)}, u32[]{:S(2)}) collective-permute-start(bf16[4,2,64,128]{3,2,1,0:T(8,128)(2,1)S(1)} %pad_maximum_fusion), channel_id=1, source_target_pairs={{0,1},{1,0},{2,3},{3,2},{4,5},{5,4},{6,7},{7,6},{8,9},{9,8},{10,11... | collective-permute-start | bytes 393224 | tf_op jit(solution)/shard_map/ppermute | solution.py:146
  40.3 3.4 %copy-start.2 = (bf16[16,16,128,128]{3,2,1,0:T(8,128)(2,1)S(1)}, bf16[16,16,128,128]{3,2,1,0:T(8,128)(2,1)}, u32[]{:S(2)}) copy-start(bf16[16,16,128,128]{3,2,1,0:T(8,128)(2,1)} %copy-done.1) | copy-start | bytes 25165828
  43.7 0.8 %copy-start.6 = (bf16[2,2,64,128]{3,2,1,0:T(8,128)(2,1)S(1)}, bf16[2,2,64,128]{3,2,1,0:T(8,128)(2,1)}, u32[]{:S(2)}) copy-start(bf16[2,2,64,128]{3,2,1,0:T(8,128)(2,1)} %get-tuple-element.17.own_ref) | copy-start | bytes 196612
  52.7 0.8 %copy-start.3 = (f32[64,2048]{1,0:T(8,128)}, f32[64,2048]{1,0:T(8,128)S(1)}, u32[]{:S(2)}) copy-start(f32[64,2048]{1,0:T(8,128)S(1)} %get-tuple-element.22.applied_ref) | copy-start | bytes 1572868
  53.5 1.2 %collective-permute-start.7 = (f32[32,128]{1,0:T(8,128)S(1)}, f32[32,128]{1,0:T(8,128)S(1)}, u32[]{:S(2)}, u32[]{:S(2)}) collective-permute-start(f32[32,128]{1,0:T(8,128)S(1)} %get-tuple-element.21), channel_id=1, source_target_pairs={{0,1},{1,0},{2,3},{3,2},{4,5},{5,4},{6,7},{7,6},{8,9},{9,8},{10,11... | collective-permute-start | bytes 49160 | tf_op jit(solution)/shard_map/ppermute | solution.py:146
  54.7 3.7 %collective-permute-start.8 = (f32[32,128]{1,0:T(8,128)S(1)}, f32[32,128]{1,0:T(8,128)S(1)}, u32[]{:S(2)}, u32[]{:S(2)}) collective-permute-start(f32[32,128]{1,0:T(8,128)S(1)} %add.12), channel_id=1, source_target_pairs={{0,2},{1,3},{2,0},{3,1},{4,6},{5,7},{6,4},{7,5},{8,10},{9,11},{10,... | collective-permute-start | bytes 49160 | tf_op jit(solution)/shard_map/ppermute | solution.py:146
  58.5 3.7 %collective-permute-start.9 = (f32[32,128]{1,0:T(8,128)S(1)}, f32[32,128]{1,0:T(8,128)S(1)}, u32[]{:S(2)}, u32[]{:S(2)}) collective-permute-start(f32[32,128]{1,0:T(8,128)S(1)} %add.13), channel_id=1, source_target_pairs={{0,4},{1,5},{2,6},{3,7},{4,0},{5,1},{6,2},{7,3},{8,12},{9,13},{10,... | collective-permute-start | bytes 49160 | tf_op jit(solution)/shard_map/ppermute | solution.py:146
  62.2 3.7 %collective-permute-start.10 = (f32[32,128]{1,0:T(8,128)S(1)}, f32[32,128]{1,0:T(8,128)S(1)}, u32[]{:S(2)}, u32[]{:S(2)}) collective-permute-start(f32[32,128]{1,0:T(8,128)S(1)} %add.14), channel_id=1, source_target_pairs={{0,8},{8,0},{16,24},{24,16},{1,9},{9,1},{17,25},{25,17},{2,10},{10... | collective-permute-start | bytes 49160 | tf_op jit(solution)/shard_map/ppermute | solution.py:146
  66.0 4.7 %copy-start.10 = (f32[32,128]{1,0:T(8,128)}, f32[32,128]{1,0:T(8,128)S(1)}, u32[]{:S(2)}) copy-start(f32[32,128]{1,0:T(8,128)S(1)} %add.15.here_ref) | copy-start | bytes 49156
  66.0 4.7 %collective-permute-start.11 = (f32[32,128]{1,0:T(8,128)S(1)}, f32[32,128]{1,0:T(8,128)S(1)}, u32[]{:S(2)}, u32[]{:S(2)}) collective-permute-start(f32[32,128]{1,0:T(8,128)S(1)} %add.15.here_ref), channel_id=1, source_target_pairs={{0,16},{8,24},{16,0},{24,8},{1,17},{9,25},{17,1},{25,9},{2,18},{10... | collective-permute-start | bytes 49160 | tf_op jit(solution)/shard_map/ppermute | solution.py:146
  70.6 0.6 copy-start.11

commit v2 on v1

v2 whole, which is shorter than its diff:
```python
import jax
import jax.numpy as jnp
from jax import lax
from jax.experimental import pallas as pl
from jax.experimental.pallas import tpu as pltpu
from jax.sharding import PartitionSpec as P

VMEM = pl.BlockSpec(memory_space=pltpu.VMEM)
SMEM = pl.BlockSpec(memory_space=pltpu.SMEM)
NT = (((1,), (1,)), ((), ()))
F32 = jnp.float32
BF16 = jnp.bfloat16


def limit(mib):
    return pltpu.CompilerParams(vmem_limit_bytes=mib << 20)


def split(x):
    high = x.astype(BF16)
    return high, (x - high.astype(F32)).astype(BF16)


def degree_kernel(count_ref, tiles_ref, sub_ref, scaled_ref, inv_ref):
    blocks, slots, rows, cols = tiles_ref.shape
    slot_of_lane = lax.broadcasted_iota(jnp.int32, (8, slots * cols), 1) // cols
    for b in range(blocks):
        live = (slot_of_lane < count_ref[b]).astype(F32).astype(BF16)
        row = jnp.concatenate([tiles_ref[b, t] for t in range(slots)], axis=1)
        degree = lax.dot_general(live, row, NT, preferred_element_type=F32)
        inv = lax.rsqrt(degree)
        lanes = slice(b * rows, (b + 1) * rows)
        inv_ref[:, lanes] = inv
        scaled_ref[b] = (sub_ref[:, lanes].astype(F32) * inv[:1]).astype(BF16)


def select_kernel(me_ref, lists_ref, scaled_ref, *send_refs):
    cap = send_refs[0].shape[1]
    me = me_ref[0]
    for i, send in enumerate(send_refs):
        for core in range(2):
            for j in range(cap):
                block = lists_ref[2 * i + core, me * cap + j]
                send[core, j] = scaled_ref[block]


def product_kernel(me_ref, count_ref, slot_ref, inv_ref, tiles_ref, own_ref, *refs):
    *near_refs, far_ref, applied_ref, gram_ref, table = refs
    blocks, slots, rows, cols = tiles_ref.shape
    cap, k_dim, _ = own_ref.shape[1:]
    me = me_ref[0]
    for i, near in enumerate([own_ref, *near_refs]):
        for j in range(cap):
            table[2 * i * cap + j] = near[0, j]
            table[(2 * i + 1) * cap + j] = far_ref[i, j]
    for b in range(blocks):
        parts = []
        for t in range(slots):
            slot = slot_ref[b, t]
            entry = (lax.div(slot, cap) ^ me) * cap + lax.rem(slot, cap)
            block = table[entry]
            parts.append(jnp.where(t < count_ref[b], block, jnp.zeros_like(block)))
        row = jnp.concatenate([tiles_ref[b, t] for t in range(slots)], axis=1)
        total = lax.dot_general(
            jnp.concatenate(parts, axis=1), row, NT, preferred_element_type=F32
        )
        lanes = slice(b * rows, (b + 1) * rows)
        high, low = split(total * inv_ref[:1, lanes])
        applied_ref[:k_dim, lanes] = high
        applied_ref[k_dim:, lanes] = low
    both = applied_ref[...]
    wide = lax.dot_general(both, both, NT, preferred_element_type=F32)
    wide = wide[:k_dim] + wide[k_dim:]
    gram = wide[:, :k_dim] + wide[:, k_dim:]
    half = k_dim // 2
    gram_ref[...] = jnp.concatenate([gram[:half], gram[half:]], axis=1)


def inverse_factor(gram):
    k_dim = gram.shape[0]
    wide, groups = 2 * k_dim, k_dim // 8
    square = (k_dim, k_dim)
    eye = (
        lax.broadcasted_iota(jnp.int32, square, 0) == lax.broadcasted_iota(jnp.int32, square, 1)
    ).astype(F32)
    diagonal = gram * eye
    row_scale = lax.rsqrt(jnp.sum(diagonal, axis=1, keepdims=True))
    col_scale = lax.rsqrt(jnp.sum(diagonal, axis=0, keepdims=True))
    whole = jnp.concatenate([gram * row_scale * col_scale, eye * col_scale], axis=1)
    rows = [whole[8 * i : 8 * i + 8] for i in range(groups)]
    row_ids = lax.broadcasted_iota(jnp.int32, (8, wide), 0)

    def spread(x):
        return jnp.broadcast_to(x, (8, wide))

    done = []
    for g in range(groups):
        column = {
            (i, b): spread(rows[i][:, 8 * g + b : 8 * g + b + 1])
            for i in range(g, groups)
            for b in range(8)
        }
        out = rows[g]
        for s in range(0, 8, 2):
            row0, row1 = spread(rows[g][s : s + 1]), spread(rows[g][s + 1 : s + 2])
            pivot0 = {b: spread(column[g, b][s : s + 1]) for b in range(s, 8)}
            pivot1 = {b: spread(column[g, b][s + 1 : s + 2]) for b in range(s, 8)}
            p00, p01, p11 = pivot0[s], pivot0[s + 1], pivot1[s + 1]
            det = p00 * p11 - p01 * p01
            inv_det = pl.reciprocal(det, approx=True)
            inv_det = inv_det * (2.0 - det * inv_det)
            q00, q01, q11 = p11 * inv_det, p01 * inv_det, p00 * inv_det
            root0 = lax.rsqrt(p00)
            ratio = p01 * (root0 * root0)
            root1 = lax.rsqrt(p11 - p01 * ratio)
            out = jnp.where(row_ids == s, row0 * root0, out)
            out = jnp.where(row_ids == s + 1, (row1 - ratio * row0) * root1, out)
            for i in range(g, groups):
                x, y = column[i, s], column[i, s + 1]
                f0, f1 = q00 * x - q01 * y, q11 * y - q01 * x
                if i == g:
                    f0 = jnp.where(row_ids > s + 1, f0, 0.0)
                    f1 = jnp.where(row_ids > s + 1, f1, 0.0)
                rows[i] = rows[i] - f0 * row0 - f1 * row1
                for b in range(s + 2, 8):
                    column[i, b] = column[i, b] - f0 * pivot0[b] - f1 * pivot1[b]
        done.append(out)
    return jnp.concatenate(done, axis=0)[:, k_dim:]


def solve_kernel(here_ref, there_ref, applied_ref, out_ref):
    k_dim = here_ref.shape[1] // 2
    packed = here_ref[...] + there_ref[...]
    gram = jnp.concatenate([packed[:, :k_dim], packed[:, k_dim:]], axis=0)
    high, low = split(inverse_factor(gram))
    out_ref[...] = jnp.dot(
        jnp.concatenate([high, high, low], axis=1),
        jnp.concatenate([applied_ref[...], applied_ref[:k_dim]], axis=0),
        preferred_element_type=F32,
    )


def swap(x, axis, mask):
    size = lax.axis_size(axis)
    return lax.ppermute(x, axis, [(i, i ^ mask) for i in range(size)])


def bits(axis):
    return [1 << i for i in range(lax.axis_size(axis).bit_length() - 1)]


def body(subspace, tiles, tile_count, tile_slot, fetch_list):
    k_dim, row_count = subspace.shape
    blocks, slots, rows, cols = tiles.shape
    peers = lax.axis_size("dev")
    cap = fetch_list.shape[2]
    chips = peers // 2
    me = lax.axis_index("dev").astype(jnp.int32).reshape(1)

    lists = fetch_list.reshape(1, peers * cap)
    for mask in bits("dev"):
        lists = jnp.concatenate([lists, swap(lists, "dev", mask)], axis=0)

    scaled, inv_root = pl.pallas_call(
        degree_kernel,
        out_shape=(
            jax.ShapeDtypeStruct((blocks, k_dim, cols), BF16),
            jax.ShapeDtypeStruct((8, row_count), F32),
        ),
        in_specs=[SMEM, VMEM, VMEM],
        out_specs=(VMEM, VMEM),
        compiler_params=limit(12),
        cost_estimate=pl.CostEstimate(
            flops=16 * tiles.size, bytes_accessed=2 * tiles.size, transcendentals=0
        ),
        name="degree",
    )(tile_count, tiles, subspace)

    sends = pl.pallas_call(
        select_kernel,
        out_shape=[jax.ShapeDtypeStruct((2, cap, k_dim, cols), BF16)] * chips,
        in_specs=[SMEM, SMEM, VMEM],
        out_specs=[VMEM] * chips,
        compiler_params=limit(4),
        name="select",
    )(me, lists, scaled)

    own = sends[0]
    near = [swap(sends[i], "dev", 2 * i) for i in range(1, chips)]
    far = swap(jnp.stack([part[1] for part in [own, *near]]), "dev", 1)

    applied, gram = pl.pallas_call(
        product_kernel,
        out_shape=(
            jax.ShapeDtypeStruct((2 * k_dim, row_count), BF16),
            jax.ShapeDtypeStruct((k_dim // 2, 2 * k_dim), F32),
        ),
        in_specs=[SMEM, SMEM, SMEM] + [VMEM] * (chips + 3),
        out_specs=(VMEM, VMEM),
        scratch_shapes=[pltpu.VMEM((peers * cap, k_dim, cols), BF16)],
        compiler_params=limit(16),
        cost_estimate=pl.CostEstimate(
            flops=2 * tiles.size * k_dim, bytes_accessed=2 * tiles.size, transcendentals=0
        ),
        name="product",
    )(me, tile_count, tile_slot, inv_root, tiles, own, *near, far)

    stages = [("dev", mask) for mask in bits("dev")] + [("grp", mask) for mask in bits("grp")]
    for axis, mask in stages[:-1]:
        gram = gram + swap(gram, axis, mask)
    other = swap(gram, *stages[-1])

    return pl.pallas_call(
        solve_kernel,
        out_shape=jax.ShapeDtypeStruct((k_dim, row_count), F32),
        in_specs=[VMEM] * 3,
        out_specs=VMEM,
        compiler_params=limit(4),
        name="solve",
    )(gram, other, applied)


def solution(mesh):
    placed = (
        P(None, ("grp", "dev")),
        P(("grp", "dev"), None, None, None),
        P(("grp", "dev")),
        P(("grp", "dev"), None),
        P(("grp", "dev"), None, None),
    )
    return jax.shard_map(
        body, mesh=mesh, in_specs=placed, out_specs=P(None, ("grp", "dev")), check_vma=False
    )
```

time: 80.3 us -> 53.9 us (0.67); the launches traced: 79.2 us -> 53.6 us
  Pallas kernels: 30.5 us -> 10.8 us
  local copies, waits for them, and re-layouts: 16.2 us -> 9.25 us
  waiting for transfers between devices: 17.3 us -> 18.5 us
    pallas_call x1, Pallas kernels: 12.6 us -> 2.82 us  [body(): pl.pallas_call(degree_kernel, out_shape=(jax.ShapeDtypeStruct((blocks, k_...]
    unnamed x25 -> x13, local copies, waits for them, and re-layouts: 15.4 us -> 9.16 us
    pallas_call x1, Pallas kernels: 7.93 us -> 3.17 us  [body(): pl.pallas_call(solve_kernel, out_shape=jax.ShapeDtypeStruct((k_dim, row_c...]
    pallas_call x1, Pallas kernels: 8.2 us -> 4.14 us  [body(): pl.pallas_call(product_kernel, out_shape=(jax.ShapeDtypeStruct((2 * k_dim...]
    ppermute x12, waiting for transfers between devices: 17.3 us -> 18.5 us  [swap(): return lax.ppermute(x, axis, [(i, i ^ mask) for i in range(size)])]
    pallas_call x1, Pallas kernels: 1.69 us -> 0.63 us  [body(): pl.pallas_call(select_kernel, out_shape=[jax.ShapeDtypeStruct((2, cap, k_...]
  transfers between devices with their start and end apart: 12 -> 12, of which waited for: 11 -> 11; matrix products, arithmetic and copies ran while one was open for 1% -> 0% of each run, Pallas kernels for 16% -> 5%
where the time goes in v2:
time: 53.9 us; the launch traced here: 53.6 us
  waiting for transfers between devices  18.5 us (34%)
  starting transfers between devices  15 us (28%)
  Pallas kernels  10.8 us (20%)
  local copies, waits for them, and re-layouts  9.25 us (17%)
    ppermute x12, waiting for transfers between devices, swap(): return lax.ppermute(x, axis, [(i, i ^ mask) for i in range(size)])  18.5 us
    ppermute x12, starting transfers between devices, swap(): return lax.ppermute(x, axis, [(i, i ^ mask) for i in range(size)])  15 us
    unnamed x13, local copies, waits for them, and re-layouts  9.16 us
    pallas_call x1, Pallas kernels, body(): pl.pallas_call(product_kernel, out_shape=(jax.ShapeDtypeStruct((2 * k_dim...  4.14 us
    pallas_call x1, Pallas kernels, body(): pl.pallas_call(solve_kernel, out_shape=jax.ShapeDtypeStruct((k_dim, row_c...  3.17 us
    pallas_call x1, Pallas kernels, body(): pl.pallas_call(degree_kernel, out_shape=(jax.ShapeDtypeStruct((blocks, k_...  2.82 us
  transfers between devices with their start and end apart: 12, of which 11 were waited for; matrix products, arithmetic and copies ran while one was open for 0% of the time, Pallas kernels for 5%

profile of v2, /device:TPU:0, one launch (start us, length us, event | category | flops | bytes accessed | tf_op | source)
XLA Modules:
  0.0 53.6 jit_solution(9547598359913178295)
XLA Ops:
  0.0 0.0 copy-start.5
  0.0 0.0 copy-start.3
  0.0 0.8 %copy.7 = s32[1,8,2]{2,1,0:T(8,128)S(1)} copy(s32[1,8,2]{1,2,0:T(2,128)} %param.9) | data formatting | bytes 128 | tf_op args[4]
  0.8 0.1 reshape.7
  0.9 0.5 collective-permute-start
  1.3 0.8 %collective-permute-done = s32[1,16]{1,0:T(1,128)S(1)} collective-permute-done((s32[1,16]{1,0:T(1,128)S(1)}, s32[1,16]{1,0:T(1,128)S(1)}, u32[]{:S(2)}, u32[]{:S(2)}) %collective-permute-start) | collective-permute-done | bytes 96 | tf_op jit(solution)/shard_map/ppermute | solution.py:145
  2.2 2.8 %collective-permute-start.1 = (s32[2,16]{1,0:T(2,128)S(1)}, s32[2,16]{1,0:T(2,128)S(1)}, u32[]{:S(2)}, u32[]{:S(2)}) collective-permute-start(s32[2,16]{1,0:T(2,128)S(1)} %pad_add_fusion.2), channel_id=1, source_target_pairs={{0,2},{1,3},{2,0},{3,1},{4,6},{5,7},{6,4},{7,5},{8,10},{9,11},{10,... | collective-permute-start | bytes 392 | tf_op jit(solution)/shard_map/ppermute | solution.py:145
  5.0 1.5 %collective-permute-done.1 = s32[2,16]{1,0:T(2,128)S(1)} collective-permute-done((s32[2,16]{1,0:T(2,128)S(1)}, s32[2,16]{1,0:T(2,128)S(1)}, u32[]{:S(2)}, u32[]{:S(2)}) %collective-permute-start.1) | collective-permute-done | bytes 160 | tf_op jit(solution)/shard_map/ppermute | solution.py:145
  6.6 2.1 %collective-permute-start.2 = (s32[4,16]{1,0:T(4,128)S(1)}, s32[4,16]{1,0:T(4,128)S(1)}, u32[]{:S(2)}, u32[]{:S(2)}) collective-permute-start(s32[4,16]{1,0:T(4,128)S(1)} %pad_add_fusion.1), channel_id=1, source_target_pairs={{0,4},{1,5},{2,6},{3,7},{4,0},{5,1},{6,2},{7,3},{8,12},{9,13},{10,... | collective-permute-start | bytes 776 | tf_op jit(solution)/shard_map/ppermute | solution.py:145
  8.7 0.0 copy-start
  8.7 3.4 %copy-done = bf16[16,16,128,128]{3,2,1,0:T(8,128)(2,1)S(1)} copy-done((bf16[16,16,128,128]{3,2,1,0:T(8,128)(2,1)S(1)}, bf16[16,16,128,128]{3,2,1,0:T(8,128)(2,1)}, u32[]{:S(2)}) %copy-start) | copy-done | bytes 8388632
  12.1 0.0 copy-start.2
  12.1 0.9 %copy-done.2 = bf16[64,2048]{1,0:T(8,128)(2,1)S(1)} copy-done((bf16[64,2048]{1,0:T(8,128)(2,1)S(1)}, bf16[64,2048]{1,0:T(8,128)(2,1)}, u32[]{:S(2)}) %copy-start.2) | copy-done | bytes 262168
  13.0 0.0 copy-start.4
  13.0 0.7 %copy-done.4 = s32[16]{0:T(128)S(1)} copy-done((s32[16]{0:T(128)S(1)}, s32[16]{0:T(128)}, u32[]{:S(2)}) %copy-start.4) | copy-done | bytes 88
  13.7 2.8 %degree.1 = (bf16[16,64,128]{2,1,0:T(8,128)(2,1)S(1)}, f32[8,2048]{1,0:T(8,128)S(1)}) custom-call(s32[16]{0:T(128)S(1)} %copy-done.4, bf16[16,16,128,128]{3,2,1,0:T(8,128)(2,1)S(1)} %copy-done, bf16[64,2048]{1,0:T(8,128)(2,1)S(1)} %copy-done.2), custom_call_target="tpu_custom_call" | custom-call | flops 67108864 | bytes 8388608 | tf_op jit(solution)/shard_map/degree/pallas_call | solution.py:164
  16.5 0.0 collective-permute-done.2
  16.5 0.6 %select.1 = (bf16[2,2,64,128]{3,2,1,0:T(8,128)(2,1)S(1)}, bf16[2,2,64,128]{3,2,1,0:T(8,128)(2,1)S(1)}, bf16[2,2,64,128]{3,2,1,0:T(8,128)(2,1)S(1)}, bf16[2,2,64,128]{3,2,1,0:T(8,128)(2,1)S(1)}) custom-call(s32[1]{0:T(128)} %bitcast.me_ref, s32[8,16]{1,0:T(8,128)S(1)} %pad_add_fusion.lists_ref, bf16[16,64,128]{2,1,0:T(8,128)(2,1)S(1)} %get-tuple-element.14.scaled_ref), custom_call_target="tpu_custom_call" | custom-call | tf_op jit(solution)/shard_map/select/pallas_call | solution.py:179
  17.2 1.6 %collective-permute-start.3 = (bf16[2,2,64,128]{3,2,1,0:T(8,128)(2,1)S(1)}, bf16[2,2,64,128]{3,2,1,0:T(8,128)(2,1)S(1)}, u32[]{:S(2)}, u32[]{:S(2)}) collective-permute-start(bf16[2,2,64,128]{3,2,1,0:T(8,128)(2,1)S(1)} %get-tuple-element.16), channel_id=1, source_target_pairs={{0,2},{1,3},{2,0},{3,1},{4,6},{5,7},{6,4},{7,5},{8,10},{9,11},{10,... | collective-permute-start | bytes 196616 | tf_op jit(solution)/shard_map/ppermute | solution.py:145
  18.7 0.5 collective-permute-start.4
  19.2 1.5 %collective-permute-start.5 = (bf16[2,2,64,128]{3,2,1,0:T(8,128)(2,1)S(1)}, bf16[2,2,64,128]{3,2,1,0:T(8,128)(2,1)S(1)}, u32[]{:S(2)}, u32[]{:S(2)}) collective-permute-start(bf16[2,2,64,128]{3,2,1,0:T(8,128)(2,1)S(1)} %get-tuple-element.18), channel_id=1, source_target_pairs={{0,6},{1,7},{2,4},{3,5},{4,2},{5,3},{6,0},{7,1},{8,14},{9,15},{10,... | collective-permute-start | bytes 196616 | tf_op jit(solution)/shard_map/ppermute | solution.py:145
  20.7 1.3 %collective-permute-done.3.refs_0_ = bf16[2,2,64,128]{3,2,1,0:T(8,128)(2,1)S(1)} collective-permute-done((bf16[2,2,64,128]{3,2,1,0:T(8,128)(2,1)S(1)}, bf16[2,2,64,128]{3,2,1,0:T(8,128)(2,1)S(1)}, u32[]{:S(2)}, u32[]{:S(2)}) %collective-permute-start.3) | collective-permute-done | bytes 65568 | tf_op jit(solution)/shard_map/ppermute | solution.py:145
  22.0 0.9 %collective-permute-done.4.refs_1_ = bf16[2,2,64,128]{3,2,1,0:T(8,128)(2,1)S(1)} collective-permute-done((bf16[2,2,64,128]{3,2,1,0:T(8,128)(2,1)S(1)}, bf16[2,2,64,128]{3,2,1,0:T(8,128)(2,1)S(1)}, u32[]{:S(2)}, u32[]{:S(2)}) %collective-permute-start.4) | collective-permute-done | bytes 65568 | tf_op jit(solution)/shard_map/ppermute | solution.py:145
  23.0 1.4 %collective-permute-done.5.refs_2_ = bf16[2,2,64,128]{3,2,1,0:T(8,128)(2,1)S(1)} collective-permute-done((bf16[2,2,64,128]{3,2,1,0:T(8,128)(2,1)S(1)}, bf16[2,2,64,128]{3,2,1,0:T(8,128)(2,1)S(1)}, u32[]{:S(2)}, u32[]{:S(2)}) %collective-permute-start.5) | collective-permute-done | bytes 65568 | tf_op jit(solution)/shard_map/ppermute | solution.py:145
  24.4 0.1 collective-permute-start.6
  24.5 1.3 %collective-permute-done.6.refs_3_ = bf16[4,2,64,128]{3,2,1,0:T(8,128)(2,1)S(1)} collective-permute-done((bf16[4,2,64,128]{3,2,1,0:T(8,128)(2,1)S(1)}, bf16[4,2,64,128]{3,2,1,0:T(8,128)(2,1)S(1)}, u32[]{:S(2)}, u32[]{:S(2)}) %collective-permute-start.6) | collective-permute-done | bytes 131104 | tf_op jit(solution)/shard_map/ppermute | solution.py:145
  25.8 0.0 copy-done.5
  25.8 0.0 copy-done.3
  25.8 0.0 copy-start.1
  25.8 3.4 %copy-done.1 = bf16[16,16,128,128]{3,2,1,0:T(8,128)(2,1)S(1)} copy-done((bf16[16,16,128,128]{3,2,1,0:T(8,128)(2,1)S(1)}, bf16[16,16,128,128]{3,2,1,0:T(8,128)(2,1)}, u32[]{:S(2)}) %copy-start.1) | copy-done | bytes 8388632
  29.2 4.1 %product.1 = (bf16[128,2048]{1,0:T(8,128)(2,1)S(1)}, f32[32,128]{1,0:T(8,128)S(1)}) custom-call(s32[1]{0:T(128)} %bitcast.me_ref, s32[16]{0:T(128)S(1)} %copy-done.5, s32[16,16]{1,0:T(8,128)S(1)} %copy-done.3, f32[8,2048]{1,0:T(8,128)S(1)} %get-tuple-element.13.inv_ref, bf16[16,16,128,128]{3,2,1,0:T(8,128)(2,1)S(1)} %copy-done.1, ...), custom_call_target="tpu_custom_call" | custom-call | flops 536870912 | bytes 8388608 | tf_op jit(solution)/shard_map/product/pallas_call | solution.py:192
  33.4 0.2 collective-permute-start.7
  33.5 1.0 %collective-permute-done.7 = f32[32,128]{1,0:T(8,128)S(1)} collective-permute-done((f32[32,128]{1,0:T(8,128)S(1)}, f32[32,128]{1,0:T(8,128)S(1)}, u32[]{:S(2)}, u32[]{:S(2)}) %collective-permute-start.7) | collective-permute-done | bytes 16416 | tf_op jit(solution)/shard_map/ppermute | solution.py:145
  34.6 0.1 collective-permute-start.8
  34.7 3.7 %collective-permute-done.8 = f32[32,128]{1,0:T(8,128)S(1)} collective-permute-done((f32[32,128]{1,0:T(8,128)S(1)}, f32[32,128]{1,0:T(8,128)S(1)}, u32[]{:S(2)}, u32[]{:S(2)}) %collective-permute-start.8) | collective-permute-done | bytes 16416 | tf_op jit(solution)/shard_map/ppermute | solution.py:145
  38.3 1.5 %collective-permute-start.9 = (f32[32,128]{1,0:T(8,128)S(1)}, f32[32,128]{1,0:T(8,128)S(1)}, u32[]{:S(2)}, u32[]{:S(2)}) collective-permute-start(f32[32,128]{1,0:T(8,128)S(1)} %add.13), channel_id=1, source_target_pairs={{0,4},{1,5},{2,6},{3,7},{4,0},{5,1},{6,2},{7,3},{8,12},{9,13},{10,... | collective-permute-start | bytes 49160 | tf_op jit(solution)/shard_map/ppermute | solution.py:145
  39.8 2.2 %collective-permute-done.9 = f32[32,128]{1,0:T(8,128)S(1)} collective-permute-done((f32[32,128]{1,0:T(8,128)S(1)}, f32[32,128]{1,0:T(8,128)S(1)}, u32[]{:S(2)}, u32[]{:S(2)}) %collective-permute-start.9) | collective-permute-done | bytes 16416 | tf_op jit(solution)/shard_map/ppermute | solution.py:145
  42.1 1.6 %collective-permute-start.10 = (f32[32,128]{1,0:T(8,128)S(1)}, f32[32,128]{1,0:T(8,128)S(1)}, u32[]{:S(2)}, u32[]{:S(2)}) collective-permute-start(f32[32,128]{1,0:T(8,128)S(1)} %add.14), channel_id=1, source_target_pairs={{0,8},{8,0},{16,24},{24,16},{1,9},{9,1},{17,25},{25,17},{2,10},{10... | collective-permute-start | bytes 49160 | tf_op jit(solution)/shard_map/ppermute | solution.py:145
  43.6 2.2 %collective-permute-done.10 = f32[32,128]{1,0:T(8,128)S(1)} collective-permute-done((f32[32,128]{1,0:T(8,128)S(1)}, f32[32,128]{1,0:T(8,128)S(1)}, u32[]{:S(2)}, u32[]{:S(2)}) %collective-permute-start.10) | collective-permute-done | bytes 16416 | tf_op jit(solution)/shard_map/ppermute | solution.py:145
  45.8 2.6 %collective-permute-start.11 = (f32[32,128]{1,0:T(8,128)S(1)}, f32[32,128]{1,0:T(8,128)S(1)}, u32[]{:S(2)}, u32[]{:S(2)}) collective-permute-start(f32[32,128]{1,0:T(8,128)S(1)} %add.15.here_ref), channel_id=1, source_target_pairs={{0,16},{8,24},{16,0},{24,8},{1,17},{9,25},{17,1},{25,9},{2,18},{10... | collective-permute-start | bytes 49160 | tf_op jit(solution)/shard_map/ppermute | solution.py:145
  48.4 2.0 %collective-permute-done.11.there_ref = f32[32,128]{1,0:T(8,128)S(1)} collective-permute-done((f32[32,128]{1,0:T(8,128)S(1)}, f32[32,128]{1,0:T(8,128)S(1)}, u32[]{:S(2)}, u32[]{:S(2)}) %collective-permute-start.11) | collective-permute-done | bytes 16416 | tf_op jit(solution)/shard_map/ppermute | solution.py:145
  50.4 3.2 %solve.1 = f32[64,2048]{1,0:T(8,128)} custom-call(f32[32,128]{1,0:T(8,128)S(1)} %add.15.here_ref, f32[32,128]{1,0:T(8,128)S(1)} %collective-permute-done.11.there_ref, bf16[128,2048]{1,0:T(8,128)(2,1)S(1)} %get-tuple-element.20.applied_ref), custom_call_target="tpu_custom_call" | custom-call | tf_op jit(solution)/shard_map/solve/pallas_call | solution.py:213
  (12 shorter events, 0.1 us)
Async XLA Ops:
  0.0 25.8 %copy-start.5 = (s32[16]{0:T(128)S(1)}, s32[16]{0:T(128)}, u32[]{:S(2)}) copy-start(s32[16]{0:T(128)} %count_ref.3) | copy-start | bytes 196
  0.0 25.8 %copy-start.3 = (s32[16,16]{1,0:T(8,128)S(1)}, s32[16,16]{1,0:T(8,128)}, u32[]{:S(2)}) copy-start(s32[16,16]{1,0:T(8,128)} %slot_ref.1) | copy-start | bytes 3076
  0.9 1.3 %collective-permute-start = (s32[1,16]{1,0:T(1,128)S(1)}, s32[1,16]{1,0:T(1,128)S(1)}, u32[]{:S(2)}, u32[]{:S(2)}) collective-permute-start(s32[1,16]{1,0:T(1,128)S(1)} %reshape.7), channel_id=1, source_target_pairs={{0,1},{1,0},{2,3},{3,2},{4,5},{5,4},{6,7},{7,6},{8,9},{9,8},{10,11... | collective-permute-start | bytes 200 | tf_op jit(solution)/shard_map/ppermute | solution.py:145
  2.2 4.4 %collective-permute-start.1 = (s32[2,16]{1,0:T(2,128)S(1)}, s32[2,16]{1,0:T(2,128)S(1)}, u32[]{:S(2)}, u32[]{:S(2)}) collective-permute-start(s32[2,16]{1,0:T(2,128)S(1)} %pad_add_fusion.2), channel_id=1, source_target_pairs={{0,2},{1,3},{2,0},{3,1},{4,6},{5,7},{6,4},{7,5},{8,10},{9,11},{10,... | collective-permute-start | bytes 392 | tf_op jit(solution)/shard_map/ppermute | solution.py:145
  6.6 9.9 %collective-permute-start.2 = (s32[4,16]{1,0:T(4,128)S(1)}, s32[4,16]{1,0:T(4,128)S(1)}, u32[]{:S(2)}, u32[]{:S(2)}) collective-permute-start(s32[4,16]{1,0:T(4,128)S(1)} %pad_add_fusion.1), channel_id=1, source_target_pairs={{0,4},{1,5},{2,6},{3,7},{4,0},{5,1},{6,2},{7,3},{8,12},{9,13},{10,... | collective-permute-start | bytes 776 | tf_op jit(solution)/shard_map/ppermute | solution.py:145
  8.7 3.4 %copy-start = (bf16[16,16,128,128]{3,2,1,0:T(8,128)(2,1)S(1)}, bf16[16,16,128,128]{3,2,1,0:T(8,128)(2,1)}, u32[]{:S(2)}) copy-start(bf16[16,16,128,128]{3,2,1,0:T(8,128)(2,1)} %tiles_ref.3) | copy-start | bytes 25165828
  12.1 0.9 %copy-start.2 = (bf16[64,2048]{1,0:T(8,128)(2,1)S(1)}, bf16[64,2048]{1,0:T(8,128)(2,1)}, u32[]{:S(2)}) copy-start(bf16[64,2048]{1,0:T(8,128)(2,1)} %sub_ref.1) | copy-start | bytes 786436
  13.0 0.7 %copy-start.4 = (s32[16]{0:T(128)S(1)}, s32[16]{0:T(128)}, u32[]{:S(2)}) copy-start(s32[16]{0:T(128)} %count_ref.3) | copy-start | bytes 196
  17.2 4.9 %collective-permute-start.3 = (bf16[2,2,64,128]{3,2,1,0:T(8,128)(2,1)S(1)}, bf16[2,2,64,128]{3,2,1,0:T(8,128)(2,1)S(1)}, u32[]{:S(2)}, u32[]{:S(2)}) collective-permute-start(bf16[2,2,64,128]{3,2,1,0:T(8,128)(2,1)S(1)} %get-tuple-element.16), channel_id=1, source_target_pairs={{0,2},{1,3},{2,0},{3,1},{4,6},{5,7},{6,4},{7,5},{8,10},{9,11},{10,... | collective-permute-start | bytes 196616 | tf_op jit(solution)/shard_map/ppermute | solution.py:145
  18.7 4.3 %collective-permute-start.4 = (bf16[2,2,64,128]{3,2,1,0:T(8,128)(2,1)S(1)}, bf16[2,2,64,128]{3,2,1,0:T(8,128)(2,1)S(1)}, u32[]{:S(2)}, u32[]{:S(2)}) collective-permute-start(bf16[2,2,64,128]{3,2,1,0:T(8,128)(2,1)S(1)} %get-tuple-element.17), channel_id=1, source_target_pairs={{0,4},{1,5},{2,6},{3,7},{4,0},{5,1},{6,2},{7,3},{8,12},{9,13},{10,... | collective-permute-start | bytes 196616 | tf_op jit(solution)/shard_map/ppermute | solution.py:145
  19.2 5.2 %collective-permute-start.5 = (bf16[2,2,64,128]{3,2,1,0:T(8,128)(2,1)S(1)}, bf16[2,2,64,128]{3,2,1,0:T(8,128)(2,1)S(1)}, u32[]{:S(2)}, u32[]{:S(2)}) collective-permute-start(bf16[2,2,64,128]{3,2,1,0:T(8,128)(2,1)S(1)} %get-tuple-element.18), channel_id=1, source_target_pairs={{0,6},{1,7},{2,4},{3,5},{4,2},{5,3},{6,0},{7,1},{8,14},{9,15},{10,... | collective-permute-start | bytes 196616 | tf_op jit(solution)/shard_map/ppermute | solution.py:145
  24.4 1.4 %collective-permute-start.6 = (bf16[4,2,64,128]{3,2,1,0:T(8,128)(2,1)S(1)}, bf16[4,2,64,128]{3,2,1,0:T(8,128)(2,1)S(1)}, u32[]{:S(2)}, u32[]{:S(2)}) collective-permute-start(bf16[4,2,64,128]{3,2,1,0:T(8,128)(2,1)S(1)} %pad_maximum_fusion), channel_id=1, source_target_pairs={{0,1},{1,0},{2,3},{3,2},{4,5},{5,4},{6,7},{7,6},{8,9},{9,8},{10,11... | collective-permute-start | bytes 393224 | tf_op jit(solution)/shard_map/ppermute | solution.py:145
  25.8 3.4 %copy-start.1 = (bf16[16,16,128,128]{3,2,1,0:T(8,128)(2,1)S(1)}, bf16[16,16,128,128]{3,2,1,0:T(8,128)(2,1)}, u32[]{:S(2)}) copy-start(bf16[16,16,128,128]{3,2,1,0:T(8,128)(2,1)} %tiles_ref.3) | copy-start | bytes 25165828
  33.4 1.2 %collective-permute-start.7 = (f32[32,128]{1,0:T(8,128)S(1)}, f32[32,128]{1,0:T(8,128)S(1)}, u32[]{:S(2)}, u32[]{:S(2)}) collective-permute-start(f32[32,128]{1,0:T(8,128)S(1)} %get-tuple-element.19), channel_id=1, source_target_pairs={{0,1},{1,0},{2,3},{3,2},{4,5},{5,4},{6,7},{7,6},{8,9},{9,8},{10,11... | collective-permute-start | bytes 49160 | tf_op jit(solution)/shard_map/ppermute | solution.py:145
  34.6 3.7 %collective-permute-start.8 = (f32[32,128]{1,0:T(8,128)S(1)}, f32[32,128]{1,0:T(8,128)S(1)}, u32[]{:S(2)}, u32[]{:S(2)}) collective-permute-start(f32[32,128]{1,0:T(8,128)S(1)} %add.12), channel_id=1, source_target_pairs={{0,2},{1,3},{2,0},{3,1},{4,6},{5,7},{6,4},{7,5},{8,10},{9,11},{10,... | collective-permute-start | bytes 49160 | tf_op jit(solution)/shard_map/ppermute | solution.py:145
  38.3 3.7 %collective-permute-start.9 = (f32[32,128]{1,0:T(8,128)S(1)}, f32[32,128]{1,0:T(8,128)S(1)}, u32[]{:S(2)}, u32[]{:S(2)}) collective-permute-start(f32[32,128]{1,0:T(8,128)S(1)} %add.13), channel_id=1, source_target_pairs={{0,4},{1,5},{2,6},{3,7},{4,0},{5,1},{6,2},{7,3},{8,12},{9,13},{10,... | collective-permute-start | bytes 49160 | tf_op jit(solution)/shard_map/ppermute | solution.py:145
  42.1 3.7 %collective-permute-start.10 = (f32[32,128]{1,0:T(8,128)S(1)}, f32[32,128]{1,0:T(8,128)S(1)}, u32[]{:S(2)}, u32[]{:S(2)}) collective-permute-start(f32[32,128]{1,0:T(8,128)S(1)} %add.14), channel_id=1, source_target_pairs={{0,8},{8,0},{16,24},{24,16},{1,9},{9,1},{17,25},{25,17},{2,10},{10... | collective-permute-start | bytes 49160 | tf_op jit(solution)/shard_map/ppermute | solution.py:145
  45.8 4.6 %collective-permute-start.11 = (f32[32,128]{1,0:T(8,128)S(1)}, f32[32,128]{1,0:T(8,128)S(1)}, u32[]{:S(2)}, u32[]{:S(2)}) collective-permute-start(f32[32,128]{1,0:T(8,128)S(1)} %add.15.here_ref), channel_id=1, source_target_pairs={{0,16},{8,24},{16,0},{24,8},{1,17},{9,25},{17,1},{25,9},{2,18},{10... | collective-permute-start | bytes 49160 | tf_op jit(solution)/shard_map/ppermute | solution.py:145

commit v3 on v2

v3 whole, which is shorter than its diff:
```python
import jax
import jax.numpy as jnp
from jax import lax
from jax.experimental import pallas as pl
from jax.experimental.pallas import tpu as pltpu
from jax.sharding import PartitionSpec as P

VMEM = pl.BlockSpec(memory_space=pltpu.VMEM)
SMEM = pl.BlockSpec(memory_space=pltpu.SMEM)
NT = (((1,), (1,)), ((), ()))
F32 = jnp.float32
BF16 = jnp.bfloat16


def limit(mib):
    return pltpu.CompilerParams(vmem_limit_bytes=mib << 20)


def split(x):
    high = x.astype(BF16)
    return high, (x - high.astype(F32)).astype(BF16)


def start_kernel(out_ref):
    out_ref[...] = jnp.zeros_like(out_ref)


def degree_kernel(first_ref, count_ref, tiles_ref, inv_ref):
    blocks, slots, rows, cols = tiles_ref.shape
    ones = jnp.ones((8, 2 * cols), BF16)
    slot_of_lane = lax.broadcasted_iota(jnp.int32, (8, slots * cols), 1) // cols
    for b in range(blocks):
        count = count_ref[b]
        tiles = [tiles_ref[b, t] for t in range(slots)]
        if b % 2:
            total = sum(
                tile.astype(F32) * jnp.where(t < count, 1.0, 0.0) for t, tile in enumerate(tiles)
            )
            live, row = ones, split(total)
        else:
            live = (slot_of_lane < count).astype(F32).astype(BF16)
            row = tiles
        degree = lax.dot_general(
            live, jnp.concatenate(row, axis=1), NT, preferred_element_type=F32
        )
        inv_ref[b : b + 1] = lax.rsqrt(degree[:1])


def select_kernel(*refs):
    chips = (len(refs) - 4) // 2
    list_refs, (sub_ref, sib_sub_ref, inv_ref, sib_inv_ref), send_refs = (
        refs[:chips],
        refs[chips : chips + 4],
        refs[chips + 4 :],
    )
    cap, cols = list_refs[0].shape[1], inv_ref.shape[1]
    me = lax.axis_index("dev")
    sources = ((me, sub_ref, inv_ref), (me ^ 1, sib_sub_ref, sib_inv_ref))
    for wanted, send in zip(list_refs, send_refs, strict=True):
        for core, (source, columns, inv) in enumerate(sources):
            for j in range(cap):
                block = wanted[0, j, source]
                lanes = pl.ds(pl.multiple_of(block * cols, cols), cols)
                scaled = columns[:, lanes].astype(F32) * inv[pl.ds(block, 1), :]
                send[core, j] = scaled.astype(BF16)


def product_kernel(count_ref, slot_ref, inv_ref, tiles_ref, *refs):
    *part_refs, applied_ref, gram_ref, table = refs
    blocks, slots, rows, cols = tiles_ref.shape
    _, cap, k_dim, _ = part_refs[0].shape
    me = lax.axis_index("dev")
    dead = table.shape[0] - 1
    table[dead] = jnp.zeros((k_dim, cols), BF16)
    for i, part in enumerate(part_refs):
        for core in range(2):
            for j in range(cap):
                table[((2 * i + core) ^ me) * cap + j] = part[core, j]
    for b in range(blocks):
        count = count_ref[b]
        parts = [table[jnp.where(t < count, slot_ref[b, t], dead)] for t in range(slots)]
        total = lax.dot_general(
            jnp.concatenate(parts, axis=1),
            jnp.concatenate([tiles_ref[b, t] for t in range(slots)], axis=1),
            NT,
            preferred_element_type=F32,
        )
        lanes = slice(b * rows, (b + 1) * rows)
        high, low = split(total * inv_ref[b : b + 1])
        applied_ref[:k_dim, lanes] = high
        applied_ref[k_dim:, lanes] = low
    both = applied_ref[...]
    wide = lax.dot_general(both, both, NT, preferred_element_type=F32)
    wide = wide[:k_dim] + wide[k_dim:]
    gram = wide[:, :k_dim] + wide[:, k_dim:]
    half = k_dim // 2
    gram_ref[...] = jnp.concatenate([gram[:half], gram[half:]], axis=1)


def inverse_factor(gram):
    k_dim = gram.shape[0]
    wide, groups = 2 * k_dim, k_dim // 8
    square = (k_dim, k_dim)
    eye = (
        lax.broadcasted_iota(jnp.int32, square, 0) == lax.broadcasted_iota(jnp.int32, square, 1)
    ).astype(F32)
    diagonal = gram * eye
    row_scale = lax.rsqrt(jnp.sum(diagonal, axis=1, keepdims=True))
    col_scale = lax.rsqrt(jnp.sum(diagonal, axis=0, keepdims=True))
    whole = jnp.concatenate([gram * row_scale * col_scale, eye * col_scale], axis=1)
    rows = [whole[8 * i : 8 * i + 8] for i in range(groups)]
    row_ids = lax.broadcasted_iota(jnp.int32, (8, wide), 0)

    def spread(x):
        return jnp.broadcast_to(x, (8, wide))

    done = []
    for g in range(groups):
        column = {
            (i, b): spread(rows[i][:, 8 * g + b : 8 * g + b + 1])
            for i in range(g, groups)
            for b in range(8)
        }
        out = rows[g]
        for s in range(0, 8, 2):
            row0, row1 = spread(rows[g][s : s + 1]), spread(rows[g][s + 1 : s + 2])
            pivot0 = {b: spread(column[g, b][s : s + 1]) for b in range(s, 8)}
            pivot1 = {b: spread(column[g, b][s + 1 : s + 2]) for b in range(s, 8)}
            p00, p01, p11 = pivot0[s], pivot0[s + 1], pivot1[s + 1]
            det = p00 * p11 - p01 * p01
            inv_det = pl.reciprocal(det, approx=True)
            inv_det = inv_det * (2.0 - det * inv_det)
            q00, q01, q11 = p11 * inv_det, p01 * inv_det, p00 * inv_det
            root0 = lax.rsqrt(p00)
            ratio = p01 * (root0 * root0)
            root1 = lax.rsqrt(p11 - p01 * ratio)
            out = jnp.where(row_ids == s, row0 * root0, out)
            out = jnp.where(row_ids == s + 1, (row1 - ratio * row0) * root1, out)
            for i in range(g, groups):
                x, y = column[i, s], column[i, s + 1]
                f0, f1 = q00 * x - q01 * y, q11 * y - q01 * x
                if i == g:
                    f0 = jnp.where(row_ids > s + 1, f0, 0.0)
                    f1 = jnp.where(row_ids > s + 1, f1, 0.0)
                rows[i] = rows[i] - f0 * row0 - f1 * row1
                for b in range(s + 2, 8):
                    column[i, b] = column[i, b] - f0 * pivot0[b] - f1 * pivot1[b]
        done.append(out)
    return jnp.concatenate(done, axis=0)[:, k_dim:]


def solve_kernel(gram_ref, applied_ref, out_ref):
    k_dim = gram_ref.shape[1] // 2
    packed = gram_ref[...]
    gram = jnp.concatenate([packed[:, :k_dim], packed[:, k_dim:]], axis=0)
    high, low = split(inverse_factor(gram))
    out_ref[...] = jnp.dot(
        jnp.concatenate([high, high, low], axis=1),
        jnp.concatenate([applied_ref[...], applied_ref[:k_dim]], axis=0),
        preferred_element_type=F32,
    )


def swap(x, axis, mask, odd_mask=None):
    odd = mask if odd_mask is None else odd_mask
    size = lax.axis_size(axis)
    core = lax.axis_size("dev") if axis != "dev" else 1
    if odd_mask is None or axis == "dev":
        return lax.ppermute(x, axis, [(i, i ^ (odd if i % 2 else mask)) for i in range(size)])
    pairs = [(i, i ^ (core * (odd if i % 2 else mask))) for i in range(size * core)]
    return lax.ppermute(x, (axis, "dev"), pairs)


def stages(axis):
    masks = [1 << i for i in range(axis == "dev", lax.axis_size(axis).bit_length() - 1)]
    return [masks[i : i + 2] for i in range(0, len(masks), 2)]


def sum_all(x):
    x = x + swap(x, "dev", 1)
    for axis in ("dev", "grp"):
        for masks in stages(axis):
            if len(masks) == 1:
                parts = [swap(x, axis, masks[0])]
            else:
                mine = swap(x, axis, *masks)
                both = swap(x, axis, masks[0] ^ masks[1])
                parts = [mine, both, swap(mine, "dev", 1)]
            x = x + sum(parts)
    return x


def body(subspace, tiles, tile_count, tile_slot, fetch_list):
    k_dim, row_count = subspace.shape
    blocks, slots, rows, cols = tiles.shape
    peers = lax.axis_size("dev")
    cap = fetch_list.shape[2]
    chips = peers // 2
    first = pl.pallas_call(
        start_kernel,
        out_shape=jax.ShapeDtypeStruct((8, 128), F32),
        out_specs=VMEM,
        compiler_params=limit(1),
        cost_estimate=pl.CostEstimate(flops=10**10, bytes_accessed=0, transcendentals=0),
        name="start",
    )()
    first, lists = lax.optimization_barrier((first, jnp.transpose(fetch_list, (0, 2, 1))))
    lists = [lists] + [swap(lists, "dev", 2 * i) for i in range(1, chips)]
    sib_columns = swap(subspace, "dev", 1)

    inv_root = pl.pallas_call(
        degree_kernel,
        out_shape=jax.ShapeDtypeStruct((blocks, rows), F32),
        in_specs=[VMEM, SMEM, VMEM],
        out_specs=VMEM,
        compiler_params=limit(4),
        cost_estimate=pl.CostEstimate(
            flops=16 * tiles.size, bytes_accessed=2 * tiles.size, transcendentals=0
        ),
        name="degree",
    )(first, tile_count, tiles)
    inv_root, *lists = lax.optimization_barrier((inv_root, *lists))
    sib_inv_root = swap(inv_root, "dev", 1)

    sends = pl.pallas_call(
        select_kernel,
        out_shape=[jax.ShapeDtypeStruct((2, cap, k_dim, cols), BF16)] * chips,
        in_specs=[SMEM] * chips + [VMEM] * 4,
        out_specs=[VMEM] * chips,
        compiler_params=limit(2),
        name="select",
    )(*lists, subspace, sib_columns, inv_root, sib_inv_root)
    parts = [sends[0]] + [swap(sends[i], "dev", 2 * i) for i in range(1, chips)]

    applied, gram = pl.pallas_call(
        product_kernel,
        out_shape=(
            jax.ShapeDtypeStruct((2 * k_dim, row_count), BF16),
            jax.ShapeDtypeStruct((k_dim // 2, 2 * k_dim), F32),
        ),
        in_specs=[SMEM, SMEM] + [VMEM] * (chips + 2),
        out_specs=(VMEM, VMEM),
        scratch_shapes=[pltpu.VMEM((peers * cap + 1, k_dim, cols), BF16)],
        compiler_params=limit(4),
        cost_estimate=pl.CostEstimate(
            flops=2 * tiles.size * k_dim, bytes_accessed=2 * tiles.size, transcendentals=0
        ),
        name="product",
    )(tile_count, tile_slot, inv_root, tiles, *parts)

    gram = sum_all(gram)

    return pl.pallas_call(
        solve_kernel,
        out_shape=jax.ShapeDtypeStruct((k_dim, row_count), F32),
        in_specs=[VMEM] * 2,
        out_specs=VMEM,
        compiler_params=limit(4),
        name="solve",
    )(gram, applied)


def solution(mesh):
    placed = (
        P(None, ("grp", "dev")),
        P(("grp", "dev"), None, None, None),
        P(("grp", "dev")),
        P(("grp", "dev"), None),
        P(("grp", "dev"), None, None),
    )
    return jax.shard_map(
        body, mesh=mesh, in_specs=placed, out_specs=P(None, ("grp", "dev")), check_vma=False
    )
```

time: 53.9 us -> 39.8 us (0.74)
  local copies, waits for them, and re-layouts: 9.25 us -> 0.16 us
  waiting for transfers between devices: 18.5 us -> 14.7 us
  Pallas kernels: 10.8 us -> 10.1 us
    unnamed x13 -> x10, local copies, waits for them, and re-layouts: 9.16 us -> 0.16 us
    ppermute x12 -> x15, waiting for transfers between devices: 18.5 us -> 14.7 us  [the longest x14 14.7 us: swap(): lax.ppermute(x, axis, [(i, i ^ (odd if i % 2 else mask)) for i in range(s...]
    pallas_call x1 -> x2, Pallas kernels: 2.82 us -> 2.11 us  [the longest x1 2.11 us: body(): pl.pallas_call(degree_kernel, out_shape=jax.ShapeDtypeStruct((blocks, row...]
    ppermute x12 -> x15, starting transfers between devices: 15 us -> 14.6 us  [the longest x14 13 us: swap(): lax.ppermute(x, axis, [(i, i ^ (odd if i % 2 else mask)) for i in range(s...]
  transfers between devices with their start and end apart: 12 -> 15, of which waited for: 11 -> 10; matrix products, arithmetic and copies ran while one was open for 0% -> 0% of each run, Pallas kernels for 5% -> 5%
where the time goes in v3:
time: 39.8 us; the launch traced here: 39.6 us
  waiting for transfers between devices  14.7 us (37%)
  starting transfers between devices  14.6 us (37%)
  Pallas kernels  10.1 us (25%)
    ppermute x14, waiting for transfers between devices, swap(): lax.ppermute(x, axis, [(i, i ^ (odd if i % 2 else mask)) for i in range(s...  14.7 us
    ppermute x14, starting transfers between devices, swap(): lax.ppermute(x, axis, [(i, i ^ (odd if i % 2 else mask)) for i in range(s...  13 us
    pallas_call x1, Pallas kernels, body(): pl.pallas_call(product_kernel, out_shape=(jax.ShapeDtypeStruct((2 * k_dim...  4.1 us
    pallas_call x1, Pallas kernels, body(): pl.pallas_call(solve_kernel, out_shape=jax.ShapeDtypeStruct((k_dim, row_c...  3.17 us
    pallas_call x1, Pallas kernels, body(): pl.pallas_call(degree_kernel, out_shape=jax.ShapeDtypeStruct((blocks, row...  2.11 us
    ppermute x1, starting transfers between devices, swap(): return lax.ppermute(x, (axis, 'dev'), pairs)  1.64 us
  transfers between devices with their start and end apart: 15, of which 10 were waited for; matrix products, arithmetic and copies ran while one was open for 0% of the time, Pallas kernels for 5%

profile of v3, /device:TPU:0, one launch (start us, length us, event | category | flops | bytes accessed | tf_op | source)
XLA Modules:
  0.0 39.6 jit_solution(6366955549310354527)
XLA Ops:
  0.0 0.0 copy-start.4
  0.0 0.0 copy-start.3
  0.0 0.0 copy-start
  0.0 0.5 %collective-permute-start.3 = (bf16[64,2048]{1,0:T(8,128)(2,1)}, bf16[64,2048]{1,0:T(8,128)(2,1)S(1)}, u32[]{:S(2)}, u32[]{:S(2)}) collective-permute-start(bf16[64,2048]{1,0:T(8,128)(2,1)} %refs_4_.1), channel_id=1, source_target_pairs={{0,1},{1,0},{2,3},{3,2},{4,5},{5,4},{6,7},{7,6},{8,9},{9,8},{10,11... | collective-permute-start | bytes 786440 | tf_op jit(solution)/shard_map/ppermute | solution.py:169
  0.5 0.0 copy-start.1
  0.5 0.0 copy-start.2
  0.5 0.1 copy-done.4
  0.7 3.9 %collective-permute-start.2 = (s32[1,2,8]{2,1,0:T(2,128)S(1)}, s32[1,2,8]{2,1,0:T(2,128)S(1)}, u32[]{:S(2)}, u32[]{:S(2)}) collective-permute-start(s32[1,2,8]{2,1,0:T(2,128)S(1)} %bitcast.1), channel_id=1, source_target_pairs={{0,6},{1,7},{2,4},{3,5},{4,2},{5,3},{6,0},{7,1},{8,14},{9,15},{10,... | collective-permute-start | bytes 200 | tf_op jit(solution)/shard_map/ppermute | solution.py:169
  4.6 0.5 %collective-permute-start.1 = (s32[1,2,8]{2,1,0:T(2,128)S(1)}, s32[1,2,8]{2,1,0:T(2,128)S(1)}, u32[]{:S(2)}, u32[]{:S(2)}) collective-permute-start(s32[1,2,8]{2,1,0:T(2,128)S(1)} %bitcast.2), channel_id=1, source_target_pairs={{0,4},{1,5},{2,6},{3,7},{4,0},{5,1},{6,2},{7,3},{8,12},{9,13},{10,... | collective-permute-start | bytes 200 | tf_op jit(solution)/shard_map/ppermute | solution.py:169
  5.1 0.1 collective-permute-start
  5.1 0.0 copy-done.3
  5.1 0.0 copy-done
  5.1 2.1 %degree.1.refs_6_.inv_ref = f32[16,128]{1,0:T(8,128)S(1)} custom-call(f32[8,128]{1,0:T(8,128)S(1)} %start.1.first_ref, s32[16]{0:T(128)S(1)} %copy-done.3, bf16[16,16,128,128]{3,2,1,0:T(8,128)(2,1)S(1)} %copy-done), custom_call_target="tpu_custom_call" | custom-call | flops 67108864 | bytes 8388608 | tf_op jit(solution)/shard_map/degree/pallas_call | solution.py:211
  7.3 0.0 collective-permute-done.2.refs_3_
  7.3 0.9 %collective-permute-done.1.refs_2_ = s32[1,2,8]{2,1,0:T(2,128)S(1)} collective-permute-done((s32[1,2,8]{2,1,0:T(2,128)S(1)}, s32[1,2,8]{2,1,0:T(2,128)S(1)}, u32[]{:S(2)}, u32[]{:S(2)}) %collective-permute-start.1) | collective-permute-done | bytes 96 | tf_op jit(solution)/shard_map/ppermute | solution.py:169
  8.1 0.5 %collective-permute-done.refs_1_ = s32[1,2,8]{2,1,0:T(2,128)S(1)} collective-permute-done((s32[1,2,8]{2,1,0:T(2,128)S(1)}, s32[1,2,8]{2,1,0:T(2,128)S(1)}, u32[]{:S(2)}, u32[]{:S(2)}) %collective-permute-start) | collective-permute-done | bytes 96 | tf_op jit(solution)/shard_map/ppermute | solution.py:169
  8.7 0.0 collective-permute-start.4
  8.7 1.2 %collective-permute-done.4.refs_7_ = f32[16,128]{1,0:T(8,128)S(1)} collective-permute-done((f32[16,128]{1,0:T(8,128)S(1)}, f32[16,128]{1,0:T(8,128)S(1)}, u32[]{:S(2)}, u32[]{:S(2)}) %collective-permute-start.4) | collective-permute-done | bytes 8224 | tf_op jit(solution)/shard_map/ppermute | solution.py:169
  9.8 0.0 collective-permute-done.3.refs_5_
  9.8 0.0 copy-done.1
  9.8 0.7 %select.1 = (bf16[2,2,64,128]{3,2,1,0:T(8,128)(2,1)S(1)}, bf16[2,2,64,128]{3,2,1,0:T(8,128)(2,1)S(1)}, bf16[2,2,64,128]{3,2,1,0:T(8,128)(2,1)S(1)}, bf16[2,2,64,128]{3,2,1,0:T(8,128)(2,1)S(1)}) custom-call(s32[1,2,8]{2,1,0:T(2,128)S(1)} %bitcast.4, s32[1,2,8]{2,1,0:T(2,128)S(1)} %collective-permute-done.refs_1_, ...), custom_call_target="tpu_custom_call" | custom-call | tf_op jit(solution)/shard_map/select/pallas_call | solution.py:225
  10.5 0.7 %collective-permute-start.5 = (bf16[2,2,64,128]{3,2,1,0:T(8,128)(2,1)S(1)}, bf16[2,2,64,128]{3,2,1,0:T(8,128)(2,1)S(1)}, u32[]{:S(2)}, u32[]{:S(2)}) collective-permute-start(bf16[2,2,64,128]{3,2,1,0:T(8,128)(2,1)S(1)} %get-tuple-element.26), channel_id=1, source_target_pairs={{0,2},{1,3},{2,0},{3,1},{4,6},{5,7},{6,4},{7,5},{8,10},{9,11},{10,... | collective-permute-start | bytes 196616 | tf_op jit(solution)/shard_map/ppermute | solution.py:169
  11.3 1.5 %collective-permute-start.6 = (bf16[2,2,64,128]{3,2,1,0:T(8,128)(2,1)S(1)}, bf16[2,2,64,128]{3,2,1,0:T(8,128)(2,1)S(1)}, u32[]{:S(2)}, u32[]{:S(2)}) collective-permute-start(bf16[2,2,64,128]{3,2,1,0:T(8,128)(2,1)S(1)} %get-tuple-element.27), channel_id=1, source_target_pairs={{0,4},{1,5},{2,6},{3,7},{4,0},{5,1},{6,2},{7,3},{8,12},{9,13},{10,... | collective-permute-start | bytes 196616 | tf_op jit(solution)/shard_map/ppermute | solution.py:169
  12.8 1.3 %collective-permute-start.7 = (bf16[2,2,64,128]{3,2,1,0:T(8,128)(2,1)S(1)}, bf16[2,2,64,128]{3,2,1,0:T(8,128)(2,1)S(1)}, u32[]{:S(2)}, u32[]{:S(2)}) collective-permute-start(bf16[2,2,64,128]{3,2,1,0:T(8,128)(2,1)S(1)} %get-tuple-element.28), channel_id=1, source_target_pairs={{0,6},{1,7},{2,4},{3,5},{4,2},{5,3},{6,0},{7,1},{8,14},{9,15},{10,... | collective-permute-start | bytes 196616 | tf_op jit(solution)/shard_map/ppermute | solution.py:169
  14.1 0.8 %collective-permute-done.5.refs_1_ = bf16[2,2,64,128]{3,2,1,0:T(8,128)(2,1)S(1)} collective-permute-done((bf16[2,2,64,128]{3,2,1,0:T(8,128)(2,1)S(1)}, bf16[2,2,64,128]{3,2,1,0:T(8,128)(2,1)S(1)}, u32[]{:S(2)}, u32[]{:S(2)}) %collective-permute-start.5) | collective-permute-done | bytes 65568 | tf_op jit(solution)/shard_map/ppermute | solution.py:169
  14.9 0.7 %collective-permute-done.6.refs_2_ = bf16[2,2,64,128]{3,2,1,0:T(8,128)(2,1)S(1)} collective-permute-done((bf16[2,2,64,128]{3,2,1,0:T(8,128)(2,1)S(1)}, bf16[2,2,64,128]{3,2,1,0:T(8,128)(2,1)S(1)}, u32[]{:S(2)}, u32[]{:S(2)}) %collective-permute-start.6) | collective-permute-done | bytes 65568 | tf_op jit(solution)/shard_map/ppermute | solution.py:169
  15.5 2.4 %collective-permute-done.7.refs_3_ = bf16[2,2,64,128]{3,2,1,0:T(8,128)(2,1)S(1)} collective-permute-done((bf16[2,2,64,128]{3,2,1,0:T(8,128)(2,1)S(1)}, bf16[2,2,64,128]{3,2,1,0:T(8,128)(2,1)S(1)}, u32[]{:S(2)}, u32[]{:S(2)}) %collective-permute-start.7) | collective-permute-done | bytes 65568 | tf_op jit(solution)/shard_map/ppermute | solution.py:169
  17.9 0.0 copy-done.2
  18.0 4.1 %product.1 = (bf16[128,2048]{1,0:T(8,128)(2,1)S(1)}, f32[32,128]{1,0:T(8,128)S(1)}) custom-call(s32[16]{0:T(128)S(1)} %copy-done.3, s32[16,16]{1,0:T(8,128)S(1)} %copy-done.2, f32[16,128]{1,0:T(8,128)S(1)} %degree.1.refs_6_.inv_ref, bf16[16,16,128,128]{3,2,1,0:T(8,128)(2,1)S(1)} %copy-done, bf16[2,2,64,128]{3,2,1,0:T(8,128)(2,1)S(1)} %get-tuple-element.25.refs_0_, ...), custom_call_target="tpu_custom_call" | custom-call | flops 536870912 | bytes 8388608 | tf_op jit(solution)/shard_map/product/pallas_call | solution.py:235
  22.0 0.0 collective-permute-start.8
  22.1 1.2 %collective-permute-done.8 = f32[32,128]{1,0:T(8,128)S(1)} collective-permute-done((f32[32,128]{1,0:T(8,128)S(1)}, f32[32,128]{1,0:T(8,128)S(1)}, u32[]{:S(2)}, u32[]{:S(2)}) %collective-permute-start.8) | collective-permute-done | bytes 16416 | tf_op jit(solution)/shard_map/ppermute | solution.py:169
  23.3 1.3 %collective-permute-start.9 = (f32[32,128]{1,0:T(8,128)S(1)}, f32[32,128]{1,0:T(8,128)S(1)}, u32[]{:S(2)}, u32[]{:S(2)}) collective-permute-start(f32[32,128]{1,0:T(8,128)S(1)} %add.21), channel_id=1, source_target_pairs={{0,2},{1,5},{2,0},{3,7},{4,6},{5,1},{6,4},{7,3},{8,10},{9,13},{10,... | collective-permute-start | bytes 49160 | tf_op jit(solution)/shard_map/ppermute | solution.py:169
  24.6 0.6 %collective-permute-start.10 = (f32[32,128]{1,0:T(8,128)S(1)}, f32[32,128]{1,0:T(8,128)S(1)}, u32[]{:S(2)}, u32[]{:S(2)}) collective-permute-start(f32[32,128]{1,0:T(8,128)S(1)} %add.21), channel_id=1, source_target_pairs={{0,6},{1,7},{2,4},{3,5},{4,2},{5,3},{6,0},{7,1},{8,14},{9,15},{10,... | collective-permute-start | bytes 49160 | tf_op jit(solution)/shard_map/ppermute | solution.py:169
  25.2 1.8 %collective-permute-done.9 = f32[32,128]{1,0:T(8,128)S(1)} collective-permute-done((f32[32,128]{1,0:T(8,128)S(1)}, f32[32,128]{1,0:T(8,128)S(1)}, u32[]{:S(2)}, u32[]{:S(2)}) %collective-permute-start.9) | collective-permute-done | bytes 16416 | tf_op jit(solution)/shard_map/ppermute | solution.py:169
  27.0 0.0 collective-permute-start.11
  27.0 2.2 %collective-permute-done.10 = f32[32,128]{1,0:T(8,128)S(1)} collective-permute-done((f32[32,128]{1,0:T(8,128)S(1)}, f32[32,128]{1,0:T(8,128)S(1)}, u32[]{:S(2)}, u32[]{:S(2)}) %collective-permute-start.10) | collective-permute-done | bytes 16416 | tf_op jit(solution)/shard_map/ppermute | solution.py:169
  29.2 0.0 collective-permute-done.11
  29.3 1.6 %collective-permute-start.12 = (f32[32,128]{1,0:T(8,128)S(1)}, f32[32,128]{1,0:T(8,128)S(1)}, u32[]{:S(2)}, u32[]{:S(2)}) collective-permute-start(f32[32,128]{1,0:T(8,128)S(1)} %add_add_fusion.1), channel_id=1, source_target_pairs={{0,8},{1,17},{2,10},{3,19},{4,12},{5,21},{6,14},{7,23},{8,0},{9,25... | collective-permute-start | bytes 49160 | tf_op jit(solution)/shard_map/ppermute | solution.py:171
  30.9 2.5 %collective-permute-start.13 = (f32[32,128]{1,0:T(8,128)S(1)}, f32[32,128]{1,0:T(8,128)S(1)}, u32[]{:S(2)}, u32[]{:S(2)}) collective-permute-start(f32[32,128]{1,0:T(8,128)S(1)} %add_add_fusion.1), channel_id=1, source_target_pairs={{0,24},{8,16},{16,8},{24,0},{1,25},{9,17},{17,9},{25,1},{2,26},{10... | collective-permute-start | bytes 49160 | tf_op jit(solution)/shard_map/ppermute | solution.py:169
  33.4 0.0 collective-permute-done.12
  33.4 0.0 collective-permute-start.14
  33.4 3.1 %collective-permute-done.13 = f32[32,128]{1,0:T(8,128)S(1)} collective-permute-done((f32[32,128]{1,0:T(8,128)S(1)}, f32[32,128]{1,0:T(8,128)S(1)}, u32[]{:S(2)}, u32[]{:S(2)}) %collective-permute-start.13) | collective-permute-done | bytes 16416 | tf_op jit(solution)/shard_map/ppermute | solution.py:169
  36.4 0.0 collective-permute-done.14
  36.4 3.2 %solve.1 = f32[64,2048]{1,0:T(8,128)} custom-call(f32[32,128]{1,0:T(8,128)S(1)} %add_add_fusion.gram_ref, bf16[128,2048]{1,0:T(8,128)(2,1)S(1)} %get-tuple-element.30.applied_ref), custom_call_target="tpu_custom_call" | custom-call | tf_op jit(solution)/shard_map/solve/pallas_call | solution.py:253
  (4 shorter events, 0.0 us)
Async XLA Ops:
  0.0 0.7 %copy-start.4 = (s32[1,8,2]{1,2,0:T(2,128)S(1)}, s32[1,8,2]{1,2,0:T(2,128)}, u32[]{:S(2)}) copy-start(s32[1,8,2]{1,2,0:T(2,128)} %param.9) | copy-start | bytes 196
  0.0 5.1 %copy-start.3 = (s32[16]{0:T(128)S(1)}, s32[16]{0:T(128)}, u32[]{:S(2)}) copy-start(s32[16]{0:T(128)} %count_ref.3) | copy-start | bytes 196
  0.0 5.1 %copy-start = (bf16[16,16,128,128]{3,2,1,0:T(8,128)(2,1)S(1)}, bf16[16,16,128,128]{3,2,1,0:T(8,128)(2,1)}, u32[]{:S(2)}) copy-start(bf16[16,16,128,128]{3,2,1,0:T(8,128)(2,1)} %tiles_ref.3) | copy-start | bytes 25165828
  0.0 9.8 %collective-permute-start.3 = (bf16[64,2048]{1,0:T(8,128)(2,1)}, bf16[64,2048]{1,0:T(8,128)(2,1)S(1)}, u32[]{:S(2)}, u32[]{:S(2)}) collective-permute-start(bf16[64,2048]{1,0:T(8,128)(2,1)} %refs_4_.1), channel_id=1, source_target_pairs={{0,1},{1,0},{2,3},{3,2},{4,5},{5,4},{6,7},{7,6},{8,9},{9,8},{10,11... | collective-permute-start | bytes 786440 | tf_op jit(solution)/shard_map/ppermute | solution.py:169
  0.5 9.3 %copy-start.1 = (bf16[64,2048]{1,0:T(8,128)(2,1)S(1)}, bf16[64,2048]{1,0:T(8,128)(2,1)}, u32[]{:S(2)}) copy-start(bf16[64,2048]{1,0:T(8,128)(2,1)} %refs_4_.1) | copy-start | bytes 786436
  0.5 17.4 %copy-start.2 = (s32[16,16]{1,0:T(8,128)S(1)}, s32[16,16]{1,0:T(8,128)}, u32[]{:S(2)}) copy-start(s32[16,16]{1,0:T(8,128)} %slot_ref.1) | copy-start | bytes 3076
  0.7 6.6 %collective-permute-start.2 = (s32[1,2,8]{2,1,0:T(2,128)S(1)}, s32[1,2,8]{2,1,0:T(2,128)S(1)}, u32[]{:S(2)}, u32[]{:S(2)}) collective-permute-start(s32[1,2,8]{2,1,0:T(2,128)S(1)} %bitcast.1), channel_id=1, source_target_pairs={{0,6},{1,7},{2,4},{3,5},{4,2},{5,3},{6,0},{7,1},{8,14},{9,15},{10,... | collective-permute-start | bytes 200 | tf_op jit(solution)/shard_map/ppermute | solution.py:169
  4.6 3.6 %collective-permute-start.1 = (s32[1,2,8]{2,1,0:T(2,128)S(1)}, s32[1,2,8]{2,1,0:T(2,128)S(1)}, u32[]{:S(2)}, u32[]{:S(2)}) collective-permute-start(s32[1,2,8]{2,1,0:T(2,128)S(1)} %bitcast.2), channel_id=1, source_target_pairs={{0,4},{1,5},{2,6},{3,7},{4,0},{5,1},{6,2},{7,3},{8,12},{9,13},{10,... | collective-permute-start | bytes 200 | tf_op jit(solution)/shard_map/ppermute | solution.py:169
  5.1 3.6 %collective-permute-start = (s32[1,2,8]{2,1,0:T(2,128)S(1)}, s32[1,2,8]{2,1,0:T(2,128)S(1)}, u32[]{:S(2)}, u32[]{:S(2)}) collective-permute-start(s32[1,2,8]{2,1,0:T(2,128)S(1)} %bitcast.3), channel_id=1, source_target_pairs={{0,2},{1,3},{2,0},{3,1},{4,6},{5,7},{6,4},{7,5},{8,10},{9,11},{10,... | collective-permute-start | bytes 200 | tf_op jit(solution)/shard_map/ppermute | solution.py:169
  8.7 1.2 %collective-permute-start.4 = (f32[16,128]{1,0:T(8,128)S(1)}, f32[16,128]{1,0:T(8,128)S(1)}, u32[]{:S(2)}, u32[]{:S(2)}) collective-permute-start(f32[16,128]{1,0:T(8,128)S(1)} %degree.1.refs_6_.inv_ref), channel_id=1, source_target_pairs={{0,1},{1,0},{2,3},{3,2},{4,5},{5,4},{6,7},{7,6},{8,9},{9,8},{10,11... | collective-permute-start | bytes 24584 | tf_op jit(solution)/shard_map/ppermute | solution.py:169
  10.5 4.3 %collective-permute-start.5 = (bf16[2,2,64,128]{3,2,1,0:T(8,128)(2,1)S(1)}, bf16[2,2,64,128]{3,2,1,0:T(8,128)(2,1)S(1)}, u32[]{:S(2)}, u32[]{:S(2)}) collective-permute-start(bf16[2,2,64,128]{3,2,1,0:T(8,128)(2,1)S(1)} %get-tuple-element.26), channel_id=1, source_target_pairs={{0,2},{1,3},{2,0},{3,1},{4,6},{5,7},{6,4},{7,5},{8,10},{9,11},{10,... | collective-permute-start | bytes 196616 | tf_op jit(solution)/shard_map/ppermute | solution.py:169
  11.3 4.3 %collective-permute-start.6 = (bf16[2,2,64,128]{3,2,1,0:T(8,128)(2,1)S(1)}, bf16[2,2,64,128]{3,2,1,0:T(8,128)(2,1)S(1)}, u32[]{:S(2)}, u32[]{:S(2)}) collective-permute-start(bf16[2,2,64,128]{3,2,1,0:T(8,128)(2,1)S(1)} %get-tuple-element.27), channel_id=1, source_target_pairs={{0,4},{1,5},{2,6},{3,7},{4,0},{5,1},{6,2},{7,3},{8,12},{9,13},{10,... | collective-permute-start | bytes 196616 | tf_op jit(solution)/shard_map/ppermute | solution.py:169
  12.8 5.2 %collective-permute-start.7 = (bf16[2,2,64,128]{3,2,1,0:T(8,128)(2,1)S(1)}, bf16[2,2,64,128]{3,2,1,0:T(8,128)(2,1)S(1)}, u32[]{:S(2)}, u32[]{:S(2)}) collective-permute-start(bf16[2,2,64,128]{3,2,1,0:T(8,128)(2,1)S(1)} %get-tuple-element.28), channel_id=1, source_target_pairs={{0,6},{1,7},{2,4},{3,5},{4,2},{5,3},{6,0},{7,1},{8,14},{9,15},{10,... | collective-permute-start | bytes 196616 | tf_op jit(solution)/shard_map/ppermute | solution.py:169
  22.0 1.2 %collective-permute-start.8 = (f32[32,128]{1,0:T(8,128)S(1)}, f32[32,128]{1,0:T(8,128)S(1)}, u32[]{:S(2)}, u32[]{:S(2)}) collective-permute-start(f32[32,128]{1,0:T(8,128)S(1)} %get-tuple-element.29), channel_id=1, source_target_pairs={{0,1},{1,0},{2,3},{3,2},{4,5},{5,4},{6,7},{7,6},{8,9},{9,8},{10,11... | collective-permute-start | bytes 49160 | tf_op jit(solution)/shard_map/ppermute | solution.py:169
  23.3 3.7 %collective-permute-start.9 = (f32[32,128]{1,0:T(8,128)S(1)}, f32[32,128]{1,0:T(8,128)S(1)}, u32[]{:S(2)}, u32[]{:S(2)}) collective-permute-start(f32[32,128]{1,0:T(8,128)S(1)} %add.21), channel_id=1, source_target_pairs={{0,2},{1,5},{2,0},{3,7},{4,6},{5,1},{6,4},{7,3},{8,10},{9,13},{10,... | collective-permute-start | bytes 49160 | tf_op jit(solution)/shard_map/ppermute | solution.py:169
  24.6 4.6 %collective-permute-start.10 = (f32[32,128]{1,0:T(8,128)S(1)}, f32[32,128]{1,0:T(8,128)S(1)}, u32[]{:S(2)}, u32[]{:S(2)}) collective-permute-start(f32[32,128]{1,0:T(8,128)S(1)} %add.21), channel_id=1, source_target_pairs={{0,6},{1,7},{2,4},{3,5},{4,2},{5,3},{6,0},{7,1},{8,14},{9,15},{10,... | collective-permute-start | bytes 49160 | tf_op jit(solution)/shard_map/ppermute | solution.py:169
  27.0 2.2 %collective-permute-start.11 = (f32[32,128]{1,0:T(8,128)S(1)}, f32[32,128]{1,0:T(8,128)S(1)}, u32[]{:S(2)}, u32[]{:S(2)}) collective-permute-start(f32[32,128]{1,0:T(8,128)S(1)} %collective-permute-done.9), channel_id=1, source_target_pairs={{0,1},{1,0},{2,3},{3,2},{4,5},{5,4},{6,7},{7,6},{8,9},{9,8},{10,11... | collective-permute-start | bytes 49160 | tf_op jit(solution)/shard_map/ppermute | solution.py:169
  29.3 4.1 %collective-permute-start.12 = (f32[32,128]{1,0:T(8,128)S(1)}, f32[32,128]{1,0:T(8,128)S(1)}, u32[]{:S(2)}, u32[]{:S(2)}) collective-permute-start(f32[32,128]{1,0:T(8,128)S(1)} %add_add_fusion.1), channel_id=1, source_target_pairs={{0,8},{1,17},{2,10},{3,19},{4,12},{5,21},{6,14},{7,23},{8,0},{9,25... | collective-permute-start | bytes 49160 | tf_op jit(solution)/shard_map/ppermute | solution.py:171
  30.9 5.5 %collective-permute-start.13 = (f32[32,128]{1,0:T(8,128)S(1)}, f32[32,128]{1,0:T(8,128)S(1)}, u32[]{:S(2)}, u32[]{:S(2)}) collective-permute-start(f32[32,128]{1,0:T(8,128)S(1)} %add_add_fusion.1), channel_id=1, source_target_pairs={{0,24},{8,16},{16,8},{24,0},{1,25},{9,17},{17,9},{25,1},{2,26},{10... | collective-permute-start | bytes 49160 | tf_op jit(solution)/shard_map/ppermute | solution.py:169
  33.4 3.1 %collective-permute-start.14 = (f32[32,128]{1,0:T(8,128)S(1)}, f32[32,128]{1,0:T(8,128)S(1)}, u32[]{:S(2)}, u32[]{:S(2)}) collective-permute-start(f32[32,128]{1,0:T(8,128)S(1)} %collective-permute-done.12), channel_id=1, source_target_pairs={{0,1},{1,0},{2,3},{3,2},{4,5},{5,4},{6,7},{7,6},{8,9},{9,8},{10,11... | collective-permute-start | bytes 49160 | tf_op jit(solution)/shard_map/ppermute | solution.py:169

commit v4 on v3

--- a/solution.py
+++ b/solution.py
@@ -1,3 +1,5 @@
+import functools
+
 import jax
 import jax.numpy as jnp
 from jax import lax
@@ -5,7 +7,9 @@
 from jax.experimental.pallas import tpu as pltpu
 from jax.sharding import PartitionSpec as P
 
+GROUP = 4
 VMEM = pl.BlockSpec(memory_space=pltpu.VMEM)
+HBM = pl.BlockSpec(memory_space=pltpu.HBM)
 SMEM = pl.BlockSpec(memory_space=pltpu.SMEM)
 NT = (((1,), (1,)), ((), ()))
 F32 = jnp.float32
@@ -30,11 +34,11 @@
     ones = jnp.ones((8, 2 * cols), BF16)
     slot_of_lane = lax.broadcasted_iota(jnp.int32, (8, slots * cols), 1) // cols
     for b in range(blocks):
-        count = count_ref[b]
+        count = count_ref[:, b : b + 1]
         tiles = [tiles_ref[b, t] for t in range(slots)]
         if b % 2:
             total = sum(
-                tile.astype(F32) * jnp.where(t < count, 1.0, 0.0) for t, tile in enumerate(tiles)
+                tile.astype(F32) * (t < count).astype(F32) for t, tile in enumerate(tiles)
             )
             live, row = ones, split(total)
         else:
@@ -46,49 +50,77 @@
         inv_ref[b : b + 1] = lax.rsqrt(degree[:1])
 
 
-def select_kernel(*refs):
-    chips = (len(refs) - 4) // 2
-    list_refs, (sub_ref, sib_sub_ref, inv_ref, sib_inv_ref), send_refs = (
-        refs[:chips],
-        refs[chips : chips + 4],
-        refs[chips + 4 :],
-    )
-    cap, cols = list_refs[0].shape[1], inv_ref.shape[1]
+def join_kernel(*refs):
+    *list_refs, out_ref, sems = refs
+    copies = [
+        pltpu.make_async_copy(ref.at[0], out_ref.at[i], sems.at[i]) for i, ref in enumerate(list_refs)
+    ]
+    for copy in copies:
+        copy.start()
+    for copy in copies:
+        copy.wait()
+
+
+def select_kernel(masks, lists_ref, sub_ref, sib_sub_ref, inv_ref, sib_inv_ref, *send_refs):
+    cap, cols = lists_ref.shape[1], inv_ref.shape[1]
     me = lax.axis_index("dev")
     sources = ((me, sub_ref, inv_ref), (me ^ 1, sib_sub_ref, sib_inv_ref))
-    for wanted, send in zip(list_refs, send_refs, strict=True):
-        for core, (source, columns, inv) in enumerate(sources):
-            for j in range(cap):
-                block = wanted[0, j, source]
-                lanes = pl.ds(pl.multiple_of(block * cols, cols), cols)
-                scaled = columns[:, lanes].astype(F32) * inv[pl.ds(block, 1), :]
-                send[core, j] = scaled.astype(BF16)
-
-
-def product_kernel(count_ref, slot_ref, inv_ref, tiles_ref, *refs):
+    ids = [
+        [lists_ref[mask // 2, j, source] for source, _, _ in sources for j in range(cap)]
+        for mask in masks
+    ]
+    for blocks, send in zip(ids, send_refs, strict=True):
+        scaled = []
+        for i, block in enumerate(blocks):
+            _, columns, inv = sources[i // cap]
+            lanes = pl.ds(pl.multiple_of(block * cols, cols), cols)
+            scaled.append(columns[:, lanes].astype(F32) * inv[pl.ds(block, 1), :])
+        for i, block in enumerate(scaled):
+            send[i // cap, i % cap] = block.astype(BF16)
+
+
+def plan_kernel(count_hbm, slot_hbm, count_ref, slot_ref, sems):
+    copies = [
+        pltpu.make_async_copy(count_hbm, count_ref, sems.at[0]),
+        pltpu.make_async_copy(slot_hbm, slot_ref, sems.at[1]),
+    ]
+    for copy in copies:
+        copy.start()
+    for copy in copies:
+        copy.wait()
+
+
+def product_kernel(masks, count_ref, slot_ref, inv_ref, tiles_ref, *refs):
     *part_refs, applied_ref, gram_ref, table = refs
     blocks, slots, rows, cols = tiles_ref.shape
     _, cap, k_dim, _ = part_refs[0].shape
     me = lax.axis_index("dev")
     dead = table.shape[0] - 1
     table[dead] = jnp.zeros((k_dim, cols), BF16)
-    for i, part in enumerate(part_refs):
+    for mask, part in zip(masks, part_refs, strict=True):
         for core in range(2):
             for j in range(cap):
-                table[((2 * i + core) ^ me) * cap + j] = part[core, j]
-    for b in range(blocks):
-        count = count_ref[b]
-        parts = [table[jnp.where(t < count, slot_ref[b, t], dead)] for t in range(slots)]
+                table[((mask + core) ^ me) * cap + j] = part[core, j]
+    for first in range(0, blocks, GROUP):
+        group = range(first, first + GROUP)
+        parts, tiles = [], []
+        for b in group:
+            count = count_ref[b]
+            entries = [jnp.where(t < count, slot_ref[b, t], dead) for t in range(slots)]
+            parts.append(jnp.concatenate([table[entry] for entry in entries], axis=1))
+            tiles.append(jnp.concatenate([tiles_ref[b, t] for t in range(slots)], axis=1))
         total = lax.dot_general(
-            jnp.concatenate(parts, axis=1),
-            jnp.concatenate([tiles_ref[b, t] for t in range(slots)], axis=1),
+            jnp.concatenate(parts, axis=0),
+            jnp.concatenate(tiles, axis=0),
             NT,
             preferred_element_type=F32,
         )
-        lanes = slice(b * rows, (b + 1) * rows)
-        high, low = split(total * inv_ref[b : b + 1])
-        applied_ref[:k_dim, lanes] = high
-        applied_ref[k_dim:, lanes] = low
+        for i, b in enumerate(group):
+            lanes = slice(b * rows, (b + 1) * rows)
+            own = total[i * k_dim : (i + 1) * k_dim, i * rows : (i + 1) * rows]
+            high, low = split(own * inv_ref[b : b + 1])
+            applied_ref[:k_dim, lanes] = high
+            applied_ref[k_dim:, lanes] = low
     both = applied_ref[...]
     wide = lax.dot_general(both, both, NT, preferred_element_type=F32)
     wide = wide[:k_dim] + wide[k_dim:]
@@ -205,35 +237,56 @@
         name="start",
     )()
     first, lists = lax.optimization_barrier((first, jnp.transpose(fetch_list, (0, 2, 1))))
+    masks = [0] + [2 * i for i in reversed(range(1, chips))]
     lists = [lists] + [swap(lists, "dev", 2 * i) for i in range(1, chips)]
     sib_columns = swap(subspace, "dev", 1)
 
     inv_root = pl.pallas_call(
         degree_kernel,
         out_shape=jax.ShapeDtypeStruct((blocks, rows), F32),
-        in_specs=[VMEM, SMEM, VMEM],
+        in_specs=[VMEM] * 3,
         out_specs=VMEM,
         compiler_params=limit(4),
         cost_estimate=pl.CostEstimate(
             flops=16 * tiles.size, bytes_accessed=2 * tiles.size, transcendentals=0
         ),
         name="degree",
-    )(first, tile_count, tiles)
-    inv_root, *lists = lax.optimization_barrier((inv_root, *lists))
+    )(first, tile_count.reshape(1, blocks), tiles)
     sib_inv_root = swap(inv_root, "dev", 1)
-
+    lists = pl.pallas_call(
+        join_kernel,
+        out_shape=pltpu.SMEM((chips, cap, peers), jnp.int32),
+        in_specs=[VMEM] * chips,
+        out_specs=SMEM,
+        scratch_shapes=[pltpu.SemaphoreType.DMA((chips,))],
+        compiler_params=limit(1),
+        cost_estimate=pl.CostEstimate(flops=2 * 10**9, bytes_accessed=0, transcendentals=0),
+        name="join",
+    )(*lists)
     sends = pl.pallas_call(
-        select_kernel,
+        functools.partial(select_kernel, masks),
         out_shape=[jax.ShapeDtypeStruct((2, cap, k_dim, cols), BF16)] * chips,
-        in_specs=[SMEM] * chips + [VMEM] * 4,
+        in_specs=[SMEM] + [VMEM] * 4,
         out_specs=[VMEM] * chips,
         compiler_params=limit(2),
         name="select",
-    )(*lists, subspace, sib_columns, inv_root, sib_inv_root)
-    parts = [sends[0]] + [swap(sends[i], "dev", 2 * i) for i in range(1, chips)]
+    )(pltpu.with_memory_space_constraint(lists, pltpu.SMEM), subspace, sib_columns, inv_root, sib_inv_root)
+    parts = [swap(x, "dev", mask) if mask else x for x, mask in zip(sends, masks, strict=True)]
+
+    plan = pl.pallas_call(
+        plan_kernel,
+        out_shape=[pltpu.SMEM(x.shape, x.dtype) for x in (tile_count, tile_slot)],
+        in_specs=[HBM] * 2,
+        out_specs=[SMEM] * 2,
+        scratch_shapes=[pltpu.SemaphoreType.DMA((2,))],
+        compiler_params=limit(1),
+        cost_estimate=pl.CostEstimate(flops=2 * 10**9, bytes_accessed=0, transcendentals=0),
+        name="plan",
+    )(*(pltpu.with_memory_space_constraint(x, pltpu.HBM) for x in (tile_count, tile_slot)))
+    plan = [pltpu.with_memory_space_constraint(x, pltpu.SMEM) for x in plan]
 
     applied, gram = pl.pallas_call(
-        product_kernel,
+        functools.partial(product_kernel, masks),
         out_shape=(
             jax.ShapeDtypeStruct((2 * k_dim, row_count), BF16),
             jax.ShapeDtypeStruct((k_dim // 2, 2 * k_dim), F32),
@@ -246,7 +299,7 @@
             flops=2 * tiles.size * k_dim, bytes_accessed=2 * tiles.size, transcendentals=0
         ),
         name="product",
-    )(tile_count, tile_slot, inv_root, tiles, *parts)
+    )(*plan, inv_root, tiles, *parts)
 
     gram = sum_all(gram)
 

time: 39.8 us -> 36.5 us (0.917)
  waiting for transfers between devices: 14.7 us -> 11.2 us
  starting transfers between devices: 14.6 us -> 15.7 us
  Pallas kernels: 10.1 us -> 9.15 us
    ppermute x14, waiting for transfers between devices: 14.7 us -> 11.2 us  [swap(): lax.ppermute(x, axis, [(i, i ^ (odd if i % 2 else mask)) for i in range(s...]
    ppermute x14, starting transfers between devices: 13 us -> 14 us  [swap(): lax.ppermute(x, axis, [(i, i ^ (odd if i % 2 else mask)) for i in range(s...]
    pallas_call x1, Pallas kernels: 2.11 us -> 1.61 us  [body(): pl.pallas_call(degree_kernel, out_shape=jax.ShapeDtypeStruct((blocks, row...]
    pallas_call x2 -> x4, Pallas kernels: 4.78 us -> 4.37 us  [the longest x1 2.83 us: body(): pl.pallas_call(functools.partial(product_kernel, masks), out_shape=(jax.S...]
  transfers between devices with their start and end apart: 15 -> 15, of which waited for: 10 -> 9; matrix products, arithmetic and copies ran while one was open for 0% -> 0% of each run, Pallas kernels for 5% -> 8%
where the time goes in v4:
time: 36.5 us; the launch traced here: 36.3 us
  starting transfers between devices  15.7 us (43%)
  waiting for transfers between devices  11.2 us (31%)
  Pallas kernels  9.15 us (25%)
    ppermute x14, starting transfers between devices, swap(): lax.ppermute(x, axis, [(i, i ^ (odd if i % 2 else mask)) for i in range(s...  14 us
    ppermute x14, waiting for transfers between devices, swap(): lax.ppermute(x, axis, [(i, i ^ (odd if i % 2 else mask)) for i in range(s...  11.2 us
    pallas_call x1, Pallas kernels, body(): pl.pallas_call(solve_kernel, out_shape=jax.ShapeDtypeStruct((k_dim, row_c...  3.17 us
    pallas_call x1, Pallas kernels, body(): pl.pallas_call(functools.partial(product_kernel, masks), out_shape=(jax.S...  2.83 us
    ppermute x1, starting transfers between devices, swap(): return lax.ppermute(x, (axis, 'dev'), pairs)  1.64 us
    pallas_call x1, Pallas kernels, body(): pl.pallas_call(degree_kernel, out_shape=jax.ShapeDtypeStruct((blocks, row...  1.61 us
    pallas_call x1, Pallas kernels, body(): pl.pallas_call(plan_kernel, out_shape=[pltpu.SMEM(x.shape, x.dtype) for x...  0.81 us
  transfers between devices with their start and end apart: 15, of which 9 were waited for; matrix products, arithmetic and copies ran while one was open for 0% of the time, Pallas kernels for 8%

profile of v4, /device:TPU:0, one launch (start us, length us, event | category | flops | bytes accessed | tf_op | source)
XLA Modules:
  0.0 36.3 jit_solution(11937451420427412435)
XLA Ops:
  0.0 0.0 copy-start.3
  0.0 0.0 copy-start
  0.0 0.0 copy-start.2
  0.0 0.5 %collective-permute-start.3 = (bf16[64,2048]{1,0:T(8,128)(2,1)}, bf16[64,2048]{1,0:T(8,128)(2,1)S(1)}, u32[]{:S(2)}, u32[]{:S(2)}) collective-permute-start(bf16[64,2048]{1,0:T(8,128)(2,1)} %sub_ref.1), channel_id=1, source_target_pairs={{0,1},{1,0},{2,3},{3,2},{4,5},{5,4},{6,7},{7,6},{8,9},{9,8},{10,11... | collective-permute-start | bytes 786440 | tf_op jit(solution)/shard_map/ppermute | solution.py:201
  0.5 0.0 copy-start.1
  0.5 0.1 copy-done.3
  0.7 3.9 %collective-permute-start.2 = (s32[1,2,8]{2,1,0:T(2,128)S(1)}, s32[1,2,8]{2,1,0:T(2,128)S(1)}, u32[]{:S(2)}, u32[]{:S(2)}) collective-permute-start(s32[1,2,8]{2,1,0:T(2,128)S(1)} %bitcast.3), channel_id=1, source_target_pairs={{0,6},{1,7},{2,4},{3,5},{4,2},{5,3},{6,0},{7,1},{8,14},{9,15},{10,... | collective-permute-start | bytes 200 | tf_op jit(solution)/shard_map/ppermute | solution.py:201
  4.6 0.5 %collective-permute-start.1 = (s32[1,2,8]{2,1,0:T(2,128)S(1)}, s32[1,2,8]{2,1,0:T(2,128)S(1)}, u32[]{:S(2)}, u32[]{:S(2)}) collective-permute-start(s32[1,2,8]{2,1,0:T(2,128)S(1)} %bitcast.4), channel_id=1, source_target_pairs={{0,4},{1,5},{2,6},{3,7},{4,0},{5,1},{6,2},{7,3},{8,12},{9,13},{10,... | collective-permute-start | bytes 200 | tf_op jit(solution)/shard_map/ppermute | solution.py:201
  5.1 0.1 collective-permute-start
  5.1 0.0 copy-done
  5.1 0.0 copy-done.2
  5.1 1.6 %degree.1.inv_ref = f32[16,128]{1,0:T(8,128)S(1)} custom-call(f32[8,128]{1,0:T(8,128)S(1)} %start.1.first_ref, s32[1,16]{1,0:T(1,128)S(1)} %bitcast.2, bf16[16,16,128,128]{3,2,1,0:T(8,128)(2,1)S(1)} %copy-done), custom_call_target="tpu_custom_call" | custom-call | flops 67108864 | bytes 8388608 | tf_op jit(solution)/shard_map/degree/pallas_call | solution.py:244
  6.8 0.0 collective-permute-start.4
  6.8 0.0 collective-permute-done.2.refs_3_
  6.8 1.3 %collective-permute-done.1.refs_2_ = s32[1,2,8]{2,1,0:T(2,128)S(1)} collective-permute-done((s32[1,2,8]{2,1,0:T(2,128)S(1)}, s32[1,2,8]{2,1,0:T(2,128)S(1)}, u32[]{:S(2)}, u32[]{:S(2)}) %collective-permute-start.1) | collective-permute-done | bytes 96 | tf_op jit(solution)/shard_map/ppermute | solution.py:201
  8.1 0.5 %collective-permute-done.refs_1_ = s32[1,2,8]{2,1,0:T(2,128)S(1)} collective-permute-done((s32[1,2,8]{2,1,0:T(2,128)S(1)}, s32[1,2,8]{2,1,0:T(2,128)S(1)}, u32[]{:S(2)}, u32[]{:S(2)}) %collective-permute-start) | collective-permute-done | bytes 96 | tf_op jit(solution)/shard_map/ppermute | solution.py:201
  8.7 0.6 %join.1.lists_ref = s32[4,2,8]{2,1,0:T(2,128)S(4)} custom-call(s32[1,2,8]{2,1,0:T(2,128)S(1)} %bitcast.6, s32[1,2,8]{2,1,0:T(2,128)S(1)} %collective-permute-done.refs_1_, s32[1,2,8]{2,1,0:T(2,128)S(1)} %collective-permute-done.1.refs_2_, s32[1,2,8]{2,1,0:T(2,128)S(1)} %collective-permute-done.2.refs_3_), custom_call_target="tpu_custom_call" | custom-call | flops 2000000000 | tf_op jit(solution)/shard_map/join/pallas_call | solution.py:256
  9.3 0.0 collective-permute-done.4.sib_inv_ref
  9.3 0.0 collective-permute-done.3.sib_sub_ref
  9.3 0.0 copy-done.1
  9.3 0.1 select.1
  9.4 1.6 %collective-permute-start.5 = (bf16[2,2,64,128]{3,2,1,0:T(8,128)(2,1)S(1)}, bf16[2,2,64,128]{3,2,1,0:T(8,128)(2,1)S(1)}, u32[]{:S(2)}, u32[]{:S(2)}) collective-permute-start(bf16[2,2,64,128]{3,2,1,0:T(8,128)(2,1)S(1)} %get-tuple-element.20), channel_id=1, source_target_pairs={{0,6},{1,7},{2,4},{3,5},{4,2},{5,3},{6,0},{7,1},{8,14},{9,15},{10,... | collective-permute-start | bytes 196616 | tf_op jit(solution)/shard_map/ppermute | solution.py:201
  11.0 0.5 %collective-permute-start.6 = (bf16[2,2,64,128]{3,2,1,0:T(8,128)(2,1)S(1)}, bf16[2,2,64,128]{3,2,1,0:T(8,128)(2,1)S(1)}, u32[]{:S(2)}, u32[]{:S(2)}) collective-permute-start(bf16[2,2,64,128]{3,2,1,0:T(8,128)(2,1)S(1)} %get-tuple-element.21), channel_id=1, source_target_pairs={{0,4},{1,5},{2,6},{3,7},{4,0},{5,1},{6,2},{7,3},{8,12},{9,13},{10,... | collective-permute-start | bytes 196616 | tf_op jit(solution)/shard_map/ppermute | solution.py:201
  11.6 1.4 %collective-permute-start.7 = (bf16[2,2,64,128]{3,2,1,0:T(8,128)(2,1)S(1)}, bf16[2,2,64,128]{3,2,1,0:T(8,128)(2,1)S(1)}, u32[]{:S(2)}, u32[]{:S(2)}) collective-permute-start(bf16[2,2,64,128]{3,2,1,0:T(8,128)(2,1)S(1)} %get-tuple-element.22), channel_id=1, source_target_pairs={{0,2},{1,3},{2,0},{3,1},{4,6},{5,7},{6,4},{7,5},{8,10},{9,11},{10,... | collective-permute-start | bytes 196616 | tf_op jit(solution)/shard_map/ppermute | solution.py:201
  13.0 0.8 %plan.1 = (s32[16]{0:T(128)S(4)}, s32[16,16]{1,0:T(8,128)S(4)}) custom-call(s32[16]{0:T(128)} %count_hbm.1, s32[16,16]{1,0:T(8,128)} %slot_hbm.1), custom_call_target="tpu_custom_call" | custom-call | flops 2000000000 | tf_op jit(solution)/shard_map/plan/pallas_call | solution.py:276
  13.8 1.0 %collective-permute-done.5.refs_1_ = bf16[2,2,64,128]{3,2,1,0:T(8,128)(2,1)S(1)} collective-permute-done((bf16[2,2,64,128]{3,2,1,0:T(8,128)(2,1)S(1)}, bf16[2,2,64,128]{3,2,1,0:T(8,128)(2,1)S(1)}, u32[]{:S(2)}, u32[]{:S(2)}) %collective-permute-start.5) | collective-permute-done | bytes 65568 | tf_op jit(solution)/shard_map/ppermute | solution.py:201
  14.8 0.9 %collective-permute-done.6.refs_2_ = bf16[2,2,64,128]{3,2,1,0:T(8,128)(2,1)S(1)} collective-permute-done((bf16[2,2,64,128]{3,2,1,0:T(8,128)(2,1)S(1)}, bf16[2,2,64,128]{3,2,1,0:T(8,128)(2,1)S(1)}, u32[]{:S(2)}, u32[]{:S(2)}) %collective-permute-start.6) | collective-permute-done | bytes 65568 | tf_op jit(solution)/shard_map/ppermute | solution.py:201
  15.6 0.2 collective-permute-done.7.refs_3_
  15.9 2.8 %product.1 = (bf16[128,2048]{1,0:T(8,128)(2,1)S(1)}, f32[32,128]{1,0:T(8,128)S(1)}) custom-call(s32[16]{0:T(128)S(4)} %get-tuple-element.15.count_ref, s32[16,16]{1,0:T(8,128)S(4)} %get-tuple-element.16.slot_ref, f32[16,128]{1,0:T(8,128)S(1)} %degree.1.inv_ref, bf16[16,16,128,128]{3,2,1,0:T(8,128)(2,1)S(1)} %copy-done, ...), custom_call_target="tpu_custom_call" | custom-call | flops 536870912 | bytes 8388608 | tf_op jit(solution)/shard_map/product/pallas_call | solution.py:288
  18.7 0.0 collective-permute-start.8
  18.7 1.2 %collective-permute-done.8 = f32[32,128]{1,0:T(8,128)S(1)} collective-permute-done((f32[32,128]{1,0:T(8,128)S(1)}, f32[32,128]{1,0:T(8,128)S(1)}, u32[]{:S(2)}, u32[]{:S(2)}) %collective-permute-start.8) | collective-permute-done | bytes 16416 | tf_op jit(solution)/shard_map/ppermute | solution.py:201
  19.9 1.4 %collective-permute-start.9 = (f32[32,128]{1,0:T(8,128)S(1)}, f32[32,128]{1,0:T(8,128)S(1)}, u32[]{:S(2)}, u32[]{:S(2)}) collective-permute-start(f32[32,128]{1,0:T(8,128)S(1)} %add.21), channel_id=1, source_target_pairs={{0,2},{1,5},{2,0},{3,7},{4,6},{5,1},{6,4},{7,3},{8,10},{9,13},{10,... | collective-permute-start | bytes 49160 | tf_op jit(solution)/shard_map/ppermute | solution.py:201
  21.3 1.6 %collective-permute-start.10 = (f32[32,128]{1,0:T(8,128)S(1)}, f32[32,128]{1,0:T(8,128)S(1)}, u32[]{:S(2)}, u32[]{:S(2)}) collective-permute-start(f32[32,128]{1,0:T(8,128)S(1)} %add.21), channel_id=1, source_target_pairs={{0,6},{1,7},{2,4},{3,5},{4,2},{5,3},{6,0},{7,1},{8,14},{9,15},{10,... | collective-permute-start | bytes 49160 | tf_op jit(solution)/shard_map/ppermute | solution.py:201
  22.9 0.8 %collective-permute-done.9 = f32[32,128]{1,0:T(8,128)S(1)} collective-permute-done((f32[32,128]{1,0:T(8,128)S(1)}, f32[32,128]{1,0:T(8,128)S(1)}, u32[]{:S(2)}, u32[]{:S(2)}) %collective-permute-start.9) | collective-permute-done | bytes 16416 | tf_op jit(solution)/shard_map/ppermute | solution.py:201
  23.6 0.0 collective-permute-start.11
  23.7 2.3 %collective-permute-done.10 = f32[32,128]{1,0:T(8,128)S(1)} collective-permute-done((f32[32,128]{1,0:T(8,128)S(1)}, f32[32,128]{1,0:T(8,128)S(1)}, u32[]{:S(2)}, u32[]{:S(2)}) %collective-permute-start.10) | collective-permute-done | bytes 16416 | tf_op jit(solution)/shard_map/ppermute | solution.py:201
  25.9 0.0 collective-permute-done.11
  25.9 1.6 %collective-permute-start.12 = (f32[32,128]{1,0:T(8,128)S(1)}, f32[32,128]{1,0:T(8,128)S(1)}, u32[]{:S(2)}, u32[]{:S(2)}) collective-permute-start(f32[32,128]{1,0:T(8,128)S(1)} %add_add_fusion.1), channel_id=1, source_target_pairs={{0,8},{1,17},{2,10},{3,19},{4,12},{5,21},{6,14},{7,23},{8,0},{9,25... | collective-permute-start | bytes 49160 | tf_op jit(solution)/shard_map/ppermute | solution.py:203
  27.6 2.5 %collective-permute-start.13 = (f32[32,128]{1,0:T(8,128)S(1)}, f32[32,128]{1,0:T(8,128)S(1)}, u32[]{:S(2)}, u32[]{:S(2)}) collective-permute-start(f32[32,128]{1,0:T(8,128)S(1)} %add_add_fusion.1), channel_id=1, source_target_pairs={{0,24},{8,16},{16,8},{24,0},{1,25},{9,17},{17,9},{25,1},{2,26},{10... | collective-permute-start | bytes 49160 | tf_op jit(solution)/shard_map/ppermute | solution.py:201
  30.1 0.0 collective-permute-done.12
  30.1 0.0 collective-permute-start.14
  30.1 3.1 %collective-permute-done.13 = f32[32,128]{1,0:T(8,128)S(1)} collective-permute-done((f32[32,128]{1,0:T(8,128)S(1)}, f32[32,128]{1,0:T(8,128)S(1)}, u32[]{:S(2)}, u32[]{:S(2)}) %collective-permute-start.13) | collective-permute-done | bytes 16416 | tf_op jit(solution)/shard_map/ppermute | solution.py:201
  33.1 0.0 collective-permute-done.14
  33.1 3.2 %solve.1 = f32[64,2048]{1,0:T(8,128)} custom-call(f32[32,128]{1,0:T(8,128)S(1)} %add_add_fusion.gram_ref, bf16[128,2048]{1,0:T(8,128)(2,1)S(1)} %get-tuple-element.24.applied_ref), custom_call_target="tpu_custom_call" | custom-call | tf_op jit(solution)/shard_map/solve/pallas_call | solution.py:306
  (4 shorter events, 0.0 us)
Async XLA Ops:
  0.0 0.7 %copy-start.3 = (s32[1,8,2]{1,2,0:T(2,128)S(1)}, s32[1,8,2]{1,2,0:T(2,128)}, u32[]{:S(2)}) copy-start(s32[1,8,2]{1,2,0:T(2,128)} %param.9) | copy-start | bytes 196
  0.0 5.1 %copy-start = (bf16[16,16,128,128]{3,2,1,0:T(8,128)(2,1)S(1)}, bf16[16,16,128,128]{3,2,1,0:T(8,128)(2,1)}, u32[]{:S(2)}) copy-start(bf16[16,16,128,128]{3,2,1,0:T(8,128)(2,1)} %tiles_ref.3) | copy-start | bytes 25165828
  0.0 5.1 %copy-start.2 = (s32[16]{0:T(128)S(1)}, s32[16]{0:T(128)}, u32[]{:S(2)}) copy-start(s32[16]{0:T(128)} %count_hbm.1) | copy-start | bytes 196
  0.0 9.3 %collective-permute-start.3 = (bf16[64,2048]{1,0:T(8,128)(2,1)}, bf16[64,2048]{1,0:T(8,128)(2,1)S(1)}, u32[]{:S(2)}, u32[]{:S(2)}) collective-permute-start(bf16[64,2048]{1,0:T(8,128)(2,1)} %sub_ref.1), channel_id=1, source_target_pairs={{0,1},{1,0},{2,3},{3,2},{4,5},{5,4},{6,7},{7,6},{8,9},{9,8},{10,11... | collective-permute-start | bytes 786440 | tf_op jit(solution)/shard_map/ppermute | solution.py:201
  0.5 8.8 %copy-start.1 = (bf16[64,2048]{1,0:T(8,128)(2,1)S(1)}, bf16[64,2048]{1,0:T(8,128)(2,1)}, u32[]{:S(2)}) copy-start(bf16[64,2048]{1,0:T(8,128)(2,1)} %sub_ref.1) | copy-start | bytes 786436
  0.7 6.1 %collective-permute-start.2 = (s32[1,2,8]{2,1,0:T(2,128)S(1)}, s32[1,2,8]{2,1,0:T(2,128)S(1)}, u32[]{:S(2)}, u32[]{:S(2)}) collective-permute-start(s32[1,2,8]{2,1,0:T(2,128)S(1)} %bitcast.3), channel_id=1, source_target_pairs={{0,6},{1,7},{2,4},{3,5},{4,2},{5,3},{6,0},{7,1},{8,14},{9,15},{10,... | collective-permute-start | bytes 200 | tf_op jit(solution)/shard_map/ppermute | solution.py:201
  4.6 3.6 %collective-permute-start.1 = (s32[1,2,8]{2,1,0:T(2,128)S(1)}, s32[1,2,8]{2,1,0:T(2,128)S(1)}, u32[]{:S(2)}, u32[]{:S(2)}) collective-permute-start(s32[1,2,8]{2,1,0:T(2,128)S(1)} %bitcast.4), channel_id=1, source_target_pairs={{0,4},{1,5},{2,6},{3,7},{4,0},{5,1},{6,2},{7,3},{8,12},{9,13},{10,... | collective-permute-start | bytes 200 | tf_op jit(solution)/shard_map/ppermute | solution.py:201
  5.1 3.6 %collective-permute-start = (s32[1,2,8]{2,1,0:T(2,128)S(1)}, s32[1,2,8]{2,1,0:T(2,128)S(1)}, u32[]{:S(2)}, u32[]{:S(2)}) collective-permute-start(s32[1,2,8]{2,1,0:T(2,128)S(1)} %bitcast.5), channel_id=1, source_target_pairs={{0,2},{1,3},{2,0},{3,1},{4,6},{5,7},{6,4},{7,5},{8,10},{9,11},{10,... | collective-permute-start | bytes 200 | tf_op jit(solution)/shard_map/ppermute | solution.py:201
  6.8 2.5 %collective-permute-start.4 = (f32[16,128]{1,0:T(8,128)S(1)}, f32[16,128]{1,0:T(8,128)S(1)}, u32[]{:S(2)}, u32[]{:S(2)}) collective-permute-start(f32[16,128]{1,0:T(8,128)S(1)} %degree.1.inv_ref), channel_id=1, source_target_pairs={{0,1},{1,0},{2,3},{3,2},{4,5},{5,4},{6,7},{7,6},{8,9},{9,8},{10,11... | collective-permute-start | bytes 24584 | tf_op jit(solution)/shard_map/ppermute | solution.py:201
  9.4 5.3 %collective-permute-start.5 = (bf16[2,2,64,128]{3,2,1,0:T(8,128)(2,1)S(1)}, bf16[2,2,64,128]{3,2,1,0:T(8,128)(2,1)S(1)}, u32[]{:S(2)}, u32[]{:S(2)}) collective-permute-start(bf16[2,2,64,128]{3,2,1,0:T(8,128)(2,1)S(1)} %get-tuple-element.20), channel_id=1, source_target_pairs={{0,6},{1,7},{2,4},{3,5},{4,2},{5,3},{6,0},{7,1},{8,14},{9,15},{10,... | collective-permute-start | bytes 196616 | tf_op jit(solution)/shard_map/ppermute | solution.py:201
  11.0 4.6 %collective-permute-start.6 = (bf16[2,2,64,128]{3,2,1,0:T(8,128)(2,1)S(1)}, bf16[2,2,64,128]{3,2,1,0:T(8,128)(2,1)S(1)}, u32[]{:S(2)}, u32[]{:S(2)}) collective-permute-start(bf16[2,2,64,128]{3,2,1,0:T(8,128)(2,1)S(1)} %get-tuple-element.21), channel_id=1, source_target_pairs={{0,4},{1,5},{2,6},{3,7},{4,0},{5,1},{6,2},{7,3},{8,12},{9,13},{10,... | collective-permute-start | bytes 196616 | tf_op jit(solution)/shard_map/ppermute | solution.py:201
  11.6 4.3 %collective-permute-start.7 = (bf16[2,2,64,128]{3,2,1,0:T(8,128)(2,1)S(1)}, bf16[2,2,64,128]{3,2,1,0:T(8,128)(2,1)S(1)}, u32[]{:S(2)}, u32[]{:S(2)}) collective-permute-start(bf16[2,2,64,128]{3,2,1,0:T(8,128)(2,1)S(1)} %get-tuple-element.22), channel_id=1, source_target_pairs={{0,2},{1,3},{2,0},{3,1},{4,6},{5,7},{6,4},{7,5},{8,10},{9,11},{10,... | collective-permute-start | bytes 196616 | tf_op jit(solution)/shard_map/ppermute | solution.py:201
  18.7 1.2 %collective-permute-start.8 = (f32[32,128]{1,0:T(8,128)S(1)}, f32[32,128]{1,0:T(8,128)S(1)}, u32[]{:S(2)}, u32[]{:S(2)}) collective-permute-start(f32[32,128]{1,0:T(8,128)S(1)} %get-tuple-element.23), channel_id=1, source_target_pairs={{0,1},{1,0},{2,3},{3,2},{4,5},{5,4},{6,7},{7,6},{8,9},{9,8},{10,11... | collective-permute-start | bytes 49160 | tf_op jit(solution)/shard_map/ppermute | solution.py:201
  19.9 3.7 %collective-permute-start.9 = (f32[32,128]{1,0:T(8,128)S(1)}, f32[32,128]{1,0:T(8,128)S(1)}, u32[]{:S(2)}, u32[]{:S(2)}) collective-permute-start(f32[32,128]{1,0:T(8,128)S(1)} %add.21), channel_id=1, source_target_pairs={{0,2},{1,5},{2,0},{3,7},{4,6},{5,1},{6,4},{7,3},{8,10},{9,13},{10,... | collective-permute-start | bytes 49160 | tf_op jit(solution)/shard_map/ppermute | solution.py:201
  21.3 4.6 %collective-permute-start.10 = (f32[32,128]{1,0:T(8,128)S(1)}, f32[32,128]{1,0:T(8,128)S(1)}, u32[]{:S(2)}, u32[]{:S(2)}) collective-permute-start(f32[32,128]{1,0:T(8,128)S(1)} %add.21), channel_id=1, source_target_pairs={{0,6},{1,7},{2,4},{3,5},{4,2},{5,3},{6,0},{7,1},{8,14},{9,15},{10,... | collective-permute-start | bytes 49160 | tf_op jit(solution)/shard_map/ppermute | solution.py:201
  23.6 2.3 %collective-permute-start.11 = (f32[32,128]{1,0:T(8,128)S(1)}, f32[32,128]{1,0:T(8,128)S(1)}, u32[]{:S(2)}, u32[]{:S(2)}) collective-permute-start(f32[32,128]{1,0:T(8,128)S(1)} %collective-permute-done.9), channel_id=1, source_target_pairs={{0,1},{1,0},{2,3},{3,2},{4,5},{5,4},{6,7},{7,6},{8,9},{9,8},{10,11... | collective-permute-start | bytes 49160 | tf_op jit(solution)/shard_map/ppermute | solution.py:201
  25.9 4.1 %collective-permute-start.12 = (f32[32,128]{1,0:T(8,128)S(1)}, f32[32,128]{1,0:T(8,128)S(1)}, u32[]{:S(2)}, u32[]{:S(2)}) collective-permute-start(f32[32,128]{1,0:T(8,128)S(1)} %add_add_fusion.1), channel_id=1, source_target_pairs={{0,8},{1,17},{2,10},{3,19},{4,12},{5,21},{6,14},{7,23},{8,0},{9,25... | collective-permute-start | bytes 49160 | tf_op jit(solution)/shard_map/ppermute | solution.py:203
  27.6 5.5 %collective-permute-start.13 = (f32[32,128]{1,0:T(8,128)S(1)}, f32[32,128]{1,0:T(8,128)S(1)}, u32[]{:S(2)}, u32[]{:S(2)}) collective-permute-start(f32[32,128]{1,0:T(8,128)S(1)} %add_add_fusion.1), channel_id=1, source_target_pairs={{0,24},{8,16},{16,8},{24,0},{1,25},{9,17},{17,9},{25,1},{2,26},{10... | collective-permute-start | bytes 49160 | tf_op jit(solution)/shard_map/ppermute | solution.py:201
  30.1 3.1 %collective-permute-start.14 = (f32[32,128]{1,0:T(8,128)S(1)}, f32[32,128]{1,0:T(8,128)S(1)}, u32[]{:S(2)}, u32[]{:S(2)}) collective-permute-start(f32[32,128]{1,0:T(8,128)S(1)} %collective-permute-done.12), channel_id=1, source_target_pairs={{0,1},{1,0},{2,3},{3,2},{4,5},{5,4},{6,7},{7,6},{8,9},{9,8},{10,11... | collective-permute-start | bytes 49160 | tf_op jit(solution)/shard_map/ppermute | solution.py:201

commit v5 on v4

--- a/solution.py
+++ b/solution.py
@@ -160,8 +160,7 @@
             pivot1 = {b: spread(column[g, b][s + 1 : s + 2]) for b in range(s, 8)}
             p00, p01, p11 = pivot0[s], pivot0[s + 1], pivot1[s + 1]
             det = p00 * p11 - p01 * p01
-            inv_det = pl.reciprocal(det, approx=True)
-            inv_det = inv_det * (2.0 - det * inv_det)
+            inv_det = 1.0 / det
             q00, q01, q11 = p11 * inv_det, p01 * inv_det, p00 * inv_det
             root0 = lax.rsqrt(p00)
             ratio = p01 * (root0 * root0)
@@ -215,8 +214,8 @@
             if len(masks) == 1:
                 parts = [swap(x, axis, masks[0])]
             else:
-                mine = swap(x, axis, *masks)
-                both = swap(x, axis, masks[0] ^ masks[1])
+                mine = swap(x, axis, masks[0], masks[0] ^ masks[1])
+                both = swap(x, axis, masks[1])
                 parts = [mine, both, swap(mine, "dev", 1)]
             x = x + sum(parts)
     return x

time: 36.5 us -> 34.7 us (0.951)
  waiting for transfers between devices: 11.2 us -> 9.25 us
    ppermute x14, waiting for transfers between devices: 11.2 us -> 9.25 us  [swap(): lax.ppermute(x, axis, [(i, i ^ (odd if i % 2 else mask)) for i in range(s...]
  transfers between devices with their start and end apart: 15 -> 15, of which waited for: 9 -> 9; matrix products, arithmetic and copies ran while one was open for 0% -> 0% of each run, Pallas kernels for 8% -> 9%
where the time goes in v5:
time: 34.7 us; the launch traced here: 34.5 us
  starting transfers between devices  16 us (46%)
  waiting for transfers between devices  9.25 us (27%)
  Pallas kernels  9.01 us (26%)
    ppermute x14, starting transfers between devices, swap(): lax.ppermute(x, axis, [(i, i ^ (odd if i % 2 else mask)) for i in range(s...  14.3 us
    ppermute x14, waiting for transfers between devices, swap(): lax.ppermute(x, axis, [(i, i ^ (odd if i % 2 else mask)) for i in range(s...  9.25 us
    pallas_call x1, Pallas kernels, body(): pl.pallas_call(solve_kernel, out_shape=jax.ShapeDtypeStruct((k_dim, row_c...  3.03 us
    pallas_call x1, Pallas kernels, body(): pl.pallas_call(functools.partial(product_kernel, masks), out_shape=(jax.S...  2.83 us
    ppermute x1, starting transfers between devices, swap(): return lax.ppermute(x, (axis, 'dev'), pairs)  1.64 us
    pallas_call x1, Pallas kernels, body(): pl.pallas_call(degree_kernel, out_shape=jax.ShapeDtypeStruct((blocks, row...  1.61 us
    pallas_call x1, Pallas kernels, body(): pl.pallas_call(plan_kernel, out_shape=[pltpu.SMEM(x.shape, x.dtype) for x...  0.81 us
  transfers between devices with their start and end apart: 15, of which 9 were waited for; matrix products, arithmetic and copies ran while one was open for 0% of the time, Pallas kernels for 9%

profile of v5, /device:TPU:0, one launch (start us, length us, event | category | flops | bytes accessed | tf_op | source)
XLA Modules:
  0.0 34.5 jit_solution(268293162701154384)
XLA Ops:
  0.0 0.0 copy-start.3
  0.0 0.0 copy-start
  0.0 0.0 copy-start.2
  0.0 0.5 %collective-permute-start.3 = (bf16[64,2048]{1,0:T(8,128)(2,1)}, bf16[64,2048]{1,0:T(8,128)(2,1)S(1)}, u32[]{:S(2)}, u32[]{:S(2)}) collective-permute-start(bf16[64,2048]{1,0:T(8,128)(2,1)} %sub_ref.1), channel_id=1, source_target_pairs={{0,1},{1,0},{2,3},{3,2},{4,5},{5,4},{6,7},{7,6},{8,9},{9,8},{10,11... | collective-permute-start | bytes 786440 | tf_op jit(solution)/shard_map/ppermute | solution.py:200
  0.5 0.0 copy-start.1
  0.5 0.1 copy-done.3
  0.7 3.9 %collective-permute-start.2 = (s32[1,2,8]{2,1,0:T(2,128)S(1)}, s32[1,2,8]{2,1,0:T(2,128)S(1)}, u32[]{:S(2)}, u32[]{:S(2)}) collective-permute-start(s32[1,2,8]{2,1,0:T(2,128)S(1)} %bitcast.3), channel_id=1, source_target_pairs={{0,6},{1,7},{2,4},{3,5},{4,2},{5,3},{6,0},{7,1},{8,14},{9,15},{10,... | collective-permute-start | bytes 200 | tf_op jit(solution)/shard_map/ppermute | solution.py:200
  4.6 0.5 %collective-permute-start.1 = (s32[1,2,8]{2,1,0:T(2,128)S(1)}, s32[1,2,8]{2,1,0:T(2,128)S(1)}, u32[]{:S(2)}, u32[]{:S(2)}) collective-permute-start(s32[1,2,8]{2,1,0:T(2,128)S(1)} %bitcast.4), channel_id=1, source_target_pairs={{0,4},{1,5},{2,6},{3,7},{4,0},{5,1},{6,2},{7,3},{8,12},{9,13},{10,... | collective-permute-start | bytes 200 | tf_op jit(solution)/shard_map/ppermute | solution.py:200
  5.1 0.1 collective-permute-start
  5.1 0.0 copy-done
  5.1 0.0 copy-done.2
  5.1 1.6 %degree.1.inv_ref = f32[16,128]{1,0:T(8,128)S(1)} custom-call(f32[8,128]{1,0:T(8,128)S(1)} %start.1.first_ref, s32[1,16]{1,0:T(1,128)S(1)} %bitcast.2, bf16[16,16,128,128]{3,2,1,0:T(8,128)(2,1)S(1)} %copy-done), custom_call_target="tpu_custom_call" | custom-call | flops 67108864 | bytes 8388608 | tf_op jit(solution)/shard_map/degree/pallas_call | solution.py:243
  6.8 0.0 collective-permute-start.4
  6.8 0.0 collective-permute-done.2.refs_3_
  6.8 1.3 %collective-permute-done.1.refs_2_ = s32[1,2,8]{2,1,0:T(2,128)S(1)} collective-permute-done((s32[1,2,8]{2,1,0:T(2,128)S(1)}, s32[1,2,8]{2,1,0:T(2,128)S(1)}, u32[]{:S(2)}, u32[]{:S(2)}) %collective-permute-start.1) | collective-permute-done | bytes 96 | tf_op jit(solution)/shard_map/ppermute | solution.py:200
  8.1 0.5 %collective-permute-done.refs_1_ = s32[1,2,8]{2,1,0:T(2,128)S(1)} collective-permute-done((s32[1,2,8]{2,1,0:T(2,128)S(1)}, s32[1,2,8]{2,1,0:T(2,128)S(1)}, u32[]{:S(2)}, u32[]{:S(2)}) %collective-permute-start) | collective-permute-done | bytes 96 | tf_op jit(solution)/shard_map/ppermute | solution.py:200
  8.7 0.6 %join.1.lists_ref = s32[4,2,8]{2,1,0:T(2,128)S(4)} custom-call(s32[1,2,8]{2,1,0:T(2,128)S(1)} %bitcast.6, s32[1,2,8]{2,1,0:T(2,128)S(1)} %collective-permute-done.refs_1_, s32[1,2,8]{2,1,0:T(2,128)S(1)} %collective-permute-done.1.refs_2_, s32[1,2,8]{2,1,0:T(2,128)S(1)} %collective-permute-done.2.refs_3_), custom_call_target="tpu_custom_call" | custom-call | flops 2000000000 | tf_op jit(solution)/shard_map/join/pallas_call | solution.py:255
  9.3 0.0 collective-permute-done.4.sib_inv_ref
  9.3 0.0 collective-permute-done.3.sib_sub_ref
  9.3 0.0 copy-done.1
  9.3 0.1 select.1
  9.4 1.6 %collective-permute-start.5 = (bf16[2,2,64,128]{3,2,1,0:T(8,128)(2,1)S(1)}, bf16[2,2,64,128]{3,2,1,0:T(8,128)(2,1)S(1)}, u32[]{:S(2)}, u32[]{:S(2)}) collective-permute-start(bf16[2,2,64,128]{3,2,1,0:T(8,128)(2,1)S(1)} %get-tuple-element.20), channel_id=1, source_target_pairs={{0,6},{1,7},{2,4},{3,5},{4,2},{5,3},{6,0},{7,1},{8,14},{9,15},{10,... | collective-permute-start | bytes 196616 | tf_op jit(solution)/shard_map/ppermute | solution.py:200
  11.0 0.5 %collective-permute-start.6 = (bf16[2,2,64,128]{3,2,1,0:T(8,128)(2,1)S(1)}, bf16[2,2,64,128]{3,2,1,0:T(8,128)(2,1)S(1)}, u32[]{:S(2)}, u32[]{:S(2)}) collective-permute-start(bf16[2,2,64,128]{3,2,1,0:T(8,128)(2,1)S(1)} %get-tuple-element.21), channel_id=1, source_target_pairs={{0,4},{1,5},{2,6},{3,7},{4,0},{5,1},{6,2},{7,3},{8,12},{9,13},{10,... | collective-permute-start | bytes 196616 | tf_op jit(solution)/shard_map/ppermute | solution.py:200
  11.6 1.4 %collective-permute-start.7 = (bf16[2,2,64,128]{3,2,1,0:T(8,128)(2,1)S(1)}, bf16[2,2,64,128]{3,2,1,0:T(8,128)(2,1)S(1)}, u32[]{:S(2)}, u32[]{:S(2)}) collective-permute-start(bf16[2,2,64,128]{3,2,1,0:T(8,128)(2,1)S(1)} %get-tuple-element.22), channel_id=1, source_target_pairs={{0,2},{1,3},{2,0},{3,1},{4,6},{5,7},{6,4},{7,5},{8,10},{9,11},{10,... | collective-permute-start | bytes 196616 | tf_op jit(solution)/shard_map/ppermute | solution.py:200
  13.0 0.8 %plan.1 = (s32[16]{0:T(128)S(4)}, s32[16,16]{1,0:T(8,128)S(4)}) custom-call(s32[16]{0:T(128)} %count_hbm.1, s32[16,16]{1,0:T(8,128)} %slot_hbm.1), custom_call_target="tpu_custom_call" | custom-call | flops 2000000000 | tf_op jit(solution)/shard_map/plan/pallas_call | solution.py:275
  13.8 1.0 %collective-permute-done.5.refs_1_ = bf16[2,2,64,128]{3,2,1,0:T(8,128)(2,1)S(1)} collective-permute-done((bf16[2,2,64,128]{3,2,1,0:T(8,128)(2,1)S(1)}, bf16[2,2,64,128]{3,2,1,0:T(8,128)(2,1)S(1)}, u32[]{:S(2)}, u32[]{:S(2)}) %collective-permute-start.5) | collective-permute-done | bytes 65568 | tf_op jit(solution)/shard_map/ppermute | solution.py:200
  14.8 0.9 %collective-permute-done.6.refs_2_ = bf16[2,2,64,128]{3,2,1,0:T(8,128)(2,1)S(1)} collective-permute-done((bf16[2,2,64,128]{3,2,1,0:T(8,128)(2,1)S(1)}, bf16[2,2,64,128]{3,2,1,0:T(8,128)(2,1)S(1)}, u32[]{:S(2)}, u32[]{:S(2)}) %collective-permute-start.6) | collective-permute-done | bytes 65568 | tf_op jit(solution)/shard_map/ppermute | solution.py:200
  15.6 0.2 collective-permute-done.7.refs_3_
  15.9 2.8 %product.1 = (bf16[128,2048]{1,0:T(8,128)(2,1)S(1)}, f32[32,128]{1,0:T(8,128)S(1)}) custom-call(s32[16]{0:T(128)S(4)} %get-tuple-element.15.count_ref, s32[16,16]{1,0:T(8,128)S(4)} %get-tuple-element.16.slot_ref, f32[16,128]{1,0:T(8,128)S(1)} %degree.1.inv_ref, bf16[16,16,128,128]{3,2,1,0:T(8,128)(2,1)S(1)} %copy-done, ...), custom_call_target="tpu_custom_call" | custom-call | flops 536870912 | bytes 8388608 | tf_op jit(solution)/shard_map/product/pallas_call | solution.py:287
  18.7 0.0 collective-permute-start.8
  18.7 1.2 %collective-permute-done.8 = f32[32,128]{1,0:T(8,128)S(1)} collective-permute-done((f32[32,128]{1,0:T(8,128)S(1)}, f32[32,128]{1,0:T(8,128)S(1)}, u32[]{:S(2)}, u32[]{:S(2)}) %collective-permute-start.8) | collective-permute-done | bytes 16416 | tf_op jit(solution)/shard_map/ppermute | solution.py:200
  19.9 1.4 %collective-permute-start.9 = (f32[32,128]{1,0:T(8,128)S(1)}, f32[32,128]{1,0:T(8,128)S(1)}, u32[]{:S(2)}, u32[]{:S(2)}) collective-permute-start(f32[32,128]{1,0:T(8,128)S(1)} %add.21), channel_id=1, source_target_pairs={{0,2},{1,7},{2,0},{3,5},{4,6},{5,3},{6,4},{7,1},{8,10},{9,15},{10,... | collective-permute-start | bytes 49160 | tf_op jit(solution)/shard_map/ppermute | solution.py:200
  21.3 1.5 %collective-permute-start.10 = (f32[32,128]{1,0:T(8,128)S(1)}, f32[32,128]{1,0:T(8,128)S(1)}, u32[]{:S(2)}, u32[]{:S(2)}) collective-permute-start(f32[32,128]{1,0:T(8,128)S(1)} %add.21), channel_id=1, source_target_pairs={{0,4},{1,5},{2,6},{3,7},{4,0},{5,1},{6,2},{7,3},{8,12},{9,13},{10,... | collective-permute-start | bytes 49160 | tf_op jit(solution)/shard_map/ppermute | solution.py:200
  22.8 0.9 %collective-permute-done.9 = f32[32,128]{1,0:T(8,128)S(1)} collective-permute-done((f32[32,128]{1,0:T(8,128)S(1)}, f32[32,128]{1,0:T(8,128)S(1)}, u32[]{:S(2)}, u32[]{:S(2)}) %collective-permute-start.9) | collective-permute-done | bytes 16416 | tf_op jit(solution)/shard_map/ppermute | solution.py:200
  23.7 0.0 collective-permute-start.11
  23.7 1.4 %collective-permute-done.10 = f32[32,128]{1,0:T(8,128)S(1)} collective-permute-done((f32[32,128]{1,0:T(8,128)S(1)}, f32[32,128]{1,0:T(8,128)S(1)}, u32[]{:S(2)}, u32[]{:S(2)}) %collective-permute-start.10) | collective-permute-done | bytes 16416 | tf_op jit(solution)/shard_map/ppermute | solution.py:200
  25.1 0.0 collective-permute-done.11
  25.1 1.6 %collective-permute-start.12 = (f32[32,128]{1,0:T(8,128)S(1)}, f32[32,128]{1,0:T(8,128)S(1)}, u32[]{:S(2)}, u32[]{:S(2)}) collective-permute-start(f32[32,128]{1,0:T(8,128)S(1)} %add_add_fusion.1), channel_id=1, source_target_pairs={{0,8},{1,25},{2,10},{3,27},{4,12},{5,29},{6,14},{7,31},{8,0},{9,17... | collective-permute-start | bytes 49160 | tf_op jit(solution)/shard_map/ppermute | solution.py:202
  26.7 2.6 %collective-permute-start.13 = (f32[32,128]{1,0:T(8,128)S(1)}, f32[32,128]{1,0:T(8,128)S(1)}, u32[]{:S(2)}, u32[]{:S(2)}) collective-permute-start(f32[32,128]{1,0:T(8,128)S(1)} %add_add_fusion.1), channel_id=1, source_target_pairs={{0,16},{8,24},{16,0},{24,8},{1,17},{9,25},{17,1},{25,9},{2,18},{10... | collective-permute-start | bytes 49160 | tf_op jit(solution)/shard_map/ppermute | solution.py:200
  29.3 0.0 collective-permute-done.12
  29.3 0.3 collective-permute-start.14
  29.6 1.9 %collective-permute-done.13 = f32[32,128]{1,0:T(8,128)S(1)} collective-permute-done((f32[32,128]{1,0:T(8,128)S(1)}, f32[32,128]{1,0:T(8,128)S(1)}, u32[]{:S(2)}, u32[]{:S(2)}) %collective-permute-start.13) | collective-permute-done | bytes 16416 | tf_op jit(solution)/shard_map/ppermute | solution.py:200
  31.5 0.0 collective-permute-done.14
  31.5 3.0 %solve.1 = f32[64,2048]{1,0:T(8,128)} custom-call(f32[32,128]{1,0:T(8,128)S(1)} %add_add_fusion.gram_ref, bf16[128,2048]{1,0:T(8,128)(2,1)S(1)} %get-tuple-element.24.applied_ref), custom_call_target="tpu_custom_call" | custom-call | tf_op jit(solution)/shard_map/solve/pallas_call | solution.py:305
  (4 shorter events, 0.0 us)
Async XLA Ops:
  0.0 0.7 %copy-start.3 = (s32[1,8,2]{1,2,0:T(2,128)S(1)}, s32[1,8,2]{1,2,0:T(2,128)}, u32[]{:S(2)}) copy-start(s32[1,8,2]{1,2,0:T(2,128)} %param.9) | copy-start | bytes 196
  0.0 5.1 %copy-start = (bf16[16,16,128,128]{3,2,1,0:T(8,128)(2,1)S(1)}, bf16[16,16,128,128]{3,2,1,0:T(8,128)(2,1)}, u32[]{:S(2)}) copy-start(bf16[16,16,128,128]{3,2,1,0:T(8,128)(2,1)} %tiles_ref.3) | copy-start | bytes 25165828
  0.0 5.1 %copy-start.2 = (s32[16]{0:T(128)S(1)}, s32[16]{0:T(128)}, u32[]{:S(2)}) copy-start(s32[16]{0:T(128)} %count_hbm.1) | copy-start | bytes 196
  0.0 9.3 %collective-permute-start.3 = (bf16[64,2048]{1,0:T(8,128)(2,1)}, bf16[64,2048]{1,0:T(8,128)(2,1)S(1)}, u32[]{:S(2)}, u32[]{:S(2)}) collective-permute-start(bf16[64,2048]{1,0:T(8,128)(2,1)} %sub_ref.1), channel_id=1, source_target_pairs={{0,1},{1,0},{2,3},{3,2},{4,5},{5,4},{6,7},{7,6},{8,9},{9,8},{10,11... | collective-permute-start | bytes 786440 | tf_op jit(solution)/shard_map/ppermute | solution.py:200
  0.5 8.8 %copy-start.1 = (bf16[64,2048]{1,0:T(8,128)(2,1)S(1)}, bf16[64,2048]{1,0:T(8,128)(2,1)}, u32[]{:S(2)}) copy-start(bf16[64,2048]{1,0:T(8,128)(2,1)} %sub_ref.1) | copy-start | bytes 786436
  0.7 6.1 %collective-permute-start.2 = (s32[1,2,8]{2,1,0:T(2,128)S(1)}, s32[1,2,8]{2,1,0:T(2,128)S(1)}, u32[]{:S(2)}, u32[]{:S(2)}) collective-permute-start(s32[1,2,8]{2,1,0:T(2,128)S(1)} %bitcast.3), channel_id=1, source_target_pairs={{0,6},{1,7},{2,4},{3,5},{4,2},{5,3},{6,0},{7,1},{8,14},{9,15},{10,... | collective-permute-start | bytes 200 | tf_op jit(solution)/shard_map/ppermute | solution.py:200
  4.6 3.6 %collective-permute-start.1 = (s32[1,2,8]{2,1,0:T(2,128)S(1)}, s32[1,2,8]{2,1,0:T(2,128)S(1)}, u32[]{:S(2)}, u32[]{:S(2)}) collective-permute-start(s32[1,2,8]{2,1,0:T(2,128)S(1)} %bitcast.4), channel_id=1, source_target_pairs={{0,4},{1,5},{2,6},{3,7},{4,0},{5,1},{6,2},{7,3},{8,12},{9,13},{10,... | collective-permute-start | bytes 200 | tf_op jit(solution)/shard_map/ppermute | solution.py:200
  5.1 3.6 %collective-permute-start = (s32[1,2,8]{2,1,0:T(2,128)S(1)}, s32[1,2,8]{2,1,0:T(2,128)S(1)}, u32[]{:S(2)}, u32[]{:S(2)}) collective-permute-start(s32[1,2,8]{2,1,0:T(2,128)S(1)} %bitcast.5), channel_id=1, source_target_pairs={{0,2},{1,3},{2,0},{3,1},{4,6},{5,7},{6,4},{7,5},{8,10},{9,11},{10,... | collective-permute-start | bytes 200 | tf_op jit(solution)/shard_map/ppermute | solution.py:200
  6.8 2.5 %collective-permute-start.4 = (f32[16,128]{1,0:T(8,128)S(1)}, f32[16,128]{1,0:T(8,128)S(1)}, u32[]{:S(2)}, u32[]{:S(2)}) collective-permute-start(f32[16,128]{1,0:T(8,128)S(1)} %degree.1.inv_ref), channel_id=1, source_target_pairs={{0,1},{1,0},{2,3},{3,2},{4,5},{5,4},{6,7},{7,6},{8,9},{9,8},{10,11... | collective-permute-start | bytes 24584 | tf_op jit(solution)/shard_map/ppermute | solution.py:200
  9.4 5.3 %collective-permute-start.5 = (bf16[2,2,64,128]{3,2,1,0:T(8,128)(2,1)S(1)}, bf16[2,2,64,128]{3,2,1,0:T(8,128)(2,1)S(1)}, u32[]{:S(2)}, u32[]{:S(2)}) collective-permute-start(bf16[2,2,64,128]{3,2,1,0:T(8,128)(2,1)S(1)} %get-tuple-element.20), channel_id=1, source_target_pairs={{0,6},{1,7},{2,4},{3,5},{4,2},{5,3},{6,0},{7,1},{8,14},{9,15},{10,... | collective-permute-start | bytes 196616 | tf_op jit(solution)/shard_map/ppermute | solution.py:200
  11.0 4.6 %collective-permute-start.6 = (bf16[2,2,64,128]{3,2,1,0:T(8,128)(2,1)S(1)}, bf16[2,2,64,128]{3,2,1,0:T(8,128)(2,1)S(1)}, u32[]{:S(2)}, u32[]{:S(2)}) collective-permute-start(bf16[2,2,64,128]{3,2,1,0:T(8,128)(2,1)S(1)} %get-tuple-element.21), channel_id=1, source_target_pairs={{0,4},{1,5},{2,6},{3,7},{4,0},{5,1},{6,2},{7,3},{8,12},{9,13},{10,... | collective-permute-start | bytes 196616 | tf_op jit(solution)/shard_map/ppermute | solution.py:200
  11.6 4.3 %collective-permute-start.7 = (bf16[2,2,64,128]{3,2,1,0:T(8,128)(2,1)S(1)}, bf16[2,2,64,128]{3,2,1,0:T(8,128)(2,1)S(1)}, u32[]{:S(2)}, u32[]{:S(2)}) collective-permute-start(bf16[2,2,64,128]{3,2,1,0:T(8,128)(2,1)S(1)} %get-tuple-element.22), channel_id=1, source_target_pairs={{0,2},{1,3},{2,0},{3,1},{4,6},{5,7},{6,4},{7,5},{8,10},{9,11},{10,... | collective-permute-start | bytes 196616 | tf_op jit(solution)/shard_map/ppermute | solution.py:200
  18.7 1.2 %collective-permute-start.8 = (f32[32,128]{1,0:T(8,128)S(1)}, f32[32,128]{1,0:T(8,128)S(1)}, u32[]{:S(2)}, u32[]{:S(2)}) collective-permute-start(f32[32,128]{1,0:T(8,128)S(1)} %get-tuple-element.23), channel_id=1, source_target_pairs={{0,1},{1,0},{2,3},{3,2},{4,5},{5,4},{6,7},{7,6},{8,9},{9,8},{10,11... | collective-permute-start | bytes 49160 | tf_op jit(solution)/shard_map/ppermute | solution.py:200
  19.9 3.8 %collective-permute-start.9 = (f32[32,128]{1,0:T(8,128)S(1)}, f32[32,128]{1,0:T(8,128)S(1)}, u32[]{:S(2)}, u32[]{:S(2)}) collective-permute-start(f32[32,128]{1,0:T(8,128)S(1)} %add.21), channel_id=1, source_target_pairs={{0,2},{1,7},{2,0},{3,5},{4,6},{5,3},{6,4},{7,1},{8,10},{9,15},{10,... | collective-permute-start | bytes 49160 | tf_op jit(solution)/shard_map/ppermute | solution.py:200
  21.3 3.8 %collective-permute-start.10 = (f32[32,128]{1,0:T(8,128)S(1)}, f32[32,128]{1,0:T(8,128)S(1)}, u32[]{:S(2)}, u32[]{:S(2)}) collective-permute-start(f32[32,128]{1,0:T(8,128)S(1)} %add.21), channel_id=1, source_target_pairs={{0,4},{1,5},{2,6},{3,7},{4,0},{5,1},{6,2},{7,3},{8,12},{9,13},{10,... | collective-permute-start | bytes 49160 | tf_op jit(solution)/shard_map/ppermute | solution.py:200
  23.7 1.4 %collective-permute-start.11 = (f32[32,128]{1,0:T(8,128)S(1)}, f32[32,128]{1,0:T(8,128)S(1)}, u32[]{:S(2)}, u32[]{:S(2)}) collective-permute-start(f32[32,128]{1,0:T(8,128)S(1)} %collective-permute-done.9), channel_id=1, source_target_pairs={{0,1},{1,0},{2,3},{3,2},{4,5},{5,4},{6,7},{7,6},{8,9},{9,8},{10,11... | collective-permute-start | bytes 49160 | tf_op jit(solution)/shard_map/ppermute | solution.py:200
  25.1 4.2 %collective-permute-start.12 = (f32[32,128]{1,0:T(8,128)S(1)}, f32[32,128]{1,0:T(8,128)S(1)}, u32[]{:S(2)}, u32[]{:S(2)}) collective-permute-start(f32[32,128]{1,0:T(8,128)S(1)} %add_add_fusion.1), channel_id=1, source_target_pairs={{0,8},{1,25},{2,10},{3,27},{4,12},{5,29},{6,14},{7,31},{8,0},{9,17... | collective-permute-start | bytes 49160 | tf_op jit(solution)/shard_map/ppermute | solution.py:202
  26.7 4.7 %collective-permute-start.13 = (f32[32,128]{1,0:T(8,128)S(1)}, f32[32,128]{1,0:T(8,128)S(1)}, u32[]{:S(2)}, u32[]{:S(2)}) collective-permute-start(f32[32,128]{1,0:T(8,128)S(1)} %add_add_fusion.1), channel_id=1, source_target_pairs={{0,16},{8,24},{16,0},{24,8},{1,17},{9,25},{17,1},{25,9},{2,18},{10... | collective-permute-start | bytes 49160 | tf_op jit(solution)/shard_map/ppermute | solution.py:200
  29.3 2.1 %collective-permute-start.14 = (f32[32,128]{1,0:T(8,128)S(1)}, f32[32,128]{1,0:T(8,128)S(1)}, u32[]{:S(2)}, u32[]{:S(2)}) collective-permute-start(f32[32,128]{1,0:T(8,128)S(1)} %collective-permute-done.12), channel_id=1, source_target_pairs={{0,1},{1,0},{2,3},{3,2},{4,5},{5,4},{6,7},{7,6},{8,9},{9,8},{10,11... | collective-permute-start | bytes 49160 | tf_op jit(solution)/shard_map/ppermute | solution.py:200

commit v6 on v5

--- a/solution.py
+++ b/solution.py
@@ -51,22 +51,21 @@
 
 
 def join_kernel(*refs):
-    *list_refs, out_ref, sems = refs
-    copies = [
-        pltpu.make_async_copy(ref.at[0], out_ref.at[i], sems.at[i]) for i, ref in enumerate(list_refs)
-    ]
-    for copy in copies:
-        copy.start()
-    for copy in copies:
-        copy.wait()
+    for i, ref in enumerate(refs[:-1]):
+        refs[-1][i] = ref[0]
 
 
 def select_kernel(masks, lists_ref, sub_ref, sib_sub_ref, inv_ref, sib_inv_ref, *send_refs):
     cap, cols = lists_ref.shape[1], inv_ref.shape[1]
     me = lax.axis_index("dev")
     sources = ((me, sub_ref, inv_ref), (me ^ 1, sib_sub_ref, sib_inv_ref))
+    peer = lax.broadcasted_iota(jnp.int32, (1, lists_ref.shape[2]), 1)
+
+    def block_id(chip, j, source):
+        return jnp.sum(jnp.where(peer == source, lists_ref[chip, j : j + 1], 0))
+
     ids = [
-        [lists_ref[mask // 2, j, source] for source, _, _ in sources for j in range(cap)]
+        [block_id(mask // 2, j, source) for source, _, _ in sources for j in range(cap)]
         for mask in masks
     ]
     for blocks, send in zip(ids, send_refs, strict=True):
@@ -254,10 +253,9 @@
     sib_inv_root = swap(inv_root, "dev", 1)
     lists = pl.pallas_call(
         join_kernel,
-        out_shape=pltpu.SMEM((chips, cap, peers), jnp.int32),
+        out_shape=jax.ShapeDtypeStruct((chips, cap, peers), jnp.int32),
         in_specs=[VMEM] * chips,
-        out_specs=SMEM,
-        scratch_shapes=[pltpu.SemaphoreType.DMA((chips,))],
+        out_specs=VMEM,
         compiler_params=limit(1),
         cost_estimate=pl.CostEstimate(flops=2 * 10**9, bytes_accessed=0, transcendentals=0),
         name="join",
@@ -265,11 +263,11 @@
     sends = pl.pallas_call(
         functools.partial(select_kernel, masks),
         out_shape=[jax.ShapeDtypeStruct((2, cap, k_dim, cols), BF16)] * chips,
-        in_specs=[SMEM] + [VMEM] * 4,
+        in_specs=[VMEM] * 5,
         out_specs=[VMEM] * chips,
         compiler_params=limit(2),
         name="select",
-    )(pltpu.with_memory_space_constraint(lists, pltpu.SMEM), subspace, sib_columns, inv_root, sib_inv_root)
+    )(lists, subspace, sib_columns, inv_root, sib_inv_root)
     parts = [swap(x, "dev", mask) if mask else x for x, mask in zip(sends, masks, strict=True)]
 
     plan = pl.pallas_call(

time: 34.7 us -> 34.7 us (level)
  waiting for transfers between devices: 9.25 us -> 10.2 us
  starting transfers between devices: 16 us -> 15.5 us
  Pallas kernels: 9.01 us -> 8.53 us
    ppermute x14, waiting for transfers between devices: 9.25 us -> 10.2 us  [swap(): lax.ppermute(x, axis, [(i, i ^ (odd if i % 2 else mask)) for i in range(s...]
    pallas_call x1, Pallas kernels: 0.63 us -> 0.01 us  [body(): pl.pallas_call(join_kernel, out_shape=jax.ShapeDtypeStruct((chips, cap, p...]
    ppermute x14, starting transfers between devices: 14.3 us -> 13.9 us  [swap(): lax.ppermute(x, axis, [(i, i ^ (odd if i % 2 else mask)) for i in range(s...]
  transfers between devices with their start and end apart: 15 -> 15, of which waited for: 9 -> 10; matrix products, arithmetic and copies ran while one was open for 0% -> 0% of each run, Pallas kernels for 9% -> 7%
where the time goes in v6:
time: 34.7 us; the launch traced here: 34.5 us
  starting transfers between devices  15.5 us (45%)
  waiting for transfers between devices  10.2 us (29%)
  Pallas kernels  8.53 us (25%)
    ppermute x14, starting transfers between devices, swap(): lax.ppermute(x, axis, [(i, i ^ (odd if i % 2 else mask)) for i in range(s...  13.9 us
    ppermute x14, waiting for transfers between devices, swap(): lax.ppermute(x, axis, [(i, i ^ (odd if i % 2 else mask)) for i in range(s...  10.2 us
    pallas_call x1, Pallas kernels, body(): pl.pallas_call(solve_kernel, out_shape=jax.ShapeDtypeStruct((k_dim, row_c...  3.03 us
    pallas_call x1, Pallas kernels, body(): pl.pallas_call(functools.partial(product_kernel, masks), out_shape=(jax.S...  2.83 us
    pallas_call x1, Pallas kernels, body(): pl.pallas_call(degree_kernel, out_shape=jax.ShapeDtypeStruct((blocks, row...  1.61 us
    ppermute x1, starting transfers between devices, swap(): return lax.ppermute(x, (axis, 'dev'), pairs)  1.58 us
    pallas_call x1, Pallas kernels, body(): pl.pallas_call(plan_kernel, out_shape=[pltpu.SMEM(x.shape, x.dtype) for x...  0.81 us
  transfers between devices with their start and end apart: 15, of which 10 were waited for; matrix products, arithmetic and copies ran while one was open for 0% of the time, Pallas kernels for 7%

profile of v6, /device:TPU:0, one launch (start us, length us, event | category | flops | bytes accessed | tf_op | source)
XLA Modules:
  0.0 34.5 jit_solution(10231480561959996216)
XLA Ops:
  0.0 0.0 copy-start.3
  0.0 0.0 copy-start
  0.0 0.0 copy-start.2
  0.0 0.5 %collective-permute-start.3 = (bf16[64,2048]{1,0:T(8,128)(2,1)}, bf16[64,2048]{1,0:T(8,128)(2,1)S(1)}, u32[]{:S(2)}, u32[]{:S(2)}) collective-permute-start(bf16[64,2048]{1,0:T(8,128)(2,1)} %sub_ref.1), channel_id=1, source_target_pairs={{0,1},{1,0},{2,3},{3,2},{4,5},{5,4},{6,7},{7,6},{8,9},{9,8},{10,11... | collective-permute-start | bytes 786440 | tf_op jit(solution)/shard_map/ppermute | solution.py:199
  0.5 0.0 copy-start.1
  0.5 0.1 copy-done.3
  0.7 3.9 %collective-permute-start.2 = (s32[1,2,8]{2,1,0:T(2,128)S(1)}, s32[1,2,8]{2,1,0:T(2,128)S(1)}, u32[]{:S(2)}, u32[]{:S(2)}) collective-permute-start(s32[1,2,8]{2,1,0:T(2,128)S(1)} %bitcast.3), channel_id=1, source_target_pairs={{0,6},{1,7},{2,4},{3,5},{4,2},{5,3},{6,0},{7,1},{8,14},{9,15},{10,... | collective-permute-start | bytes 200 | tf_op jit(solution)/shard_map/ppermute | solution.py:199
  4.6 0.5 %collective-permute-start.1 = (s32[1,2,8]{2,1,0:T(2,128)S(1)}, s32[1,2,8]{2,1,0:T(2,128)S(1)}, u32[]{:S(2)}, u32[]{:S(2)}) collective-permute-start(s32[1,2,8]{2,1,0:T(2,128)S(1)} %bitcast.4), channel_id=1, source_target_pairs={{0,4},{1,5},{2,6},{3,7},{4,0},{5,1},{6,2},{7,3},{8,12},{9,13},{10,... | collective-permute-start | bytes 200 | tf_op jit(solution)/shard_map/ppermute | solution.py:199
  5.1 0.1 collective-permute-start
  5.1 0.0 copy-done
  5.1 0.0 copy-done.2
  5.1 1.6 %degree.1.inv_ref = f32[16,128]{1,0:T(8,128)S(1)} custom-call(f32[8,128]{1,0:T(8,128)S(1)} %start.1.first_ref, s32[1,16]{1,0:T(1,128)S(1)} %bitcast.2, bf16[16,16,128,128]{3,2,1,0:T(8,128)(2,1)S(1)} %copy-done), custom_call_target="tpu_custom_call" | custom-call | flops 67108864 | bytes 8388608 | tf_op jit(solution)/shard_map/degree/pallas_call | solution.py:242
  6.8 0.0 collective-permute-start.4
  6.8 0.0 collective-permute-done.2.refs_3_
  6.8 1.3 %collective-permute-done.1.refs_2_ = s32[1,2,8]{2,1,0:T(2,128)S(1)} collective-permute-done((s32[1,2,8]{2,1,0:T(2,128)S(1)}, s32[1,2,8]{2,1,0:T(2,128)S(1)}, u32[]{:S(2)}, u32[]{:S(2)}) %collective-permute-start.1) | collective-permute-done | bytes 96 | tf_op jit(solution)/shard_map/ppermute | solution.py:199
  8.1 0.5 %collective-permute-done.refs_1_ = s32[1,2,8]{2,1,0:T(2,128)S(1)} collective-permute-done((s32[1,2,8]{2,1,0:T(2,128)S(1)}, s32[1,2,8]{2,1,0:T(2,128)S(1)}, u32[]{:S(2)}, u32[]{:S(2)}) %collective-permute-start) | collective-permute-done | bytes 96 | tf_op jit(solution)/shard_map/ppermute | solution.py:199
  8.7 0.0 collective-permute-done.4.sib_inv_ref
  8.7 0.0 collective-permute-done.3.sib_sub_ref
  8.7 0.0 copy-done.1
  8.7 0.2 select.1
  8.9 2.3 %collective-permute-start.5 = (bf16[2,2,64,128]{3,2,1,0:T(8,128)(2,1)S(1)}, bf16[2,2,64,128]{3,2,1,0:T(8,128)(2,1)S(1)}, u32[]{:S(2)}, u32[]{:S(2)}) collective-permute-start(bf16[2,2,64,128]{3,2,1,0:T(8,128)(2,1)S(1)} %get-tuple-element.20), channel_id=1, source_target_pairs={{0,6},{1,7},{2,4},{3,5},{4,2},{5,3},{6,0},{7,1},{8,14},{9,15},{10,... | collective-permute-start | bytes 196616 | tf_op jit(solution)/shard_map/ppermute | solution.py:199
  11.2 0.5 %collective-permute-start.6 = (bf16[2,2,64,128]{3,2,1,0:T(8,128)(2,1)S(1)}, bf16[2,2,64,128]{3,2,1,0:T(8,128)(2,1)S(1)}, u32[]{:S(2)}, u32[]{:S(2)}) collective-permute-start(bf16[2,2,64,128]{3,2,1,0:T(8,128)(2,1)S(1)} %get-tuple-element.21), channel_id=1, source_target_pairs={{0,4},{1,5},{2,6},{3,7},{4,0},{5,1},{6,2},{7,3},{8,12},{9,13},{10,... | collective-permute-start | bytes 196616 | tf_op jit(solution)/shard_map/ppermute | solution.py:199
  11.7 0.8 %collective-permute-start.7 = (bf16[2,2,64,128]{3,2,1,0:T(8,128)(2,1)S(1)}, bf16[2,2,64,128]{3,2,1,0:T(8,128)(2,1)S(1)}, u32[]{:S(2)}, u32[]{:S(2)}) collective-permute-start(bf16[2,2,64,128]{3,2,1,0:T(8,128)(2,1)S(1)} %get-tuple-element.22), channel_id=1, source_target_pairs={{0,2},{1,3},{2,0},{3,1},{4,6},{5,7},{6,4},{7,5},{8,10},{9,11},{10,... | collective-permute-start | bytes 196616 | tf_op jit(solution)/shard_map/ppermute | solution.py:199
  12.5 0.8 %plan.1 = (s32[16]{0:T(128)S(4)}, s32[16,16]{1,0:T(8,128)S(4)}) custom-call(s32[16]{0:T(128)} %count_hbm.1, s32[16,16]{1,0:T(8,128)} %slot_hbm.1), custom_call_target="tpu_custom_call" | custom-call | flops 2000000000 | tf_op jit(solution)/shard_map/plan/pallas_call | solution.py:273
  13.3 0.9 %collective-permute-done.5.refs_1_ = bf16[2,2,64,128]{3,2,1,0:T(8,128)(2,1)S(1)} collective-permute-done((bf16[2,2,64,128]{3,2,1,0:T(8,128)(2,1)S(1)}, bf16[2,2,64,128]{3,2,1,0:T(8,128)(2,1)S(1)}, u32[]{:S(2)}, u32[]{:S(2)}) %collective-permute-start.5) | collective-permute-done | bytes 65568 | tf_op jit(solution)/shard_map/ppermute | solution.py:199
  14.2 1.4 %collective-permute-done.6.refs_2_ = bf16[2,2,64,128]{3,2,1,0:T(8,128)(2,1)S(1)} collective-permute-done((bf16[2,2,64,128]{3,2,1,0:T(8,128)(2,1)S(1)}, bf16[2,2,64,128]{3,2,1,0:T(8,128)(2,1)S(1)}, u32[]{:S(2)}, u32[]{:S(2)}) %collective-permute-start.6) | collective-permute-done | bytes 65568 | tf_op jit(solution)/shard_map/ppermute | solution.py:199
  15.5 0.4 %collective-permute-done.7.refs_3_ = bf16[2,2,64,128]{3,2,1,0:T(8,128)(2,1)S(1)} collective-permute-done((bf16[2,2,64,128]{3,2,1,0:T(8,128)(2,1)S(1)}, bf16[2,2,64,128]{3,2,1,0:T(8,128)(2,1)S(1)}, u32[]{:S(2)}, u32[]{:S(2)}) %collective-permute-start.7) | collective-permute-done | bytes 65568 | tf_op jit(solution)/shard_map/ppermute | solution.py:199
  16.0 2.8 %product.1 = (bf16[128,2048]{1,0:T(8,128)(2,1)S(1)}, f32[32,128]{1,0:T(8,128)S(1)}) custom-call(s32[16]{0:T(128)S(4)} %get-tuple-element.15.count_ref, s32[16,16]{1,0:T(8,128)S(4)} %get-tuple-element.16.slot_ref, f32[16,128]{1,0:T(8,128)S(1)} %degree.1.inv_ref, bf16[16,16,128,128]{3,2,1,0:T(8,128)(2,1)S(1)} %copy-done, ...), custom_call_target="tpu_custom_call" | custom-call | flops 536870912 | bytes 8388608 | tf_op jit(solution)/shard_map/product/pallas_call | solution.py:285
  18.8 0.0 collective-permute-start.8
  18.8 1.2 %collective-permute-done.8 = f32[32,128]{1,0:T(8,128)S(1)} collective-permute-done((f32[32,128]{1,0:T(8,128)S(1)}, f32[32,128]{1,0:T(8,128)S(1)}, u32[]{:S(2)}, u32[]{:S(2)}) %collective-permute-start.8) | collective-permute-done | bytes 16416 | tf_op jit(solution)/shard_map/ppermute | solution.py:199
  20.0 0.8 %collective-permute-start.9 = (f32[32,128]{1,0:T(8,128)S(1)}, f32[32,128]{1,0:T(8,128)S(1)}, u32[]{:S(2)}, u32[]{:S(2)}) collective-permute-start(f32[32,128]{1,0:T(8,128)S(1)} %add.21), channel_id=1, source_target_pairs={{0,2},{1,7},{2,0},{3,5},{4,6},{5,3},{6,4},{7,1},{8,10},{9,15},{10,... | collective-permute-start | bytes 49160 | tf_op jit(solution)/shard_map/ppermute | solution.py:199
  20.8 1.5 %collective-permute-start.10 = (f32[32,128]{1,0:T(8,128)S(1)}, f32[32,128]{1,0:T(8,128)S(1)}, u32[]{:S(2)}, u32[]{:S(2)}) collective-permute-start(f32[32,128]{1,0:T(8,128)S(1)} %add.21), channel_id=1, source_target_pairs={{0,4},{1,5},{2,6},{3,7},{4,0},{5,1},{6,2},{7,3},{8,12},{9,13},{10,... | collective-permute-start | bytes 49160 | tf_op jit(solution)/shard_map/ppermute | solution.py:199
  22.3 1.5 %collective-permute-done.9 = f32[32,128]{1,0:T(8,128)S(1)} collective-permute-done((f32[32,128]{1,0:T(8,128)S(1)}, f32[32,128]{1,0:T(8,128)S(1)}, u32[]{:S(2)}, u32[]{:S(2)}) %collective-permute-start.9) | collective-permute-done | bytes 16416 | tf_op jit(solution)/shard_map/ppermute | solution.py:199
  23.8 0.0 collective-permute-start.11
  23.8 0.8 %collective-permute-done.10 = f32[32,128]{1,0:T(8,128)S(1)} collective-permute-done((f32[32,128]{1,0:T(8,128)S(1)}, f32[32,128]{1,0:T(8,128)S(1)}, u32[]{:S(2)}, u32[]{:S(2)}) %collective-permute-start.10) | collective-permute-done | bytes 16416 | tf_op jit(solution)/shard_map/ppermute | solution.py:199
  24.6 0.4 %collective-permute-done.11 = f32[32,128]{1,0:T(8,128)S(1)} collective-permute-done((f32[32,128]{1,0:T(8,128)S(1)}, f32[32,128]{1,0:T(8,128)S(1)}, u32[]{:S(2)}, u32[]{:S(2)}) %collective-permute-start.11) | collective-permute-done | bytes 16416 | tf_op jit(solution)/shard_map/ppermute | solution.py:199
  25.0 1.6 %collective-permute-start.12 = (f32[32,128]{1,0:T(8,128)S(1)}, f32[32,128]{1,0:T(8,128)S(1)}, u32[]{:S(2)}, u32[]{:S(2)}) collective-permute-start(f32[32,128]{1,0:T(8,128)S(1)} %add_add_fusion.1), channel_id=1, source_target_pairs={{0,8},{1,25},{2,10},{3,27},{4,12},{5,29},{6,14},{7,31},{8,0},{9,17... | collective-permute-start | bytes 49160 | tf_op jit(solution)/shard_map/ppermute | solution.py:201
  26.6 2.6 %collective-permute-start.13 = (f32[32,128]{1,0:T(8,128)S(1)}, f32[32,128]{1,0:T(8,128)S(1)}, u32[]{:S(2)}, u32[]{:S(2)}) collective-permute-start(f32[32,128]{1,0:T(8,128)S(1)} %add_add_fusion.1), channel_id=1, source_target_pairs={{0,16},{8,24},{16,0},{24,8},{1,17},{9,25},{17,1},{25,9},{2,18},{10... | collective-permute-start | bytes 49160 | tf_op jit(solution)/shard_map/ppermute | solution.py:199
  29.1 0.0 collective-permute-done.12
  29.2 0.4 %collective-permute-start.14 = (f32[32,128]{1,0:T(8,128)S(1)}, f32[32,128]{1,0:T(8,128)S(1)}, u32[]{:S(2)}, u32[]{:S(2)}) collective-permute-start(f32[32,128]{1,0:T(8,128)S(1)} %collective-permute-done.12), channel_id=1, source_target_pairs={{0,1},{1,0},{2,3},{3,2},{4,5},{5,4},{6,7},{7,6},{8,9},{9,8},{10,11... | collective-permute-start | bytes 49160 | tf_op jit(solution)/shard_map/ppermute | solution.py:199
  29.6 1.8 %collective-permute-done.13 = f32[32,128]{1,0:T(8,128)S(1)} collective-permute-done((f32[32,128]{1,0:T(8,128)S(1)}, f32[32,128]{1,0:T(8,128)S(1)}, u32[]{:S(2)}, u32[]{:S(2)}) %collective-permute-start.13) | collective-permute-done | bytes 16416 | tf_op jit(solution)/shard_map/ppermute | solution.py:199
  31.4 0.0 collective-permute-done.14
  31.4 3.0 %solve.1 = f32[64,2048]{1,0:T(8,128)} custom-call(f32[32,128]{1,0:T(8,128)S(1)} %add_add_fusion.gram_ref, bf16[128,2048]{1,0:T(8,128)(2,1)S(1)} %get-tuple-element.24.applied_ref), custom_call_target="tpu_custom_call" | custom-call | tf_op jit(solution)/shard_map/solve/pallas_call | solution.py:303
  (5 shorter events, 0.0 us)
Async XLA Ops:
  0.0 0.7 %copy-start.3 = (s32[1,8,2]{1,2,0:T(2,128)S(1)}, s32[1,8,2]{1,2,0:T(2,128)}, u32[]{:S(2)}) copy-start(s32[1,8,2]{1,2,0:T(2,128)} %param.9) | copy-start | bytes 196
  0.0 5.1 %copy-start = (bf16[16,16,128,128]{3,2,1,0:T(8,128)(2,1)S(1)}, bf16[16,16,128,128]{3,2,1,0:T(8,128)(2,1)}, u32[]{:S(2)}) copy-start(bf16[16,16,128,128]{3,2,1,0:T(8,128)(2,1)} %tiles_ref.3) | copy-start | bytes 25165828
  0.0 5.1 %copy-start.2 = (s32[16]{0:T(128)S(1)}, s32[16]{0:T(128)}, u32[]{:S(2)}) copy-start(s32[16]{0:T(128)} %count_hbm.1) | copy-start | bytes 196
  0.0 8.7 %collective-permute-start.3 = (bf16[64,2048]{1,0:T(8,128)(2,1)}, bf16[64,2048]{1,0:T(8,128)(2,1)S(1)}, u32[]{:S(2)}, u32[]{:S(2)}) collective-permute-start(bf16[64,2048]{1,0:T(8,128)(2,1)} %sub_ref.1), channel_id=1, source_target_pairs={{0,1},{1,0},{2,3},{3,2},{4,5},{5,4},{6,7},{7,6},{8,9},{9,8},{10,11... | collective-permute-start | bytes 786440 | tf_op jit(solution)/shard_map/ppermute | solution.py:199
  0.5 8.1 %copy-start.1 = (bf16[64,2048]{1,0:T(8,128)(2,1)S(1)}, bf16[64,2048]{1,0:T(8,128)(2,1)}, u32[]{:S(2)}) copy-start(bf16[64,2048]{1,0:T(8,128)(2,1)} %sub_ref.1) | copy-start | bytes 786436
  0.7 6.1 %collective-permute-start.2 = (s32[1,2,8]{2,1,0:T(2,128)S(1)}, s32[1,2,8]{2,1,0:T(2,128)S(1)}, u32[]{:S(2)}, u32[]{:S(2)}) collective-permute-start(s32[1,2,8]{2,1,0:T(2,128)S(1)} %bitcast.3), channel_id=1, source_target_pairs={{0,6},{1,7},{2,4},{3,5},{4,2},{5,3},{6,0},{7,1},{8,14},{9,15},{10,... | collective-permute-start | bytes 200 | tf_op jit(solution)/shard_map/ppermute | solution.py:199
  4.6 3.6 %collective-permute-start.1 = (s32[1,2,8]{2,1,0:T(2,128)S(1)}, s32[1,2,8]{2,1,0:T(2,128)S(1)}, u32[]{:S(2)}, u32[]{:S(2)}) collective-permute-start(s32[1,2,8]{2,1,0:T(2,128)S(1)} %bitcast.4), channel_id=1, source_target_pairs={{0,4},{1,5},{2,6},{3,7},{4,0},{5,1},{6,2},{7,3},{8,12},{9,13},{10,... | collective-permute-start | bytes 200 | tf_op jit(solution)/shard_map/ppermute | solution.py:199
  5.1 3.6 %collective-permute-start = (s32[1,2,8]{2,1,0:T(2,128)S(1)}, s32[1,2,8]{2,1,0:T(2,128)S(1)}, u32[]{:S(2)}, u32[]{:S(2)}) collective-permute-start(s32[1,2,8]{2,1,0:T(2,128)S(1)} %bitcast.5), channel_id=1, source_target_pairs={{0,2},{1,3},{2,0},{3,1},{4,6},{5,7},{6,4},{7,5},{8,10},{9,11},{10,... | collective-permute-start | bytes 200 | tf_op jit(solution)/shard_map/ppermute | solution.py:199
  6.8 1.9 %collective-permute-start.4 = (f32[16,128]{1,0:T(8,128)S(1)}, f32[16,128]{1,0:T(8,128)S(1)}, u32[]{:S(2)}, u32[]{:S(2)}) collective-permute-start(f32[16,128]{1,0:T(8,128)S(1)} %degree.1.inv_ref), channel_id=1, source_target_pairs={{0,1},{1,0},{2,3},{3,2},{4,5},{5,4},{6,7},{7,6},{8,9},{9,8},{10,11... | collective-permute-start | bytes 24584 | tf_op jit(solution)/shard_map/ppermute | solution.py:199
  8.9 5.3 %collective-permute-start.5 = (bf16[2,2,64,128]{3,2,1,0:T(8,128)(2,1)S(1)}, bf16[2,2,64,128]{3,2,1,0:T(8,128)(2,1)S(1)}, u32[]{:S(2)}, u32[]{:S(2)}) collective-permute-start(bf16[2,2,64,128]{3,2,1,0:T(8,128)(2,1)S(1)} %get-tuple-element.20), channel_id=1, source_target_pairs={{0,6},{1,7},{2,4},{3,5},{4,2},{5,3},{6,0},{7,1},{8,14},{9,15},{10,... | collective-permute-start | bytes 196616 | tf_op jit(solution)/shard_map/ppermute | solution.py:199
  11.2 4.3 %collective-permute-start.6 = (bf16[2,2,64,128]{3,2,1,0:T(8,128)(2,1)S(1)}, bf16[2,2,64,128]{3,2,1,0:T(8,128)(2,1)S(1)}, u32[]{:S(2)}, u32[]{:S(2)}) collective-permute-start(bf16[2,2,64,128]{3,2,1,0:T(8,128)(2,1)S(1)} %get-tuple-element.21), channel_id=1, source_target_pairs={{0,4},{1,5},{2,6},{3,7},{4,0},{5,1},{6,2},{7,3},{8,12},{9,13},{10,... | collective-permute-start | bytes 196616 | tf_op jit(solution)/shard_map/ppermute | solution.py:199
  11.7 4.3 %collective-permute-start.7 = (bf16[2,2,64,128]{3,2,1,0:T(8,128)(2,1)S(1)}, bf16[2,2,64,128]{3,2,1,0:T(8,128)(2,1)S(1)}, u32[]{:S(2)}, u32[]{:S(2)}) collective-permute-start(bf16[2,2,64,128]{3,2,1,0:T(8,128)(2,1)S(1)} %get-tuple-element.22), channel_id=1, source_target_pairs={{0,2},{1,3},{2,0},{3,1},{4,6},{5,7},{6,4},{7,5},{8,10},{9,11},{10,... | collective-permute-start | bytes 196616 | tf_op jit(solution)/shard_map/ppermute | solution.py:199
  18.8 1.2 %collective-permute-start.8 = (f32[32,128]{1,0:T(8,128)S(1)}, f32[32,128]{1,0:T(8,128)S(1)}, u32[]{:S(2)}, u32[]{:S(2)}) collective-permute-start(f32[32,128]{1,0:T(8,128)S(1)} %get-tuple-element.23), channel_id=1, source_target_pairs={{0,1},{1,0},{2,3},{3,2},{4,5},{5,4},{6,7},{7,6},{8,9},{9,8},{10,11... | collective-permute-start | bytes 49160 | tf_op jit(solution)/shard_map/ppermute | solution.py:199
  20.0 3.8 %collective-permute-start.9 = (f32[32,128]{1,0:T(8,128)S(1)}, f32[32,128]{1,0:T(8,128)S(1)}, u32[]{:S(2)}, u32[]{:S(2)}) collective-permute-start(f32[32,128]{1,0:T(8,128)S(1)} %add.21), channel_id=1, source_target_pairs={{0,2},{1,7},{2,0},{3,5},{4,6},{5,3},{6,4},{7,1},{8,10},{9,15},{10,... | collective-permute-start | bytes 49160 | tf_op jit(solution)/shard_map/ppermute | solution.py:199
  20.8 3.8 %collective-permute-start.10 = (f32[32,128]{1,0:T(8,128)S(1)}, f32[32,128]{1,0:T(8,128)S(1)}, u32[]{:S(2)}, u32[]{:S(2)}) collective-permute-start(f32[32,128]{1,0:T(8,128)S(1)} %add.21), channel_id=1, source_target_pairs={{0,4},{1,5},{2,6},{3,7},{4,0},{5,1},{6,2},{7,3},{8,12},{9,13},{10,... | collective-permute-start | bytes 49160 | tf_op jit(solution)/shard_map/ppermute | solution.py:199
  23.8 1.2 %collective-permute-start.11 = (f32[32,128]{1,0:T(8,128)S(1)}, f32[32,128]{1,0:T(8,128)S(1)}, u32[]{:S(2)}, u32[]{:S(2)}) collective-permute-start(f32[32,128]{1,0:T(8,128)S(1)} %collective-permute-done.9), channel_id=1, source_target_pairs={{0,1},{1,0},{2,3},{3,2},{4,5},{5,4},{6,7},{7,6},{8,9},{9,8},{10,11... | collective-permute-start | bytes 49160 | tf_op jit(solution)/shard_map/ppermute | solution.py:199
  25.0 4.2 %collective-permute-start.12 = (f32[32,128]{1,0:T(8,128)S(1)}, f32[32,128]{1,0:T(8,128)S(1)}, u32[]{:S(2)}, u32[]{:S(2)}) collective-permute-start(f32[32,128]{1,0:T(8,128)S(1)} %add_add_fusion.1), channel_id=1, source_target_pairs={{0,8},{1,25},{2,10},{3,27},{4,12},{5,29},{6,14},{7,31},{8,0},{9,17... | collective-permute-start | bytes 49160 | tf_op jit(solution)/shard_map/ppermute | solution.py:201
  26.6 4.9 %collective-permute-start.13 = (f32[32,128]{1,0:T(8,128)S(1)}, f32[32,128]{1,0:T(8,128)S(1)}, u32[]{:S(2)}, u32[]{:S(2)}) collective-permute-start(f32[32,128]{1,0:T(8,128)S(1)} %add_add_fusion.1), channel_id=1, source_target_pairs={{0,16},{8,24},{16,0},{24,8},{1,17},{9,25},{17,1},{25,9},{2,18},{10... | collective-permute-start | bytes 49160 | tf_op jit(solution)/shard_map/ppermute | solution.py:199
  29.2 2.3 %collective-permute-start.14 = (f32[32,128]{1,0:T(8,128)S(1)}, f32[32,128]{1,0:T(8,128)S(1)}, u32[]{:S(2)}, u32[]{:S(2)}) collective-permute-start(f32[32,128]{1,0:T(8,128)S(1)} %collective-permute-done.12), channel_id=1, source_target_pairs={{0,1},{1,0},{2,3},{3,2},{4,5},{5,4},{6,7},{7,6},{8,9},{9,8},{10,11... | collective-permute-start | bytes 49160 | tf_op jit(solution)/shard_map/ppermute | solution.py:199

commit v7 on v6

--- a/solution.py
+++ b/solution.py
@@ -226,6 +226,11 @@
     peers = lax.axis_size("dev")
     cap = fetch_list.shape[2]
     chips = peers // 2
+    lists = jnp.transpose(fetch_list, (0, 2, 1))
+    masks = [0] + [2 * i for i in reversed(range(1, chips))]
+    lists = [lists] + [swap(lists, "dev", 2 * i) for i in range(1, chips)]
+    sib_columns = swap(subspace, "dev", 1)
+
     first = pl.pallas_call(
         start_kernel,
         out_shape=jax.ShapeDtypeStruct((8, 128), F32),
@@ -234,11 +239,6 @@
         cost_estimate=pl.CostEstimate(flops=10**10, bytes_accessed=0, transcendentals=0),
         name="start",
     )()
-    first, lists = lax.optimization_barrier((first, jnp.transpose(fetch_list, (0, 2, 1))))
-    masks = [0] + [2 * i for i in reversed(range(1, chips))]
-    lists = [lists] + [swap(lists, "dev", 2 * i) for i in range(1, chips)]
-    sib_columns = swap(subspace, "dev", 1)
-
     inv_root = pl.pallas_call(
         degree_kernel,
         out_shape=jax.ShapeDtypeStruct((blocks, rows), F32),

time: 34.7 us -> 34.3 us (0.988)
  waiting for transfers between devices: 10.2 us -> 9.76 us
    ppermute x14, waiting for transfers between devices: 10.2 us -> 9.76 us  [swap(): lax.ppermute(x, axis, [(i, i ^ (odd if i % 2 else mask)) for i in range(s...]
where the time goes in v7:
time: 34.3 us; the launch traced here: 34.1 us
  starting transfers between devices  15.6 us (45%)
  waiting for transfers between devices  9.76 us (28%)
  Pallas kernels  8.53 us (25%)
    ppermute x14, starting transfers between devices, swap(): lax.ppermute(x, axis, [(i, i ^ (odd if i % 2 else mask)) for i in range(s...  14.1 us
    ppermute x14, waiting for transfers between devices, swap(): lax.ppermute(x, axis, [(i, i ^ (odd if i % 2 else mask)) for i in range(s...  9.76 us
    pallas_call x1, Pallas kernels, body(): pl.pallas_call(solve_kernel, out_shape=jax.ShapeDtypeStruct((k_dim, row_c...  3.03 us
    pallas_call x1, Pallas kernels, body(): pl.pallas_call(functools.partial(product_kernel, masks), out_shape=(jax.S...  2.83 us
    pallas_call x1, Pallas kernels, body(): pl.pallas_call(degree_kernel, out_shape=jax.ShapeDtypeStruct((blocks, row...  1.61 us
    ppermute x1, starting transfers between devices, swap(): return lax.ppermute(x, (axis, 'dev'), pairs)  1.59 us
    pallas_call x1, Pallas kernels, body(): pl.pallas_call(plan_kernel, out_shape=[pltpu.SMEM(x.shape, x.dtype) for x...  0.81 us
  transfers between devices with their start and end apart: 15, of which 10 were waited for; matrix products, arithmetic and copies ran while one was open for 0% of the time, Pallas kernels for 7%

profile of v7, /device:TPU:0, one launch (start us, length us, event | category | flops | bytes accessed | tf_op | source)
XLA Modules:
  0.0 34.1 jit_solution(11874850960068451445)
XLA Ops:
  0.0 0.0 slice-start
  0.0 0.0 slice-start.1
  0.0 0.0 copy-start.1
  0.0 4.0 %collective-permute-start.2 = (s32[1,2,8]{2,1,0:T(2,128)}, s32[1,2,8]{2,1,0:T(2,128)S(1)}, u32[]{:S(2)}, u32[]{:S(2)}) collective-permute-start(s32[1,2,8]{2,1,0:T(2,128)} %bitcast.5), channel_id=1, source_target_pairs={{0,6},{1,7},{2,4},{3,5},{4,2},{5,3},{6,0},{7,1},{8,14},{9,15},{10,... | collective-permute-start | bytes 200 | tf_op jit(solution)/shard_map/ppermute | solution.py:199
  4.0 0.5 %collective-permute-start.1 = (s32[1,2,8]{2,1,0:T(2,128)}, s32[1,2,8]{2,1,0:T(2,128)S(1)}, u32[]{:S(2)}, u32[]{:S(2)}) collective-permute-start(s32[1,2,8]{2,1,0:T(2,128)} %bitcast.6), channel_id=1, source_target_pairs={{0,4},{1,5},{2,6},{3,7},{4,0},{5,1},{6,2},{7,3},{8,12},{9,13},{10,... | collective-permute-start | bytes 200 | tf_op jit(solution)/shard_map/ppermute | solution.py:199
  4.5 0.1 collective-permute-start
  4.6 0.0 collective-permute-start.3
  4.6 0.0 copy-start.2
  4.6 0.0 copy-start
  4.6 0.0 slice-done
  4.6 0.0 slice-done.1
  4.6 0.0 copy-done.1
  4.7 1.6 %degree.1.inv_ref = f32[16,128]{1,0:T(8,128)S(1)} custom-call(f32[8,128]{1,0:T(8,128)S(1)} %start.1.first_ref, s32[1,16]{1,0:T(1,128)S(1)} %bitcast.4, bf16[16,16,128,128]{3,2,1,0:T(8,128)(2,1)S(1)} %bitcast.3), custom_call_target="tpu_custom_call" | custom-call | flops 67108864 | bytes 8388608 | tf_op jit(solution)/shard_map/degree/pallas_call | solution.py:242
  6.3 0.5 %collective-permute-start.4 = (f32[16,128]{1,0:T(8,128)S(1)}, f32[16,128]{1,0:T(8,128)S(1)}, u32[]{:S(2)}, u32[]{:S(2)}) collective-permute-start(f32[16,128]{1,0:T(8,128)S(1)} %degree.1.inv_ref), channel_id=1, source_target_pairs={{0,1},{1,0},{2,3},{3,2},{4,5},{5,4},{6,7},{7,6},{8,9},{9,8},{10,11... | collective-permute-start | bytes 24584 | tf_op jit(solution)/shard_map/ppermute | solution.py:199
  6.8 0.0 collective-permute-done.2.refs_3_
  6.8 0.9 %collective-permute-done.1.refs_2_ = s32[1,2,8]{2,1,0:T(2,128)S(1)} collective-permute-done((s32[1,2,8]{2,1,0:T(2,128)}, s32[1,2,8]{2,1,0:T(2,128)S(1)}, u32[]{:S(2)}, u32[]{:S(2)}) %collective-permute-start.1) | collective-permute-done | bytes 96 | tf_op jit(solution)/shard_map/ppermute | solution.py:199
  7.7 0.5 %collective-permute-done.refs_1_ = s32[1,2,8]{2,1,0:T(2,128)S(1)} collective-permute-done((s32[1,2,8]{2,1,0:T(2,128)}, s32[1,2,8]{2,1,0:T(2,128)S(1)}, u32[]{:S(2)}, u32[]{:S(2)}) %collective-permute-start) | collective-permute-done | bytes 96 | tf_op jit(solution)/shard_map/ppermute | solution.py:199
  8.3 0.0 copy-done.2
  8.3 0.0 collective-permute-done.4.sib_inv_ref
  8.3 0.0 collective-permute-done.3.sib_sub_ref
  8.3 0.0 copy-done
  8.3 0.2 select.1
  8.5 2.3 %collective-permute-start.5 = (bf16[2,2,64,128]{3,2,1,0:T(8,128)(2,1)S(1)}, bf16[2,2,64,128]{3,2,1,0:T(8,128)(2,1)S(1)}, u32[]{:S(2)}, u32[]{:S(2)}) collective-permute-start(bf16[2,2,64,128]{3,2,1,0:T(8,128)(2,1)S(1)} %get-tuple-element.16), channel_id=1, source_target_pairs={{0,6},{1,7},{2,4},{3,5},{4,2},{5,3},{6,0},{7,1},{8,14},{9,15},{10,... | collective-permute-start | bytes 196616 | tf_op jit(solution)/shard_map/ppermute | solution.py:199
  10.8 0.5 %collective-permute-start.6 = (bf16[2,2,64,128]{3,2,1,0:T(8,128)(2,1)S(1)}, bf16[2,2,64,128]{3,2,1,0:T(8,128)(2,1)S(1)}, u32[]{:S(2)}, u32[]{:S(2)}) collective-permute-start(bf16[2,2,64,128]{3,2,1,0:T(8,128)(2,1)S(1)} %get-tuple-element.17), channel_id=1, source_target_pairs={{0,4},{1,5},{2,6},{3,7},{4,0},{5,1},{6,2},{7,3},{8,12},{9,13},{10,... | collective-permute-start | bytes 196616 | tf_op jit(solution)/shard_map/ppermute | solution.py:199
  11.3 0.8 %collective-permute-start.7 = (bf16[2,2,64,128]{3,2,1,0:T(8,128)(2,1)S(1)}, bf16[2,2,64,128]{3,2,1,0:T(8,128)(2,1)S(1)}, u32[]{:S(2)}, u32[]{:S(2)}) collective-permute-start(bf16[2,2,64,128]{3,2,1,0:T(8,128)(2,1)S(1)} %get-tuple-element.18), channel_id=1, source_target_pairs={{0,2},{1,3},{2,0},{3,1},{4,6},{5,7},{6,4},{7,5},{8,10},{9,11},{10,... | collective-permute-start | bytes 196616 | tf_op jit(solution)/shard_map/ppermute | solution.py:199
  12.1 0.8 %plan.1 = (s32[16]{0:T(128)S(4)}, s32[16,16]{1,0:T(8,128)S(4)}) custom-call(s32[16]{0:T(128)} %count_hbm.1, s32[16,16]{1,0:T(8,128)} %slot_hbm.1), custom_call_target="tpu_custom_call" | custom-call | flops 2000000000 | tf_op jit(solution)/shard_map/plan/pallas_call | solution.py:273
  12.9 0.9 %collective-permute-done.5.refs_1_ = bf16[2,2,64,128]{3,2,1,0:T(8,128)(2,1)S(1)} collective-permute-done((bf16[2,2,64,128]{3,2,1,0:T(8,128)(2,1)S(1)}, bf16[2,2,64,128]{3,2,1,0:T(8,128)(2,1)S(1)}, u32[]{:S(2)}, u32[]{:S(2)}) %collective-permute-start.5) | collective-permute-done | bytes 65568 | tf_op jit(solution)/shard_map/ppermute | solution.py:199
  13.8 1.4 %collective-permute-done.6.refs_2_ = bf16[2,2,64,128]{3,2,1,0:T(8,128)(2,1)S(1)} collective-permute-done((bf16[2,2,64,128]{3,2,1,0:T(8,128)(2,1)S(1)}, bf16[2,2,64,128]{3,2,1,0:T(8,128)(2,1)S(1)}, u32[]{:S(2)}, u32[]{:S(2)}) %collective-permute-start.6) | collective-permute-done | bytes 65568 | tf_op jit(solution)/shard_map/ppermute | solution.py:199
  15.2 0.4 %collective-permute-done.7.refs_3_ = bf16[2,2,64,128]{3,2,1,0:T(8,128)(2,1)S(1)} collective-permute-done((bf16[2,2,64,128]{3,2,1,0:T(8,128)(2,1)S(1)}, bf16[2,2,64,128]{3,2,1,0:T(8,128)(2,1)S(1)}, u32[]{:S(2)}, u32[]{:S(2)}) %collective-permute-start.7) | collective-permute-done | bytes 65568 | tf_op jit(solution)/shard_map/ppermute | solution.py:199
  15.6 2.8 %product.1 = (bf16[128,2048]{1,0:T(8,128)(2,1)S(1)}, f32[32,128]{1,0:T(8,128)S(1)}) custom-call(s32[16]{0:T(128)S(4)} %get-tuple-element.13.count_ref, s32[16,16]{1,0:T(8,128)S(4)} %get-tuple-element.14.slot_ref, f32[16,128]{1,0:T(8,128)S(1)} %degree.1.inv_ref, bf16[16,16,128,128]{3,2,1,0:T(8,128)(2,1)S(1)} %bitcast.3, ...), custom_call_target="tpu_custom_call" | custom-call | flops 536870912 | bytes 8388608 | tf_op jit(solution)/shard_map/product/pallas_call | solution.py:285
  18.4 0.0 collective-permute-start.8
  18.4 1.2 %collective-permute-done.8 = f32[32,128]{1,0:T(8,128)S(1)} collective-permute-done((f32[32,128]{1,0:T(8,128)S(1)}, f32[32,128]{1,0:T(8,128)S(1)}, u32[]{:S(2)}, u32[]{:S(2)}) %collective-permute-start.8) | collective-permute-done | bytes 16416 | tf_op jit(solution)/shard_map/ppermute | solution.py:199
  19.6 1.0 %collective-permute-start.9 = (f32[32,128]{1,0:T(8,128)S(1)}, f32[32,128]{1,0:T(8,128)S(1)}, u32[]{:S(2)}, u32[]{:S(2)}) collective-permute-start(f32[32,128]{1,0:T(8,128)S(1)} %add.21), channel_id=1, source_target_pairs={{0,2},{1,7},{2,0},{3,5},{4,6},{5,3},{6,4},{7,1},{8,10},{9,15},{10,... | collective-permute-start | bytes 49160 | tf_op jit(solution)/shard_map/ppermute | solution.py:199
  20.6 1.3 %collective-permute-start.10 = (f32[32,128]{1,0:T(8,128)S(1)}, f32[32,128]{1,0:T(8,128)S(1)}, u32[]{:S(2)}, u32[]{:S(2)}) collective-permute-start(f32[32,128]{1,0:T(8,128)S(1)} %add.21), channel_id=1, source_target_pairs={{0,4},{1,5},{2,6},{3,7},{4,0},{5,1},{6,2},{7,3},{8,12},{9,13},{10,... | collective-permute-start | bytes 49160 | tf_op jit(solution)/shard_map/ppermute | solution.py:199
  21.9 1.5 %collective-permute-done.9 = f32[32,128]{1,0:T(8,128)S(1)} collective-permute-done((f32[32,128]{1,0:T(8,128)S(1)}, f32[32,128]{1,0:T(8,128)S(1)}, u32[]{:S(2)}, u32[]{:S(2)}) %collective-permute-start.9) | collective-permute-done | bytes 16416 | tf_op jit(solution)/shard_map/ppermute | solution.py:199
  23.4 0.0 collective-permute-start.11
  23.4 1.0 %collective-permute-done.10 = f32[32,128]{1,0:T(8,128)S(1)} collective-permute-done((f32[32,128]{1,0:T(8,128)S(1)}, f32[32,128]{1,0:T(8,128)S(1)}, u32[]{:S(2)}, u32[]{:S(2)}) %collective-permute-start.10) | collective-permute-done | bytes 16416 | tf_op jit(solution)/shard_map/ppermute | solution.py:199
  24.3 0.2 collective-permute-done.11
  24.6 1.6 %collective-permute-start.12 = (f32[32,128]{1,0:T(8,128)S(1)}, f32[32,128]{1,0:T(8,128)S(1)}, u32[]{:S(2)}, u32[]{:S(2)}) collective-permute-start(f32[32,128]{1,0:T(8,128)S(1)} %add_add_fusion.1), channel_id=1, source_target_pairs={{0,8},{1,25},{2,10},{3,27},{4,12},{5,29},{6,14},{7,31},{8,0},{9,17... | collective-permute-start | bytes 49160 | tf_op jit(solution)/shard_map/ppermute | solution.py:201
  26.2 2.6 %collective-permute-start.13 = (f32[32,128]{1,0:T(8,128)S(1)}, f32[32,128]{1,0:T(8,128)S(1)}, u32[]{:S(2)}, u32[]{:S(2)}) collective-permute-start(f32[32,128]{1,0:T(8,128)S(1)} %add_add_fusion.1), channel_id=1, source_target_pairs={{0,16},{8,24},{16,0},{24,8},{1,17},{9,25},{17,1},{25,9},{2,18},{10... | collective-permute-start | bytes 49160 | tf_op jit(solution)/shard_map/ppermute | solution.py:199
  28.7 0.0 collective-permute-done.12
  28.7 0.4 %collective-permute-start.14 = (f32[32,128]{1,0:T(8,128)S(1)}, f32[32,128]{1,0:T(8,128)S(1)}, u32[]{:S(2)}, u32[]{:S(2)}) collective-permute-start(f32[32,128]{1,0:T(8,128)S(1)} %collective-permute-done.12), channel_id=1, source_target_pairs={{0,1},{1,0},{2,3},{3,2},{4,5},{5,4},{6,7},{7,6},{8,9},{9,8},{10,11... | collective-permute-start | bytes 49160 | tf_op jit(solution)/shard_map/ppermute | solution.py:199
  29.2 1.8 %collective-permute-done.13 = f32[32,128]{1,0:T(8,128)S(1)} collective-permute-done((f32[32,128]{1,0:T(8,128)S(1)}, f32[32,128]{1,0:T(8,128)S(1)}, u32[]{:S(2)}, u32[]{:S(2)}) %collective-permute-start.13) | collective-permute-done | bytes 16416 | tf_op jit(solution)/shard_map/ppermute | solution.py:199
  31.0 0.0 collective-permute-done.14
  31.0 3.0 %solve.1 = f32[64,2048]{1,0:T(8,128)} custom-call(f32[32,128]{1,0:T(8,128)S(1)} %add_add_fusion.gram_ref, bf16[128,2048]{1,0:T(8,128)(2,1)S(1)} %get-tuple-element.20.applied_ref), custom_call_target="tpu_custom_call" | custom-call | tf_op jit(solution)/shard_map/solve/pallas_call | solution.py:303
  (6 shorter events, 0.0 us)
Async XLA Ops:
  0.0 4.6 %slice-start = ((s8[8388608]{0:T(1024)(128)(4,1)}), s8[4194304]{0:T(1024)(128)(4,1)S(1)}, s32[]{:S(2)}) async-start(s8[8388608]{0:T(1024)(128)(4,1)} %bitcast.2), calls=%async_computation | async-start | bytes 8388608
  0.0 4.6 %slice-start.1 = ((s8[8388608]{0:T(1024)(128)(4,1)}), s8[4194304]{0:T(1024)(128)(4,1)S(1)}, s32[]{:S(2)}) async-start(s8[8388608]{0:T(1024)(128)(4,1)} %bitcast.2), calls=%async_computation.1 | async-start | bytes 8388608
  0.0 4.6 %copy-start.1 = (s32[16]{0:T(128)S(1)}, s32[16]{0:T(128)}, u32[]{:S(2)}) copy-start(s32[16]{0:T(128)} %count_hbm.1) | copy-start | bytes 196
  0.0 6.8 %collective-permute-start.2 = (s32[1,2,8]{2,1,0:T(2,128)}, s32[1,2,8]{2,1,0:T(2,128)S(1)}, u32[]{:S(2)}, u32[]{:S(2)}) collective-permute-start(s32[1,2,8]{2,1,0:T(2,128)} %bitcast.5), channel_id=1, source_target_pairs={{0,6},{1,7},{2,4},{3,5},{4,2},{5,3},{6,0},{7,1},{8,14},{9,15},{10,... | collective-permute-start | bytes 200 | tf_op jit(solution)/shard_map/ppermute | solution.py:199
  4.0 3.8 %collective-permute-start.1 = (s32[1,2,8]{2,1,0:T(2,128)}, s32[1,2,8]{2,1,0:T(2,128)S(1)}, u32[]{:S(2)}, u32[]{:S(2)}) collective-permute-start(s32[1,2,8]{2,1,0:T(2,128)} %bitcast.6), channel_id=1, source_target_pairs={{0,4},{1,5},{2,6},{3,7},{4,0},{5,1},{6,2},{7,3},{8,12},{9,13},{10,... | collective-permute-start | bytes 200 | tf_op jit(solution)/shard_map/ppermute | solution.py:199
  4.5 3.8 %collective-permute-start = (s32[1,2,8]{2,1,0:T(2,128)}, s32[1,2,8]{2,1,0:T(2,128)S(1)}, u32[]{:S(2)}, u32[]{:S(2)}) collective-permute-start(s32[1,2,8]{2,1,0:T(2,128)} %bitcast.7), channel_id=1, source_target_pairs={{0,2},{1,3},{2,0},{3,1},{4,6},{5,7},{6,4},{7,5},{8,10},{9,11},{10,... | collective-permute-start | bytes 200 | tf_op jit(solution)/shard_map/ppermute | solution.py:199
  4.6 3.7 %collective-permute-start.3 = (bf16[64,2048]{1,0:T(8,128)(2,1)}, bf16[64,2048]{1,0:T(8,128)(2,1)S(1)}, u32[]{:S(2)}, u32[]{:S(2)}) collective-permute-start(bf16[64,2048]{1,0:T(8,128)(2,1)} %sub_ref.1), channel_id=1, source_target_pairs={{0,1},{1,0},{2,3},{3,2},{4,5},{5,4},{6,7},{7,6},{8,9},{9,8},{10,11... | collective-permute-start | bytes 786440 | tf_op jit(solution)/shard_map/ppermute | solution.py:199
  4.6 3.6 %copy-start.2 = (s32[1,8,2]{1,2,0:T(2,128)S(1)}, s32[1,8,2]{1,2,0:T(2,128)}, u32[]{:S(2)}) copy-start(s32[1,8,2]{1,2,0:T(2,128)} %param.9) | copy-start | bytes 196
  4.6 3.7 %copy-start = (bf16[64,2048]{1,0:T(8,128)(2,1)S(1)}, bf16[64,2048]{1,0:T(8,128)(2,1)}, u32[]{:S(2)}) copy-start(bf16[64,2048]{1,0:T(8,128)(2,1)} %sub_ref.1) | copy-start | bytes 786436
  6.3 2.0 %collective-permute-start.4 = (f32[16,128]{1,0:T(8,128)S(1)}, f32[16,128]{1,0:T(8,128)S(1)}, u32[]{:S(2)}, u32[]{:S(2)}) collective-permute-start(f32[16,128]{1,0:T(8,128)S(1)} %degree.1.inv_ref), channel_id=1, source_target_pairs={{0,1},{1,0},{2,3},{3,2},{4,5},{5,4},{6,7},{7,6},{8,9},{9,8},{10,11... | collective-permute-start | bytes 24584 | tf_op jit(solution)/shard_map/ppermute | solution.py:199
  8.5 5.3 %collective-permute-start.5 = (bf16[2,2,64,128]{3,2,1,0:T(8,128)(2,1)S(1)}, bf16[2,2,64,128]{3,2,1,0:T(8,128)(2,1)S(1)}, u32[]{:S(2)}, u32[]{:S(2)}) collective-permute-start(bf16[2,2,64,128]{3,2,1,0:T(8,128)(2,1)S(1)} %get-tuple-element.16), channel_id=1, source_target_pairs={{0,6},{1,7},{2,4},{3,5},{4,2},{5,3},{6,0},{7,1},{8,14},{9,15},{10,... | collective-permute-start | bytes 196616 | tf_op jit(solution)/shard_map/ppermute | solution.py:199
  10.8 4.4 %collective-permute-start.6 = (bf16[2,2,64,128]{3,2,1,0:T(8,128)(2,1)S(1)}, bf16[2,2,64,128]{3,2,1,0:T(8,128)(2,1)S(1)}, u32[]{:S(2)}, u32[]{:S(2)}) collective-permute-start(bf16[2,2,64,128]{3,2,1,0:T(8,128)(2,1)S(1)} %get-tuple-element.17), channel_id=1, source_target_pairs={{0,4},{1,5},{2,6},{3,7},{4,0},{5,1},{6,2},{7,3},{8,12},{9,13},{10,... | collective-permute-start | bytes 196616 | tf_op jit(solution)/shard_map/ppermute | solution.py:199
  11.3 4.3 %collective-permute-start.7 = (bf16[2,2,64,128]{3,2,1,0:T(8,128)(2,1)S(1)}, bf16[2,2,64,128]{3,2,1,0:T(8,128)(2,1)S(1)}, u32[]{:S(2)}, u32[]{:S(2)}) collective-permute-start(bf16[2,2,64,128]{3,2,1,0:T(8,128)(2,1)S(1)} %get-tuple-element.18), channel_id=1, source_target_pairs={{0,2},{1,3},{2,0},{3,1},{4,6},{5,7},{6,4},{7,5},{8,10},{9,11},{10,... | collective-permute-start | bytes 196616 | tf_op jit(solution)/shard_map/ppermute | solution.py:199
  18.4 1.2 %collective-permute-start.8 = (f32[32,128]{1,0:T(8,128)S(1)}, f32[32,128]{1,0:T(8,128)S(1)}, u32[]{:S(2)}, u32[]{:S(2)}) collective-permute-start(f32[32,128]{1,0:T(8,128)S(1)} %get-tuple-element.19), channel_id=1, source_target_pairs={{0,1},{1,0},{2,3},{3,2},{4,5},{5,4},{6,7},{7,6},{8,9},{9,8},{10,11... | collective-permute-start | bytes 49160 | tf_op jit(solution)/shard_map/ppermute | solution.py:199
  19.6 3.8 %collective-permute-start.9 = (f32[32,128]{1,0:T(8,128)S(1)}, f32[32,128]{1,0:T(8,128)S(1)}, u32[]{:S(2)}, u32[]{:S(2)}) collective-permute-start(f32[32,128]{1,0:T(8,128)S(1)} %add.21), channel_id=1, source_target_pairs={{0,2},{1,7},{2,0},{3,5},{4,6},{5,3},{6,4},{7,1},{8,10},{9,15},{10,... | collective-permute-start | bytes 49160 | tf_op jit(solution)/shard_map/ppermute | solution.py:199
  20.6 3.7 %collective-permute-start.10 = (f32[32,128]{1,0:T(8,128)S(1)}, f32[32,128]{1,0:T(8,128)S(1)}, u32[]{:S(2)}, u32[]{:S(2)}) collective-permute-start(f32[32,128]{1,0:T(8,128)S(1)} %add.21), channel_id=1, source_target_pairs={{0,4},{1,5},{2,6},{3,7},{4,0},{5,1},{6,2},{7,3},{8,12},{9,13},{10,... | collective-permute-start | bytes 49160 | tf_op jit(solution)/shard_map/ppermute | solution.py:199
  23.4 1.2 %collective-permute-start.11 = (f32[32,128]{1,0:T(8,128)S(1)}, f32[32,128]{1,0:T(8,128)S(1)}, u32[]{:S(2)}, u32[]{:S(2)}) collective-permute-start(f32[32,128]{1,0:T(8,128)S(1)} %collective-permute-done.9), channel_id=1, source_target_pairs={{0,1},{1,0},{2,3},{3,2},{4,5},{5,4},{6,7},{7,6},{8,9},{9,8},{10,11... | collective-permute-start | bytes 49160 | tf_op jit(solution)/shard_map/ppermute | solution.py:199
  24.6 4.2 %collective-permute-start.12 = (f32[32,128]{1,0:T(8,128)S(1)}, f32[32,128]{1,0:T(8,128)S(1)}, u32[]{:S(2)}, u32[]{:S(2)}) collective-permute-start(f32[32,128]{1,0:T(8,128)S(1)} %add_add_fusion.1), channel_id=1, source_target_pairs={{0,8},{1,25},{2,10},{3,27},{4,12},{5,29},{6,14},{7,31},{8,0},{9,17... | collective-permute-start | bytes 49160 | tf_op jit(solution)/shard_map/ppermute | solution.py:201
  26.2 4.9 %collective-permute-start.13 = (f32[32,128]{1,0:T(8,128)S(1)}, f32[32,128]{1,0:T(8,128)S(1)}, u32[]{:S(2)}, u32[]{:S(2)}) collective-permute-start(f32[32,128]{1,0:T(8,128)S(1)} %add_add_fusion.1), channel_id=1, source_target_pairs={{0,16},{8,24},{16,0},{24,8},{1,17},{9,25},{17,1},{25,9},{2,18},{10... | collective-permute-start | bytes 49160 | tf_op jit(solution)/shard_map/ppermute | solution.py:199
  28.7 2.3 %collective-permute-start.14 = (f32[32,128]{1,0:T(8,128)S(1)}, f32[32,128]{1,0:T(8,128)S(1)}, u32[]{:S(2)}, u32[]{:S(2)}) collective-permute-start(f32[32,128]{1,0:T(8,128)S(1)} %collective-permute-done.12), channel_id=1, source_target_pairs={{0,1},{1,0},{2,3},{3,2},{4,5},{5,4},{6,7},{7,6},{8,9},{9,8},{10,11... | collective-permute-start | bytes 49160 | tf_op jit(solution)/shard_map/ppermute | solution.py:199

commit v8 on v7

--- a/solution.py
+++ b/solution.py
@@ -8,6 +8,7 @@
 from jax.sharding import PartitionSpec as P
 
 GROUP = 4
+SOLVE_PARTS = 4
 VMEM = pl.BlockSpec(memory_space=pltpu.VMEM)
 HBM = pl.BlockSpec(memory_space=pltpu.HBM)
 SMEM = pl.BlockSpec(memory_space=pltpu.SMEM)
@@ -145,7 +146,6 @@
     def spread(x):
         return jnp.broadcast_to(x, (8, wide))
 
-    done = []
     for g in range(groups):
         column = {
             (i, b): spread(rows[i][:, 8 * g + b : 8 * g + b + 1])
@@ -175,20 +175,30 @@
                 rows[i] = rows[i] - f0 * row0 - f1 * row1
                 for b in range(s + 2, 8):
                     column[i, b] = column[i, b] - f0 * pivot0[b] - f1 * pivot1[b]
-        done.append(out)
-    return jnp.concatenate(done, axis=0)[:, k_dim:]
-
-
-def solve_kernel(gram_ref, applied_ref, out_ref):
+        yield out[:, k_dim:]
+
+
+def solve_kernel(gram_ref, applied_ref, out_hbm, out_ref, sems):
     k_dim = gram_ref.shape[1] // 2
+    parts = sems.shape[0]
     packed = gram_ref[...]
     gram = jnp.concatenate([packed[:, :k_dim], packed[:, k_dim:]], axis=0)
-    high, low = split(inverse_factor(gram))
-    out_ref[...] = jnp.dot(
-        jnp.concatenate([high, high, low], axis=1),
-        jnp.concatenate([applied_ref[...], applied_ref[:k_dim]], axis=0),
-        preferred_element_type=F32,
-    )
+    applied = jnp.concatenate([applied_ref[...], applied_ref[:k_dim]], axis=0)
+    done, copies = [], []
+    for rows in inverse_factor(gram):
+        done.append(rows)
+        if len(done) * 8 * parts < k_dim:
+            continue
+        high, low = split(jnp.concatenate(done, axis=0))
+        part = pl.ds(len(copies) * 8 * len(done), 8 * len(done))
+        out_ref[part] = jnp.dot(
+            jnp.concatenate([high, high, low], axis=1), applied, preferred_element_type=F32
+        )
+        copies.append(pltpu.make_async_copy(out_ref.at[part], out_hbm.at[part], sems.at[len(copies)]))
+        copies[-1].start()
+        done = []
+    for copy in copies:
+        copy.wait()
 
 
 def swap(x, axis, mask, odd_mask=None):
@@ -304,7 +314,11 @@
         solve_kernel,
         out_shape=jax.ShapeDtypeStruct((k_dim, row_count), F32),
         in_specs=[VMEM] * 2,
-        out_specs=VMEM,
+        out_specs=HBM,
+        scratch_shapes=[
+            pltpu.VMEM((k_dim, row_count), F32),
+            pltpu.SemaphoreType.DMA((SOLVE_PARTS,)),
+        ],
         compiler_params=limit(4),
         name="solve",
     )(gram, applied)

time: 34.3 us -> 34.2 us (level)
  no operation moved by 1% of the time
where the time goes in v8:
time: 34.2 us; the launch traced here: 34 us
  starting transfers between devices  15.6 us (46%)
  waiting for transfers between devices  9.76 us (29%)
  Pallas kernels  8.43 us (25%)
    ppermute x14, starting transfers between devices, swap(): lax.ppermute(x, axis, [(i, i ^ (odd if i % 2 else mask)) for i in range(s...  14.1 us
    ppermute x14, waiting for transfers between devices, swap(): lax.ppermute(x, axis, [(i, i ^ (odd if i % 2 else mask)) for i in range(s...  9.75 us
    pallas_call x1, Pallas kernels, body(): pl.pallas_call(solve_kernel, out_shape=jax.ShapeDtypeStruct((k_dim, row_c...  2.93 us
    pallas_call x1, Pallas kernels, body(): pl.pallas_call(functools.partial(product_kernel, masks), out_shape=(jax.S...  2.83 us
    pallas_call x1, Pallas kernels, body(): pl.pallas_call(degree_kernel, out_shape=jax.ShapeDtypeStruct((blocks, row...  1.61 us
    ppermute x1, starting transfers between devices, swap(): return lax.ppermute(x, (axis, 'dev'), pairs)  1.59 us
    pallas_call x1, Pallas kernels, body(): pl.pallas_call(plan_kernel, out_shape=[pltpu.SMEM(x.shape, x.dtype) for x...  0.81 us
  transfers between devices with their start and end apart: 15, of which 10 were waited for; matrix products, arithmetic and copies ran while one was open for 0% of the time, Pallas kernels for 7%

profile of v8, /device:TPU:0, one launch (start us, length us, event | category | flops | bytes accessed | tf_op | source)
XLA Modules:
  0.0 34.0 jit_solution(1637630299461365053)
XLA Ops:
  0.0 0.0 slice-start
  0.0 0.0 slice-start.1
  0.0 0.0 copy-start.1
  0.0 4.0 %collective-permute-start.2 = (s32[1,2,8]{2,1,0:T(2,128)}, s32[1,2,8]{2,1,0:T(2,128)S(1)}, u32[]{:S(2)}, u32[]{:S(2)}) collective-permute-start(s32[1,2,8]{2,1,0:T(2,128)} %bitcast.5), channel_id=1, source_target_pairs={{0,6},{1,7},{2,4},{3,5},{4,2},{5,3},{6,0},{7,1},{8,14},{9,15},{10,... | collective-permute-start | bytes 200 | tf_op jit(solution)/shard_map/ppermute | solution.py:209
  4.0 0.5 %collective-permute-start.1 = (s32[1,2,8]{2,1,0:T(2,128)}, s32[1,2,8]{2,1,0:T(2,128)S(1)}, u32[]{:S(2)}, u32[]{:S(2)}) collective-permute-start(s32[1,2,8]{2,1,0:T(2,128)} %bitcast.6), channel_id=1, source_target_pairs={{0,4},{1,5},{2,6},{3,7},{4,0},{5,1},{6,2},{7,3},{8,12},{9,13},{10,... | collective-permute-start | bytes 200 | tf_op jit(solution)/shard_map/ppermute | solution.py:209
  4.5 0.1 collective-permute-start
  4.6 0.0 collective-permute-start.3
  4.6 0.0 copy-start.2
  4.6 0.0 copy-start
  4.6 0.0 slice-done
  4.6 0.0 slice-done.1
  4.6 0.0 copy-done.1
  4.7 1.6 %degree.1.inv_ref = f32[16,128]{1,0:T(8,128)S(1)} custom-call(f32[8,128]{1,0:T(8,128)S(1)} %start.1.first_ref, s32[1,16]{1,0:T(1,128)S(1)} %bitcast.4, bf16[16,16,128,128]{3,2,1,0:T(8,128)(2,1)S(1)} %bitcast.3), custom_call_target="tpu_custom_call" | custom-call | flops 67108864 | bytes 8388608 | tf_op jit(solution)/shard_map/degree/pallas_call | solution.py:252
  6.3 0.5 %collective-permute-start.4 = (f32[16,128]{1,0:T(8,128)S(1)}, f32[16,128]{1,0:T(8,128)S(1)}, u32[]{:S(2)}, u32[]{:S(2)}) collective-permute-start(f32[16,128]{1,0:T(8,128)S(1)} %degree.1.inv_ref), channel_id=1, source_target_pairs={{0,1},{1,0},{2,3},{3,2},{4,5},{5,4},{6,7},{7,6},{8,9},{9,8},{10,11... | collective-permute-start | bytes 24584 | tf_op jit(solution)/shard_map/ppermute | solution.py:209
  6.8 0.0 collective-permute-done.2.refs_3_
  6.8 0.9 %collective-permute-done.1.refs_2_ = s32[1,2,8]{2,1,0:T(2,128)S(1)} collective-permute-done((s32[1,2,8]{2,1,0:T(2,128)}, s32[1,2,8]{2,1,0:T(2,128)S(1)}, u32[]{:S(2)}, u32[]{:S(2)}) %collective-permute-start.1) | collective-permute-done | bytes 96 | tf_op jit(solution)/shard_map/ppermute | solution.py:209
  7.7 0.5 %collective-permute-done.refs_1_ = s32[1,2,8]{2,1,0:T(2,128)S(1)} collective-permute-done((s32[1,2,8]{2,1,0:T(2,128)}, s32[1,2,8]{2,1,0:T(2,128)S(1)}, u32[]{:S(2)}, u32[]{:S(2)}) %collective-permute-start) | collective-permute-done | bytes 96 | tf_op jit(solution)/shard_map/ppermute | solution.py:209
  8.3 0.0 copy-done.2
  8.3 0.0 collective-permute-done.4.sib_inv_ref
  8.3 0.0 collective-permute-done.3.sib_sub_ref
  8.3 0.0 copy-done
  8.3 0.2 select.1
  8.5 2.3 %collective-permute-start.5 = (bf16[2,2,64,128]{3,2,1,0:T(8,128)(2,1)S(1)}, bf16[2,2,64,128]{3,2,1,0:T(8,128)(2,1)S(1)}, u32[]{:S(2)}, u32[]{:S(2)}) collective-permute-start(bf16[2,2,64,128]{3,2,1,0:T(8,128)(2,1)S(1)} %get-tuple-element.16), channel_id=1, source_target_pairs={{0,6},{1,7},{2,4},{3,5},{4,2},{5,3},{6,0},{7,1},{8,14},{9,15},{10,... | collective-permute-start | bytes 196616 | tf_op jit(solution)/shard_map/ppermute | solution.py:209
  10.8 0.5 %collective-permute-start.6 = (bf16[2,2,64,128]{3,2,1,0:T(8,128)(2,1)S(1)}, bf16[2,2,64,128]{3,2,1,0:T(8,128)(2,1)S(1)}, u32[]{:S(2)}, u32[]{:S(2)}) collective-permute-start(bf16[2,2,64,128]{3,2,1,0:T(8,128)(2,1)S(1)} %get-tuple-element.17), channel_id=1, source_target_pairs={{0,4},{1,5},{2,6},{3,7},{4,0},{5,1},{6,2},{7,3},{8,12},{9,13},{10,... | collective-permute-start | bytes 196616 | tf_op jit(solution)/shard_map/ppermute | solution.py:209
  11.3 0.8 %collective-permute-start.7 = (bf16[2,2,64,128]{3,2,1,0:T(8,128)(2,1)S(1)}, bf16[2,2,64,128]{3,2,1,0:T(8,128)(2,1)S(1)}, u32[]{:S(2)}, u32[]{:S(2)}) collective-permute-start(bf16[2,2,64,128]{3,2,1,0:T(8,128)(2,1)S(1)} %get-tuple-element.18), channel_id=1, source_target_pairs={{0,2},{1,3},{2,0},{3,1},{4,6},{5,7},{6,4},{7,5},{8,10},{9,11},{10,... | collective-permute-start | bytes 196616 | tf_op jit(solution)/shard_map/ppermute | solution.py:209
  12.1 0.8 %plan.1 = (s32[16]{0:T(128)S(4)}, s32[16,16]{1,0:T(8,128)S(4)}) custom-call(s32[16]{0:T(128)} %count_hbm.1, s32[16,16]{1,0:T(8,128)} %slot_hbm.1), custom_call_target="tpu_custom_call" | custom-call | flops 2000000000 | tf_op jit(solution)/shard_map/plan/pallas_call | solution.py:283
  12.9 0.9 %collective-permute-done.5.refs_1_ = bf16[2,2,64,128]{3,2,1,0:T(8,128)(2,1)S(1)} collective-permute-done((bf16[2,2,64,128]{3,2,1,0:T(8,128)(2,1)S(1)}, bf16[2,2,64,128]{3,2,1,0:T(8,128)(2,1)S(1)}, u32[]{:S(2)}, u32[]{:S(2)}) %collective-permute-start.5) | collective-permute-done | bytes 65568 | tf_op jit(solution)/shard_map/ppermute | solution.py:209
  13.8 1.4 %collective-permute-done.6.refs_2_ = bf16[2,2,64,128]{3,2,1,0:T(8,128)(2,1)S(1)} collective-permute-done((bf16[2,2,64,128]{3,2,1,0:T(8,128)(2,1)S(1)}, bf16[2,2,64,128]{3,2,1,0:T(8,128)(2,1)S(1)}, u32[]{:S(2)}, u32[]{:S(2)}) %collective-permute-start.6) | collective-permute-done | bytes 65568 | tf_op jit(solution)/shard_map/ppermute | solution.py:209
  15.2 0.4 %collective-permute-done.7.refs_3_ = bf16[2,2,64,128]{3,2,1,0:T(8,128)(2,1)S(1)} collective-permute-done((bf16[2,2,64,128]{3,2,1,0:T(8,128)(2,1)S(1)}, bf16[2,2,64,128]{3,2,1,0:T(8,128)(2,1)S(1)}, u32[]{:S(2)}, u32[]{:S(2)}) %collective-permute-start.7) | collective-permute-done | bytes 65568 | tf_op jit(solution)/shard_map/ppermute | solution.py:209
  15.6 2.8 %product.1 = (bf16[128,2048]{1,0:T(8,128)(2,1)S(1)}, f32[32,128]{1,0:T(8,128)S(1)}) custom-call(s32[16]{0:T(128)S(4)} %get-tuple-element.13.count_ref, s32[16,16]{1,0:T(8,128)S(4)} %get-tuple-element.14.slot_ref, f32[16,128]{1,0:T(8,128)S(1)} %degree.1.inv_ref, bf16[16,16,128,128]{3,2,1,0:T(8,128)(2,1)S(1)} %bitcast.3, ...), custom_call_target="tpu_custom_call" | custom-call | flops 536870912 | bytes 8388608 | tf_op jit(solution)/shard_map/product/pallas_call | solution.py:295
  18.4 0.0 collective-permute-start.8
  18.4 1.2 %collective-permute-done.8 = f32[32,128]{1,0:T(8,128)S(1)} collective-permute-done((f32[32,128]{1,0:T(8,128)S(1)}, f32[32,128]{1,0:T(8,128)S(1)}, u32[]{:S(2)}, u32[]{:S(2)}) %collective-permute-start.8) | collective-permute-done | bytes 16416 | tf_op jit(solution)/shard_map/ppermute | solution.py:209
  19.6 1.0 %collective-permute-start.9 = (f32[32,128]{1,0:T(8,128)S(1)}, f32[32,128]{1,0:T(8,128)S(1)}, u32[]{:S(2)}, u32[]{:S(2)}) collective-permute-start(f32[32,128]{1,0:T(8,128)S(1)} %add.21), channel_id=1, source_target_pairs={{0,2},{1,7},{2,0},{3,5},{4,6},{5,3},{6,4},{7,1},{8,10},{9,15},{10,... | collective-permute-start | bytes 49160 | tf_op jit(solution)/shard_map/ppermute | solution.py:209
  20.6 1.3 %collective-permute-start.10 = (f32[32,128]{1,0:T(8,128)S(1)}, f32[32,128]{1,0:T(8,128)S(1)}, u32[]{:S(2)}, u32[]{:S(2)}) collective-permute-start(f32[32,128]{1,0:T(8,128)S(1)} %add.21), channel_id=1, source_target_pairs={{0,4},{1,5},{2,6},{3,7},{4,0},{5,1},{6,2},{7,3},{8,12},{9,13},{10,... | collective-permute-start | bytes 49160 | tf_op jit(solution)/shard_map/ppermute | solution.py:209
  21.9 1.5 %collective-permute-done.9 = f32[32,128]{1,0:T(8,128)S(1)} collective-permute-done((f32[32,128]{1,0:T(8,128)S(1)}, f32[32,128]{1,0:T(8,128)S(1)}, u32[]{:S(2)}, u32[]{:S(2)}) %collective-permute-start.9) | collective-permute-done | bytes 16416 | tf_op jit(solution)/shard_map/ppermute | solution.py:209
  23.4 0.0 collective-permute-start.11
  23.4 0.9 %collective-permute-done.10 = f32[32,128]{1,0:T(8,128)S(1)} collective-permute-done((f32[32,128]{1,0:T(8,128)S(1)}, f32[32,128]{1,0:T(8,128)S(1)}, u32[]{:S(2)}, u32[]{:S(2)}) %collective-permute-start.10) | collective-permute-done | bytes 16416 | tf_op jit(solution)/shard_map/ppermute | solution.py:209
  24.3 0.2 collective-permute-done.11
  24.6 1.6 %collective-permute-start.12 = (f32[32,128]{1,0:T(8,128)S(1)}, f32[32,128]{1,0:T(8,128)S(1)}, u32[]{:S(2)}, u32[]{:S(2)}) collective-permute-start(f32[32,128]{1,0:T(8,128)S(1)} %add_add_fusion.1), channel_id=1, source_target_pairs={{0,8},{1,25},{2,10},{3,27},{4,12},{5,29},{6,14},{7,31},{8,0},{9,17... | collective-permute-start | bytes 49160 | tf_op jit(solution)/shard_map/ppermute | solution.py:211
  26.2 2.6 %collective-permute-start.13 = (f32[32,128]{1,0:T(8,128)S(1)}, f32[32,128]{1,0:T(8,128)S(1)}, u32[]{:S(2)}, u32[]{:S(2)}) collective-permute-start(f32[32,128]{1,0:T(8,128)S(1)} %add_add_fusion.1), channel_id=1, source_target_pairs={{0,16},{8,24},{16,0},{24,8},{1,17},{9,25},{17,1},{25,9},{2,18},{10... | collective-permute-start | bytes 49160 | tf_op jit(solution)/shard_map/ppermute | solution.py:209
  28.7 0.0 collective-permute-done.12
  28.7 0.4 %collective-permute-start.14 = (f32[32,128]{1,0:T(8,128)S(1)}, f32[32,128]{1,0:T(8,128)S(1)}, u32[]{:S(2)}, u32[]{:S(2)}) collective-permute-start(f32[32,128]{1,0:T(8,128)S(1)} %collective-permute-done.12), channel_id=1, source_target_pairs={{0,1},{1,0},{2,3},{3,2},{4,5},{5,4},{6,7},{7,6},{8,9},{9,8},{10,11... | collective-permute-start | bytes 49160 | tf_op jit(solution)/shard_map/ppermute | solution.py:209
  29.2 1.8 %collective-permute-done.13 = f32[32,128]{1,0:T(8,128)S(1)} collective-permute-done((f32[32,128]{1,0:T(8,128)S(1)}, f32[32,128]{1,0:T(8,128)S(1)}, u32[]{:S(2)}, u32[]{:S(2)}) %collective-permute-start.13) | collective-permute-done | bytes 16416 | tf_op jit(solution)/shard_map/ppermute | solution.py:209
  31.0 0.0 collective-permute-done.14
  31.0 2.9 %solve.1 = f32[64,2048]{1,0:T(8,128)} custom-call(f32[32,128]{1,0:T(8,128)S(1)} %add_add_fusion.gram_ref, bf16[128,2048]{1,0:T(8,128)(2,1)S(1)} %get-tuple-element.20.applied_ref), custom_call_target="tpu_custom_call" | custom-call | tf_op jit(solution)/shard_map/solve/pallas_call | solution.py:313
  (6 shorter events, 0.0 us)
Async XLA Ops:
  0.0 4.6 %slice-start = ((s8[8388608]{0:T(1024)(128)(4,1)}), s8[4194304]{0:T(1024)(128)(4,1)S(1)}, s32[]{:S(2)}) async-start(s8[8388608]{0:T(1024)(128)(4,1)} %bitcast.2), calls=%async_computation | async-start | bytes 8388608
  0.0 4.6 %slice-start.1 = ((s8[8388608]{0:T(1024)(128)(4,1)}), s8[4194304]{0:T(1024)(128)(4,1)S(1)}, s32[]{:S(2)}) async-start(s8[8388608]{0:T(1024)(128)(4,1)} %bitcast.2), calls=%async_computation.1 | async-start | bytes 8388608
  0.0 4.6 %copy-start.1 = (s32[16]{0:T(128)S(1)}, s32[16]{0:T(128)}, u32[]{:S(2)}) copy-start(s32[16]{0:T(128)} %count_hbm.1) | copy-start | bytes 196
  0.0 6.8 %collective-permute-start.2 = (s32[1,2,8]{2,1,0:T(2,128)}, s32[1,2,8]{2,1,0:T(2,128)S(1)}, u32[]{:S(2)}, u32[]{:S(2)}) collective-permute-start(s32[1,2,8]{2,1,0:T(2,128)} %bitcast.5), channel_id=1, source_target_pairs={{0,6},{1,7},{2,4},{3,5},{4,2},{5,3},{6,0},{7,1},{8,14},{9,15},{10,... | collective-permute-start | bytes 200 | tf_op jit(solution)/shard_map/ppermute | solution.py:209
  4.0 3.8 %collective-permute-start.1 = (s32[1,2,8]{2,1,0:T(2,128)}, s32[1,2,8]{2,1,0:T(2,128)S(1)}, u32[]{:S(2)}, u32[]{:S(2)}) collective-permute-start(s32[1,2,8]{2,1,0:T(2,128)} %bitcast.6), channel_id=1, source_target_pairs={{0,4},{1,5},{2,6},{3,7},{4,0},{5,1},{6,2},{7,3},{8,12},{9,13},{10,... | collective-permute-start | bytes 200 | tf_op jit(solution)/shard_map/ppermute | solution.py:209
  4.5 3.8 %collective-permute-start = (s32[1,2,8]{2,1,0:T(2,128)}, s32[1,2,8]{2,1,0:T(2,128)S(1)}, u32[]{:S(2)}, u32[]{:S(2)}) collective-permute-start(s32[1,2,8]{2,1,0:T(2,128)} %bitcast.7), channel_id=1, source_target_pairs={{0,2},{1,3},{2,0},{3,1},{4,6},{5,7},{6,4},{7,5},{8,10},{9,11},{10,... | collective-permute-start | bytes 200 | tf_op jit(solution)/shard_map/ppermute | solution.py:209
  4.6 3.7 %collective-permute-start.3 = (bf16[64,2048]{1,0:T(8,128)(2,1)}, bf16[64,2048]{1,0:T(8,128)(2,1)S(1)}, u32[]{:S(2)}, u32[]{:S(2)}) collective-permute-start(bf16[64,2048]{1,0:T(8,128)(2,1)} %sub_ref.1), channel_id=1, source_target_pairs={{0,1},{1,0},{2,3},{3,2},{4,5},{5,4},{6,7},{7,6},{8,9},{9,8},{10,11... | collective-permute-start | bytes 786440 | tf_op jit(solution)/shard_map/ppermute | solution.py:209
  4.6 3.6 %copy-start.2 = (s32[1,8,2]{1,2,0:T(2,128)S(1)}, s32[1,8,2]{1,2,0:T(2,128)}, u32[]{:S(2)}) copy-start(s32[1,8,2]{1,2,0:T(2,128)} %param.9) | copy-start | bytes 196
  4.6 3.7 %copy-start = (bf16[64,2048]{1,0:T(8,128)(2,1)S(1)}, bf16[64,2048]{1,0:T(8,128)(2,1)}, u32[]{:S(2)}) copy-start(bf16[64,2048]{1,0:T(8,128)(2,1)} %sub_ref.1) | copy-start | bytes 786436
  6.3 2.0 %collective-permute-start.4 = (f32[16,128]{1,0:T(8,128)S(1)}, f32[16,128]{1,0:T(8,128)S(1)}, u32[]{:S(2)}, u32[]{:S(2)}) collective-permute-start(f32[16,128]{1,0:T(8,128)S(1)} %degree.1.inv_ref), channel_id=1, source_target_pairs={{0,1},{1,0},{2,3},{3,2},{4,5},{5,4},{6,7},{7,6},{8,9},{9,8},{10,11... | collective-permute-start | bytes 24584 | tf_op jit(solution)/shard_map/ppermute | solution.py:209
  8.5 5.3 %collective-permute-start.5 = (bf16[2,2,64,128]{3,2,1,0:T(8,128)(2,1)S(1)}, bf16[2,2,64,128]{3,2,1,0:T(8,128)(2,1)S(1)}, u32[]{:S(2)}, u32[]{:S(2)}) collective-permute-start(bf16[2,2,64,128]{3,2,1,0:T(8,128)(2,1)S(1)} %get-tuple-element.16), channel_id=1, source_target_pairs={{0,6},{1,7},{2,4},{3,5},{4,2},{5,3},{6,0},{7,1},{8,14},{9,15},{10,... | collective-permute-start | bytes 196616 | tf_op jit(solution)/shard_map/ppermute | solution.py:209
  10.8 4.4 %collective-permute-start.6 = (bf16[2,2,64,128]{3,2,1,0:T(8,128)(2,1)S(1)}, bf16[2,2,64,128]{3,2,1,0:T(8,128)(2,1)S(1)}, u32[]{:S(2)}, u32[]{:S(2)}) collective-permute-start(bf16[2,2,64,128]{3,2,1,0:T(8,128)(2,1)S(1)} %get-tuple-element.17), channel_id=1, source_target_pairs={{0,4},{1,5},{2,6},{3,7},{4,0},{5,1},{6,2},{7,3},{8,12},{9,13},{10,... | collective-permute-start | bytes 196616 | tf_op jit(solution)/shard_map/ppermute | solution.py:209
  11.3 4.3 %collective-permute-start.7 = (bf16[2,2,64,128]{3,2,1,0:T(8,128)(2,1)S(1)}, bf16[2,2,64,128]{3,2,1,0:T(8,128)(2,1)S(1)}, u32[]{:S(2)}, u32[]{:S(2)}) collective-permute-start(bf16[2,2,64,128]{3,2,1,0:T(8,128)(2,1)S(1)} %get-tuple-element.18), channel_id=1, source_target_pairs={{0,2},{1,3},{2,0},{3,1},{4,6},{5,7},{6,4},{7,5},{8,10},{9,11},{10,... | collective-permute-start | bytes 196616 | tf_op jit(solution)/shard_map/ppermute | solution.py:209
  18.4 1.2 %collective-permute-start.8 = (f32[32,128]{1,0:T(8,128)S(1)}, f32[32,128]{1,0:T(8,128)S(1)}, u32[]{:S(2)}, u32[]{:S(2)}) collective-permute-start(f32[32,128]{1,0:T(8,128)S(1)} %get-tuple-element.19), channel_id=1, source_target_pairs={{0,1},{1,0},{2,3},{3,2},{4,5},{5,4},{6,7},{7,6},{8,9},{9,8},{10,11... | collective-permute-start | bytes 49160 | tf_op jit(solution)/shard_map/ppermute | solution.py:209
  19.6 3.8 %collective-permute-start.9 = (f32[32,128]{1,0:T(8,128)S(1)}, f32[32,128]{1,0:T(8,128)S(1)}, u32[]{:S(2)}, u32[]{:S(2)}) collective-permute-start(f32[32,128]{1,0:T(8,128)S(1)} %add.21), channel_id=1, source_target_pairs={{0,2},{1,7},{2,0},{3,5},{4,6},{5,3},{6,4},{7,1},{8,10},{9,15},{10,... | collective-permute-start | bytes 49160 | tf_op jit(solution)/shard_map/ppermute | solution.py:209
  20.6 3.7 %collective-permute-start.10 = (f32[32,128]{1,0:T(8,128)S(1)}, f32[32,128]{1,0:T(8,128)S(1)}, u32[]{:S(2)}, u32[]{:S(2)}) collective-permute-start(f32[32,128]{1,0:T(8,128)S(1)} %add.21), channel_id=1, source_target_pairs={{0,4},{1,5},{2,6},{3,7},{4,0},{5,1},{6,2},{7,3},{8,12},{9,13},{10,... | collective-permute-start | bytes 49160 | tf_op jit(solution)/shard_map/ppermute | solution.py:209
  23.4 1.2 %collective-permute-start.11 = (f32[32,128]{1,0:T(8,128)S(1)}, f32[32,128]{1,0:T(8,128)S(1)}, u32[]{:S(2)}, u32[]{:S(2)}) collective-permute-start(f32[32,128]{1,0:T(8,128)S(1)} %collective-permute-done.9), channel_id=1, source_target_pairs={{0,1},{1,0},{2,3},{3,2},{4,5},{5,4},{6,7},{7,6},{8,9},{9,8},{10,11... | collective-permute-start | bytes 49160 | tf_op jit(solution)/shard_map/ppermute | solution.py:209
  24.6 4.2 %collective-permute-start.12 = (f32[32,128]{1,0:T(8,128)S(1)}, f32[32,128]{1,0:T(8,128)S(1)}, u32[]{:S(2)}, u32[]{:S(2)}) collective-permute-start(f32[32,128]{1,0:T(8,128)S(1)} %add_add_fusion.1), channel_id=1, source_target_pairs={{0,8},{1,25},{2,10},{3,27},{4,12},{5,29},{6,14},{7,31},{8,0},{9,17... | collective-permute-start | bytes 49160 | tf_op jit(solution)/shard_map/ppermute | solution.py:211
  26.2 4.9 %collective-permute-start.13 = (f32[32,128]{1,0:T(8,128)S(1)}, f32[32,128]{1,0:T(8,128)S(1)}, u32[]{:S(2)}, u32[]{:S(2)}) collective-permute-start(f32[32,128]{1,0:T(8,128)S(1)} %add_add_fusion.1), channel_id=1, source_target_pairs={{0,16},{8,24},{16,0},{24,8},{1,17},{9,25},{17,1},{25,9},{2,18},{10... | collective-permute-start | bytes 49160 | tf_op jit(solution)/shard_map/ppermute | solution.py:209
  28.7 2.3 %collective-permute-start.14 = (f32[32,128]{1,0:T(8,128)S(1)}, f32[32,128]{1,0:T(8,128)S(1)}, u32[]{:S(2)}, u32[]{:S(2)}) collective-permute-start(f32[32,128]{1,0:T(8,128)S(1)} %collective-permute-done.12), channel_id=1, source_target_pairs={{0,1},{1,0},{2,3},{3,2},{4,5},{5,4},{6,7},{7,6},{8,9},{9,8},{10,11... | collective-permute-start | bytes 49160 | tf_op jit(solution)/shard_map/ppermute | solution.py:209

commit v9 on v8

--- a/solution.py
+++ b/solution.py
@@ -218,7 +218,7 @@
 
 def sum_all(x):
     x = x + swap(x, "dev", 1)
-    for axis in ("dev", "grp"):
+    for axis in ("grp", "dev"):
         for masks in stages(axis):
             if len(masks) == 1:
                 parts = [swap(x, axis, masks[0])]

time: 34.2 us -> 34.2 us (level)
  starting transfers between devices: 15.6 us -> 16 us
    ppermute x14, starting transfers between devices: 14.1 us -> 14.4 us  [swap(): lax.ppermute(x, axis, [(i, i ^ (odd if i % 2 else mask)) for i in range(s...]
where the time goes in v9:
time: 34.2 us; the launch traced here: 34 us
  starting transfers between devices  16 us (47%)
  waiting for transfers between devices  9.44 us (28%)
  Pallas kernels  8.43 us (25%)
    ppermute x14, starting transfers between devices, swap(): lax.ppermute(x, axis, [(i, i ^ (odd if i % 2 else mask)) for i in range(s...  14.4 us
    ppermute x14, waiting for transfers between devices, swap(): lax.ppermute(x, axis, [(i, i ^ (odd if i % 2 else mask)) for i in range(s...  9.44 us
    pallas_call x1, Pallas kernels, body(): pl.pallas_call(solve_kernel, out_shape=jax.ShapeDtypeStruct((k_dim, row_c...  2.93 us
    pallas_call x1, Pallas kernels, body(): pl.pallas_call(functools.partial(product_kernel, masks), out_shape=(jax.S...  2.83 us
    pallas_call x1, Pallas kernels, body(): pl.pallas_call(degree_kernel, out_shape=jax.ShapeDtypeStruct((blocks, row...  1.61 us
    ppermute x1, starting transfers between devices, swap(): return lax.ppermute(x, (axis, 'dev'), pairs)  1.58 us
    pallas_call x1, Pallas kernels, body(): pl.pallas_call(plan_kernel, out_shape=[pltpu.SMEM(x.shape, x.dtype) for x...  0.81 us
  transfers between devices with their start and end apart: 15, of which 10 were waited for; matrix products, arithmetic and copies ran while one was open for 0% of the time, Pallas kernels for 7%

profile of v9, /device:TPU:0, one launch (start us, length us, event | category | flops | bytes accessed | tf_op | source)
XLA Modules:
  0.0 34.0 jit_solution(14496284620959375405)
XLA Ops:
  0.0 0.0 slice-start
  0.0 0.0 slice-start.1
  0.0 0.0 copy-start.1
  0.0 4.0 %collective-permute-start.2 = (s32[1,2,8]{2,1,0:T(2,128)}, s32[1,2,8]{2,1,0:T(2,128)S(1)}, u32[]{:S(2)}, u32[]{:S(2)}) collective-permute-start(s32[1,2,8]{2,1,0:T(2,128)} %bitcast.5), channel_id=1, source_target_pairs={{0,6},{1,7},{2,4},{3,5},{4,2},{5,3},{6,0},{7,1},{8,14},{9,15},{10,... | collective-permute-start | bytes 200 | tf_op jit(solution)/shard_map/ppermute | solution.py:209
  4.0 0.5 %collective-permute-start.1 = (s32[1,2,8]{2,1,0:T(2,128)}, s32[1,2,8]{2,1,0:T(2,128)S(1)}, u32[]{:S(2)}, u32[]{:S(2)}) collective-permute-start(s32[1,2,8]{2,1,0:T(2,128)} %bitcast.6), channel_id=1, source_target_pairs={{0,4},{1,5},{2,6},{3,7},{4,0},{5,1},{6,2},{7,3},{8,12},{9,13},{10,... | collective-permute-start | bytes 200 | tf_op jit(solution)/shard_map/ppermute | solution.py:209
  4.5 0.1 collective-permute-start
  4.6 0.0 collective-permute-start.3
  4.6 0.0 copy-start.2
  4.6 0.0 copy-start
  4.6 0.0 slice-done
  4.6 0.0 slice-done.1
  4.6 0.0 copy-done.1
  4.7 1.6 %degree.1.inv_ref = f32[16,128]{1,0:T(8,128)S(1)} custom-call(f32[8,128]{1,0:T(8,128)S(1)} %start.1.first_ref, s32[1,16]{1,0:T(1,128)S(1)} %bitcast.4, bf16[16,16,128,128]{3,2,1,0:T(8,128)(2,1)S(1)} %bitcast.3), custom_call_target="tpu_custom_call" | custom-call | flops 67108864 | bytes 8388608 | tf_op jit(solution)/shard_map/degree/pallas_call | solution.py:252
  6.3 0.5 %collective-permute-start.4 = (f32[16,128]{1,0:T(8,128)S(1)}, f32[16,128]{1,0:T(8,128)S(1)}, u32[]{:S(2)}, u32[]{:S(2)}) collective-permute-start(f32[16,128]{1,0:T(8,128)S(1)} %degree.1.inv_ref), channel_id=1, source_target_pairs={{0,1},{1,0},{2,3},{3,2},{4,5},{5,4},{6,7},{7,6},{8,9},{9,8},{10,11... | collective-permute-start | bytes 24584 | tf_op jit(solution)/shard_map/ppermute | solution.py:209
  6.8 0.0 collective-permute-done.2.refs_3_
  6.8 0.9 %collective-permute-done.1.refs_2_ = s32[1,2,8]{2,1,0:T(2,128)S(1)} collective-permute-done((s32[1,2,8]{2,1,0:T(2,128)}, s32[1,2,8]{2,1,0:T(2,128)S(1)}, u32[]{:S(2)}, u32[]{:S(2)}) %collective-permute-start.1) | collective-permute-done | bytes 96 | tf_op jit(solution)/shard_map/ppermute | solution.py:209
  7.7 0.5 %collective-permute-done.refs_1_ = s32[1,2,8]{2,1,0:T(2,128)S(1)} collective-permute-done((s32[1,2,8]{2,1,0:T(2,128)}, s32[1,2,8]{2,1,0:T(2,128)S(1)}, u32[]{:S(2)}, u32[]{:S(2)}) %collective-permute-start) | collective-permute-done | bytes 96 | tf_op jit(solution)/shard_map/ppermute | solution.py:209
  8.3 0.0 copy-done.2
  8.3 0.0 collective-permute-done.4.sib_inv_ref
  8.3 0.0 collective-permute-done.3.sib_sub_ref
  8.3 0.0 copy-done
  8.3 0.2 select.1
  8.5 2.3 %collective-permute-start.5 = (bf16[2,2,64,128]{3,2,1,0:T(8,128)(2,1)S(1)}, bf16[2,2,64,128]{3,2,1,0:T(8,128)(2,1)S(1)}, u32[]{:S(2)}, u32[]{:S(2)}) collective-permute-start(bf16[2,2,64,128]{3,2,1,0:T(8,128)(2,1)S(1)} %get-tuple-element.16), channel_id=1, source_target_pairs={{0,6},{1,7},{2,4},{3,5},{4,2},{5,3},{6,0},{7,1},{8,14},{9,15},{10,... | collective-permute-start | bytes 196616 | tf_op jit(solution)/shard_map/ppermute | solution.py:209
  10.8 0.5 %collective-permute-start.6 = (bf16[2,2,64,128]{3,2,1,0:T(8,128)(2,1)S(1)}, bf16[2,2,64,128]{3,2,1,0:T(8,128)(2,1)S(1)}, u32[]{:S(2)}, u32[]{:S(2)}) collective-permute-start(bf16[2,2,64,128]{3,2,1,0:T(8,128)(2,1)S(1)} %get-tuple-element.17), channel_id=1, source_target_pairs={{0,4},{1,5},{2,6},{3,7},{4,0},{5,1},{6,2},{7,3},{8,12},{9,13},{10,... | collective-permute-start | bytes 196616 | tf_op jit(solution)/shard_map/ppermute | solution.py:209
  11.3 0.8 %collective-permute-start.7 = (bf16[2,2,64,128]{3,2,1,0:T(8,128)(2,1)S(1)}, bf16[2,2,64,128]{3,2,1,0:T(8,128)(2,1)S(1)}, u32[]{:S(2)}, u32[]{:S(2)}) collective-permute-start(bf16[2,2,64,128]{3,2,1,0:T(8,128)(2,1)S(1)} %get-tuple-element.18), channel_id=1, source_target_pairs={{0,2},{1,3},{2,0},{3,1},{4,6},{5,7},{6,4},{7,5},{8,10},{9,11},{10,... | collective-permute-start | bytes 196616 | tf_op jit(solution)/shard_map/ppermute | solution.py:209
  12.1 0.8 %plan.1 = (s32[16]{0:T(128)S(4)}, s32[16,16]{1,0:T(8,128)S(4)}) custom-call(s32[16]{0:T(128)} %count_hbm.1, s32[16,16]{1,0:T(8,128)} %slot_hbm.1), custom_call_target="tpu_custom_call" | custom-call | flops 2000000000 | tf_op jit(solution)/shard_map/plan/pallas_call | solution.py:283
  12.9 0.9 %collective-permute-done.5.refs_1_ = bf16[2,2,64,128]{3,2,1,0:T(8,128)(2,1)S(1)} collective-permute-done((bf16[2,2,64,128]{3,2,1,0:T(8,128)(2,1)S(1)}, bf16[2,2,64,128]{3,2,1,0:T(8,128)(2,1)S(1)}, u32[]{:S(2)}, u32[]{:S(2)}) %collective-permute-start.5) | collective-permute-done | bytes 65568 | tf_op jit(solution)/shard_map/ppermute | solution.py:209
  13.8 1.4 %collective-permute-done.6.refs_2_ = bf16[2,2,64,128]{3,2,1,0:T(8,128)(2,1)S(1)} collective-permute-done((bf16[2,2,64,128]{3,2,1,0:T(8,128)(2,1)S(1)}, bf16[2,2,64,128]{3,2,1,0:T(8,128)(2,1)S(1)}, u32[]{:S(2)}, u32[]{:S(2)}) %collective-permute-start.6) | collective-permute-done | bytes 65568 | tf_op jit(solution)/shard_map/ppermute | solution.py:209
  15.2 0.4 %collective-permute-done.7.refs_3_ = bf16[2,2,64,128]{3,2,1,0:T(8,128)(2,1)S(1)} collective-permute-done((bf16[2,2,64,128]{3,2,1,0:T(8,128)(2,1)S(1)}, bf16[2,2,64,128]{3,2,1,0:T(8,128)(2,1)S(1)}, u32[]{:S(2)}, u32[]{:S(2)}) %collective-permute-start.7) | collective-permute-done | bytes 65568 | tf_op jit(solution)/shard_map/ppermute | solution.py:209
  15.6 2.8 %product.1 = (bf16[128,2048]{1,0:T(8,128)(2,1)S(1)}, f32[32,128]{1,0:T(8,128)S(1)}) custom-call(s32[16]{0:T(128)S(4)} %get-tuple-element.13.count_ref, s32[16,16]{1,0:T(8,128)S(4)} %get-tuple-element.14.slot_ref, f32[16,128]{1,0:T(8,128)S(1)} %degree.1.inv_ref, bf16[16,16,128,128]{3,2,1,0:T(8,128)(2,1)S(1)} %bitcast.3, ...), custom_call_target="tpu_custom_call" | custom-call | flops 536870912 | bytes 8388608 | tf_op jit(solution)/shard_map/product/pallas_call | solution.py:295
  18.4 0.0 collective-permute-start.8
  18.4 1.2 %collective-permute-done.8 = f32[32,128]{1,0:T(8,128)S(1)} collective-permute-done((f32[32,128]{1,0:T(8,128)S(1)}, f32[32,128]{1,0:T(8,128)S(1)}, u32[]{:S(2)}, u32[]{:S(2)}) %collective-permute-start.8) | collective-permute-done | bytes 16416 | tf_op jit(solution)/shard_map/ppermute | solution.py:209
  19.6 1.6 %collective-permute-start.9 = (f32[32,128]{1,0:T(8,128)S(1)}, f32[32,128]{1,0:T(8,128)S(1)}, u32[]{:S(2)}, u32[]{:S(2)}) collective-permute-start(f32[32,128]{1,0:T(8,128)S(1)} %add.21), channel_id=1, source_target_pairs={{0,8},{1,25},{2,10},{3,27},{4,12},{5,29},{6,14},{7,31},{8,0},{9,17... | collective-permute-start | bytes 49160 | tf_op jit(solution)/shard_map/ppermute | solution.py:211
  21.2 2.6 %collective-permute-start.10 = (f32[32,128]{1,0:T(8,128)S(1)}, f32[32,128]{1,0:T(8,128)S(1)}, u32[]{:S(2)}, u32[]{:S(2)}) collective-permute-start(f32[32,128]{1,0:T(8,128)S(1)} %add.21), channel_id=1, source_target_pairs={{0,16},{8,24},{16,0},{24,8},{1,17},{9,25},{17,1},{25,9},{2,18},{10... | collective-permute-start | bytes 49160 | tf_op jit(solution)/shard_map/ppermute | solution.py:209
  23.8 0.0 collective-permute-done.9
  23.8 0.4 %collective-permute-start.11 = (f32[32,128]{1,0:T(8,128)S(1)}, f32[32,128]{1,0:T(8,128)S(1)}, u32[]{:S(2)}, u32[]{:S(2)}) collective-permute-start(f32[32,128]{1,0:T(8,128)S(1)} %collective-permute-done.9), channel_id=1, source_target_pairs={{0,1},{1,0},{2,3},{3,2},{4,5},{5,4},{6,7},{7,6},{8,9},{9,8},{10,11... | collective-permute-start | bytes 49160 | tf_op jit(solution)/shard_map/ppermute | solution.py:209
  24.2 1.8 %collective-permute-done.10 = f32[32,128]{1,0:T(8,128)S(1)} collective-permute-done((f32[32,128]{1,0:T(8,128)S(1)}, f32[32,128]{1,0:T(8,128)S(1)}, u32[]{:S(2)}, u32[]{:S(2)}) %collective-permute-start.10) | collective-permute-done | bytes 16416 | tf_op jit(solution)/shard_map/ppermute | solution.py:209
  26.1 0.0 collective-permute-done.11
  26.1 1.0 %collective-permute-start.12 = (f32[32,128]{1,0:T(8,128)S(1)}, f32[32,128]{1,0:T(8,128)S(1)}, u32[]{:S(2)}, u32[]{:S(2)}) collective-permute-start(f32[32,128]{1,0:T(8,128)S(1)} %add_add_fusion.1), channel_id=1, source_target_pairs={{0,2},{1,7},{2,0},{3,5},{4,6},{5,3},{6,4},{7,1},{8,10},{9,15},{10,... | collective-permute-start | bytes 49160 | tf_op jit(solution)/shard_map/ppermute | solution.py:209
  27.1 1.3 %collective-permute-start.13 = (f32[32,128]{1,0:T(8,128)S(1)}, f32[32,128]{1,0:T(8,128)S(1)}, u32[]{:S(2)}, u32[]{:S(2)}) collective-permute-start(f32[32,128]{1,0:T(8,128)S(1)} %add_add_fusion.1), channel_id=1, source_target_pairs={{0,4},{1,5},{2,6},{3,7},{4,0},{5,1},{6,2},{7,3},{8,12},{9,13},{10,... | collective-permute-start | bytes 49160 | tf_op jit(solution)/shard_map/ppermute | solution.py:209
  28.5 1.4 %collective-permute-done.12 = f32[32,128]{1,0:T(8,128)S(1)} collective-permute-done((f32[32,128]{1,0:T(8,128)S(1)}, f32[32,128]{1,0:T(8,128)S(1)}, u32[]{:S(2)}, u32[]{:S(2)}) %collective-permute-start.12) | collective-permute-done | bytes 16416 | tf_op jit(solution)/shard_map/ppermute | solution.py:209
  29.9 0.3 collective-permute-start.14
  30.2 0.8 %collective-permute-done.13 = f32[32,128]{1,0:T(8,128)S(1)} collective-permute-done((f32[32,128]{1,0:T(8,128)S(1)}, f32[32,128]{1,0:T(8,128)S(1)}, u32[]{:S(2)}, u32[]{:S(2)}) %collective-permute-start.13) | collective-permute-done | bytes 16416 | tf_op jit(solution)/shard_map/ppermute | solution.py:209
  31.0 0.1 collective-permute-done.14
  31.1 2.9 %solve.1 = f32[64,2048]{1,0:T(8,128)} custom-call(f32[32,128]{1,0:T(8,128)S(1)} %add_add_fusion.gram_ref, bf16[128,2048]{1,0:T(8,128)(2,1)S(1)} %get-tuple-element.20.applied_ref), custom_call_target="tpu_custom_call" | custom-call | tf_op jit(solution)/shard_map/solve/pallas_call | solution.py:313
  (6 shorter events, 0.0 us)
Async XLA Ops:
  0.0 4.6 %slice-start = ((s8[8388608]{0:T(1024)(128)(4,1)}), s8[4194304]{0:T(1024)(128)(4,1)S(1)}, s32[]{:S(2)}) async-start(s8[8388608]{0:T(1024)(128)(4,1)} %bitcast.2), calls=%async_computation | async-start | bytes 8388608
  0.0 4.6 %slice-start.1 = ((s8[8388608]{0:T(1024)(128)(4,1)}), s8[4194304]{0:T(1024)(128)(4,1)S(1)}, s32[]{:S(2)}) async-start(s8[8388608]{0:T(1024)(128)(4,1)} %bitcast.2), calls=%async_computation.1 | async-start | bytes 8388608
  0.0 4.6 %copy-start.1 = (s32[16]{0:T(128)S(1)}, s32[16]{0:T(128)}, u32[]{:S(2)}) copy-start(s32[16]{0:T(128)} %count_hbm.1) | copy-start | bytes 196
  0.0 6.8 %collective-permute-start.2 = (s32[1,2,8]{2,1,0:T(2,128)}, s32[1,2,8]{2,1,0:T(2,128)S(1)}, u32[]{:S(2)}, u32[]{:S(2)}) collective-permute-start(s32[1,2,8]{2,1,0:T(2,128)} %bitcast.5), channel_id=1, source_target_pairs={{0,6},{1,7},{2,4},{3,5},{4,2},{5,3},{6,0},{7,1},{8,14},{9,15},{10,... | collective-permute-start | bytes 200 | tf_op jit(solution)/shard_map/ppermute | solution.py:209
  4.0 3.8 %collective-permute-start.1 = (s32[1,2,8]{2,1,0:T(2,128)}, s32[1,2,8]{2,1,0:T(2,128)S(1)}, u32[]{:S(2)}, u32[]{:S(2)}) collective-permute-start(s32[1,2,8]{2,1,0:T(2,128)} %bitcast.6), channel_id=1, source_target_pairs={{0,4},{1,5},{2,6},{3,7},{4,0},{5,1},{6,2},{7,3},{8,12},{9,13},{10,... | collective-permute-start | bytes 200 | tf_op jit(solution)/shard_map/ppermute | solution.py:209
  4.5 3.8 %collective-permute-start = (s32[1,2,8]{2,1,0:T(2,128)}, s32[1,2,8]{2,1,0:T(2,128)S(1)}, u32[]{:S(2)}, u32[]{:S(2)}) collective-permute-start(s32[1,2,8]{2,1,0:T(2,128)} %bitcast.7), channel_id=1, source_target_pairs={{0,2},{1,3},{2,0},{3,1},{4,6},{5,7},{6,4},{7,5},{8,10},{9,11},{10,... | collective-permute-start | bytes 200 | tf_op jit(solution)/shard_map/ppermute | solution.py:209
  4.6 3.7 %collective-permute-start.3 = (bf16[64,2048]{1,0:T(8,128)(2,1)}, bf16[64,2048]{1,0:T(8,128)(2,1)S(1)}, u32[]{:S(2)}, u32[]{:S(2)}) collective-permute-start(bf16[64,2048]{1,0:T(8,128)(2,1)} %sub_ref.1), channel_id=1, source_target_pairs={{0,1},{1,0},{2,3},{3,2},{4,5},{5,4},{6,7},{7,6},{8,9},{9,8},{10,11... | collective-permute-start | bytes 786440 | tf_op jit(solution)/shard_map/ppermute | solution.py:209
  4.6 3.6 %copy-start.2 = (s32[1,8,2]{1,2,0:T(2,128)S(1)}, s32[1,8,2]{1,2,0:T(2,128)}, u32[]{:S(2)}) copy-start(s32[1,8,2]{1,2,0:T(2,128)} %param.9) | copy-start | bytes 196
  4.6 3.7 %copy-start = (bf16[64,2048]{1,0:T(8,128)(2,1)S(1)}, bf16[64,2048]{1,0:T(8,128)(2,1)}, u32[]{:S(2)}) copy-start(bf16[64,2048]{1,0:T(8,128)(2,1)} %sub_ref.1) | copy-start | bytes 786436
  6.3 2.0 %collective-permute-start.4 = (f32[16,128]{1,0:T(8,128)S(1)}, f32[16,128]{1,0:T(8,128)S(1)}, u32[]{:S(2)}, u32[]{:S(2)}) collective-permute-start(f32[16,128]{1,0:T(8,128)S(1)} %degree.1.inv_ref), channel_id=1, source_target_pairs={{0,1},{1,0},{2,3},{3,2},{4,5},{5,4},{6,7},{7,6},{8,9},{9,8},{10,11... | collective-permute-start | bytes 24584 | tf_op jit(solution)/shard_map/ppermute | solution.py:209
  8.5 5.3 %collective-permute-start.5 = (bf16[2,2,64,128]{3,2,1,0:T(8,128)(2,1)S(1)}, bf16[2,2,64,128]{3,2,1,0:T(8,128)(2,1)S(1)}, u32[]{:S(2)}, u32[]{:S(2)}) collective-permute-start(bf16[2,2,64,128]{3,2,1,0:T(8,128)(2,1)S(1)} %get-tuple-element.16), channel_id=1, source_target_pairs={{0,6},{1,7},{2,4},{3,5},{4,2},{5,3},{6,0},{7,1},{8,14},{9,15},{10,... | collective-permute-start | bytes 196616 | tf_op jit(solution)/shard_map/ppermute | solution.py:209
  10.8 4.4 %collective-permute-start.6 = (bf16[2,2,64,128]{3,2,1,0:T(8,128)(2,1)S(1)}, bf16[2,2,64,128]{3,2,1,0:T(8,128)(2,1)S(1)}, u32[]{:S(2)}, u32[]{:S(2)}) collective-permute-start(bf16[2,2,64,128]{3,2,1,0:T(8,128)(2,1)S(1)} %get-tuple-element.17), channel_id=1, source_target_pairs={{0,4},{1,5},{2,6},{3,7},{4,0},{5,1},{6,2},{7,3},{8,12},{9,13},{10,... | collective-permute-start | bytes 196616 | tf_op jit(solution)/shard_map/ppermute | solution.py:209
  11.3 4.3 %collective-permute-start.7 = (bf16[2,2,64,128]{3,2,1,0:T(8,128)(2,1)S(1)}, bf16[2,2,64,128]{3,2,1,0:T(8,128)(2,1)S(1)}, u32[]{:S(2)}, u32[]{:S(2)}) collective-permute-start(bf16[2,2,64,128]{3,2,1,0:T(8,128)(2,1)S(1)} %get-tuple-element.18), channel_id=1, source_target_pairs={{0,2},{1,3},{2,0},{3,1},{4,6},{5,7},{6,4},{7,5},{8,10},{9,11},{10,... | collective-permute-start | bytes 196616 | tf_op jit(solution)/shard_map/ppermute | solution.py:209
  18.4 1.2 %collective-permute-start.8 = (f32[32,128]{1,0:T(8,128)S(1)}, f32[32,128]{1,0:T(8,128)S(1)}, u32[]{:S(2)}, u32[]{:S(2)}) collective-permute-start(f32[32,128]{1,0:T(8,128)S(1)} %get-tuple-element.19), channel_id=1, source_target_pairs={{0,1},{1,0},{2,3},{3,2},{4,5},{5,4},{6,7},{7,6},{8,9},{9,8},{10,11... | collective-permute-start | bytes 49160 | tf_op jit(solution)/shard_map/ppermute | solution.py:209
  19.6 4.2 %collective-permute-start.9 = (f32[32,128]{1,0:T(8,128)S(1)}, f32[32,128]{1,0:T(8,128)S(1)}, u32[]{:S(2)}, u32[]{:S(2)}) collective-permute-start(f32[32,128]{1,0:T(8,128)S(1)} %add.21), channel_id=1, source_target_pairs={{0,8},{1,25},{2,10},{3,27},{4,12},{5,29},{6,14},{7,31},{8,0},{9,17... | collective-permute-start | bytes 49160 | tf_op jit(solution)/shard_map/ppermute | solution.py:211
  21.2 4.9 %collective-permute-start.10 = (f32[32,128]{1,0:T(8,128)S(1)}, f32[32,128]{1,0:T(8,128)S(1)}, u32[]{:S(2)}, u32[]{:S(2)}) collective-permute-start(f32[32,128]{1,0:T(8,128)S(1)} %add.21), channel_id=1, source_target_pairs={{0,16},{8,24},{16,0},{24,8},{1,17},{9,25},{17,1},{25,9},{2,18},{10... | collective-permute-start | bytes 49160 | tf_op jit(solution)/shard_map/ppermute | solution.py:209
  23.8 2.3 %collective-permute-start.11 = (f32[32,128]{1,0:T(8,128)S(1)}, f32[32,128]{1,0:T(8,128)S(1)}, u32[]{:S(2)}, u32[]{:S(2)}) collective-permute-start(f32[32,128]{1,0:T(8,128)S(1)} %collective-permute-done.9), channel_id=1, source_target_pairs={{0,1},{1,0},{2,3},{3,2},{4,5},{5,4},{6,7},{7,6},{8,9},{9,8},{10,11... | collective-permute-start | bytes 49160 | tf_op jit(solution)/shard_map/ppermute | solution.py:209
  26.1 3.8 %collective-permute-start.12 = (f32[32,128]{1,0:T(8,128)S(1)}, f32[32,128]{1,0:T(8,128)S(1)}, u32[]{:S(2)}, u32[]{:S(2)}) collective-permute-start(f32[32,128]{1,0:T(8,128)S(1)} %add_add_fusion.1), channel_id=1, source_target_pairs={{0,2},{1,7},{2,0},{3,5},{4,6},{5,3},{6,4},{7,1},{8,10},{9,15},{10,... | collective-permute-start | bytes 49160 | tf_op jit(solution)/shard_map/ppermute | solution.py:209
  27.1 3.9 %collective-permute-start.13 = (f32[32,128]{1,0:T(8,128)S(1)}, f32[32,128]{1,0:T(8,128)S(1)}, u32[]{:S(2)}, u32[]{:S(2)}) collective-permute-start(f32[32,128]{1,0:T(8,128)S(1)} %add_add_fusion.1), channel_id=1, source_target_pairs={{0,4},{1,5},{2,6},{3,7},{4,0},{5,1},{6,2},{7,3},{8,12},{9,13},{10,... | collective-permute-start | bytes 49160 | tf_op jit(solution)/shard_map/ppermute | solution.py:209
  29.9 1.2 %collective-permute-start.14 = (f32[32,128]{1,0:T(8,128)S(1)}, f32[32,128]{1,0:T(8,128)S(1)}, u32[]{:S(2)}, u32[]{:S(2)}) collective-permute-start(f32[32,128]{1,0:T(8,128)S(1)} %collective-permute-done.12), channel_id=1, source_target_pairs={{0,1},{1,0},{2,3},{3,2},{4,5},{5,4},{6,7},{7,6},{8,9},{9,8},{10,11... | collective-permute-start | bytes 49160 | tf_op jit(solution)/shard_map/ppermute | solution.py:209
